TPU v7x, 32 devices: a whole 2x2x4 slice. The times are simulated.
32 devices in a mesh: req: 2 (over y), seq: 4 (over z), branch: 2 (over core), tp: 2 (over x).
Axes of the slice: x: 2, y: 2, z: 4, core: 2. Of those that a mesh axis runs over, the one named last changes fastest.
Arguments:
- projected: bfloat16 [2, 768, 3, 4096], P('branch', ('req', 'seq', 'tp')), parts along dimension 1, may hold values from -24 to 24
- hint_gain: float32 [4096], replicated, may hold values from 0.3 to 1.5
- block_map: int32 [4], replicated, may hold values from 0 to 3, each once
- token_perm: int32 [8, 48], replicated, may hold values from 0 to 47, each once within a row
Outputs:
- combined: bfloat16 [2, 768, 4096], P('branch', ('req', 'seq', 'tp')), parts along dimension 1
There are 2 independent parts, one for each index of `req`. A program takes and returns all parts, laid end to end along the dimension named above; an argument that names none is the same for every part. Nothing has to cross between parts.
Inputs may be any that keep to these rules, and one draw needn't show every extreme that they name: `block_map`: a permutation of the 4 sequence shards. `token_perm`: each row is a permutation of 0 to 47.
All inputs are finite; a program needn't handle non-finite values.
Results may differ from a plain program's by a relative error of at most 0.0055.
Values may be sent and summed in bfloat16 or wider, within the bound.
No kernel may reach another device: no remote copies, remote signals or barrier semaphores. Data moves between devices by JAX's collectives and lax.ppermute only.
A program may use at most 64 MiB of HBM per device.

v0:
```python
import math

import jax
import jax.numpy as jnp
from jax import lax
from jax.sharding import PartitionSpec as P

HD = 128


key_block = 512


def passed_along(x, axis, by):
    count = lax.axis_size(axis)
    pairs = [(i, i + by) for i in range(count) if 0 <= i + by < count]
    return lax.ppermute(x, axis, pairs)


def attend(queries, key_rows, value_rows):
    row_count, columns = queries.shape
    local_heads = columns // HD
    query_heads = queries.reshape(row_count, local_heads, HD)
    scaling = 1.0 / math.sqrt(HD)
    initial = (
        jnp.full((local_heads, row_count), -jnp.inf, jnp.float32),
        jnp.zeros((local_heads, row_count), jnp.float32),
        jnp.zeros((local_heads, row_count, HD), jnp.float32),
    )
    running = initial
    key_piece = lax.all_gather(key_rows, "tp", axis=0, tiled=True)
    value_piece = lax.all_gather(value_rows, "tp", axis=0, tiled=True)
    length = key_piece.shape[0]
    step_rows = key_block if length % key_block == 0 else length
    number = length // step_rows
    key_blocks = key_piece.reshape(number, step_rows, local_heads, HD)
    value_blocks = value_piece.reshape(number, step_rows, local_heads, HD)

    def update(carried, blocks_now):
        highest, totals, summed = carried
        key_now, value_now = blocks_now
        scores = (
            jnp.einsum("qhd,khd->hqk", query_heads, key_now, preferred_element_type=jnp.float32)
            * scaling
        )
        new_highest = jnp.maximum(highest, jnp.max(scores, axis=2))
        fading = jnp.exp(highest - new_highest)
        weights = jnp.exp(scores - new_highest[..., None])
        totals = totals * fading + jnp.sum(weights, axis=2)
        summed = summed * fading[..., None] + jnp.einsum(
            "hqk,khd->hqd",
            weights.astype(jnp.bfloat16),
            value_now,
            preferred_element_type=jnp.float32,
        )
        return ((new_highest, totals, summed), None)

    running, unused = lax.scan(update, running, (key_blocks, value_blocks))
    highest, totals, summed = running
    result = summed / totals[..., None]
    return jnp.transpose(result, (1, 0, 2)).reshape(row_count, columns).astype(jnp.bfloat16)


def to_tokens(head_rows):
    return lax.all_to_all(head_rows, "seq", split_axis=0, concat_axis=1, tiled=True)


def on_device(projected, hint_gain, block_map, token_perm):
    block_rows = projected.shape[1]
    features = projected.shape[3]
    seq_count = lax.axis_size("seq")
    tp_count = lax.axis_size("tp")
    branch_index = lax.axis_index("branch")
    seq_index = lax.axis_index("seq")
    tp_index = lax.axis_index("tp")
    arrived = lax.all_to_all(projected[0], "seq", split_axis=2, concat_axis=0, tiled=True)
    columns = features // seq_count
    attended = attend(arrived[:, 0], arrived[:, 1], arrived[:, 2])
    attended = lax.optimization_barrier(attended)
    partner = passed_along(attended, "branch", -1)
    perm_table = token_perm.reshape(seq_count, tp_count, block_rows)
    column = lax.dynamic_index_in_dim(perm_table, tp_index, 1, keepdims=False)
    picked = (block_map[:, None] * block_rows + column).reshape(-1)
    control = jnp.take(partner, picked, axis=0).astype(jnp.float32)
    gain_slice = lax.dynamic_slice_in_dim(hint_gain, seq_index * columns, columns)
    summed = (attended.astype(jnp.float32) + gain_slice * control).astype(jnp.bfloat16)
    result = to_tokens(jnp.where(branch_index == 0, summed, attended))
    return result[None]


def solution(mesh):
    return jax.shard_map(
        on_device,
        mesh=mesh,
        in_specs=(P("branch", ("req", "seq", "tp"), None, None), P(), P(), P()),
        out_specs=P("branch", ("req", "seq", "tp"), None),
        check_vma=False,
    )
```

profile of v0, /device:TPU:0, one launch (start us, length us, event | category | flops | bytes accessed | tf_op | source)
XLA Modules:
  0.0 113.2 jit_solution(10417822175712787521)
XLA Ops:
  0.0 6.2 %copy.21 = bf16[1,48,3,4096]{1,2,3,0:T(4,128)(2,1)} copy(bf16[1,48,3,4096]{3,1,2,0:T(8,128)(2,1)} %param.4) | data formatting | bytes 2359296 | tf_op args[0]
  6.2 5.3 %bitcast_bitcast_fusion = bf16[4096,3,48]{2,1,0:T(4,128)(2,1)} fusion(bf16[1,48,3,4096]{1,2,3,0:T(4,128)(2,1)} %copy.21), kind=kLoop, calls=%fused_computation.28 | loop fusion | bytes 2359296
  11.5 6.9 %reshape.89 = bf16[4,2,73728]{2,1,0:T(2,128)(2,1)} reshape(bf16[4096,3,48]{2,1,0:T(4,128)(2,1)} %bitcast_bitcast_fusion) | data formatting | bytes 2359296
  18.4 0.0 copy-start.2
  18.4 0.0 copy-start.3
  18.4 6.4 %all-to-all-start = ((bf16[4,2,73728]{2,1,0:T(2,128)(2,1)}), bf16[4,2,73728]{2,1,0:T(2,128)(2,1)S(1)}, u32[]{:S(2)}, u32[]{:S(2)}) async-start(bf16[4,2,73728]{2,1,0:T(2,128)(2,1)} %reshape.89), calls=%async_computation | async-start | bytes 2359296 | tf_op jit(solution)/shard_map/all_to_all | solution.py:76
  24.8 0.5 broadcast.77
  25.3 0.0 copy-done.2
  25.3 0.7 fusion.13
  26.0 0.6 squeeze.30
  26.6 0.0 copy-done.3
  26.6 0.1 add.74
  26.7 0.6 add.80
  27.3 26.0 %all-to-all-done = bf16[4,2,73728]{2,1,0:T(2,128)(2,1)S(1)} async-done(((bf16[4,2,73728]{2,1,0:T(2,128)(2,1)}), bf16[4,2,73728]{2,1,0:T(2,128)(2,1)S(1)}, u32[]{:S(2)}, u32[]{:S(2)}) %all-to-all-start) | async-done | bytes 1179680 | tf_op jit(solution)/shard_map/all_to_all | solution.py:76
  53.3 6.3 %reshape.90 = bf16[4096,3,48]{2,1,0:T(4,128)(2,1)} reshape(bf16[4,2,73728]{2,1,0:T(2,128)(2,1)S(1)} %all-to-all-done) | data formatting | bytes 2359296
  59.6 5.4 %copy.23 = bf16[4,48,3,1024]{3,1,0,2:T(8,128)(2,1)S(1)} copy(bf16[4,48,3,1024]{1,2,3,0:T(4,128)(2,1)} %bitcast.45) | data formatting | bytes 2359296 | tf_op jit(solution)/shard_map/all_to_all | solution.py:76
  65.0 0.1 slice_bitcast_fusion
  65.1 10.8 %all-gather = bf16[384,1,1024]{2,0,1:T(8,128)(2,1)S(1)} all-gather(bf16[192,1,1024]{2,0,1:T(8,128)(2,1)S(1)} %get-tuple-element.28), channel_id=2, replica_groups=mesh['req'=2,'seq'=4,'branch'=2,'tp'=2] {'tp'}, dimensions={0}, use_global_device_ids=true | all-gather | bytes 1179648 | tf_op jit(solution)/shard_map/all_gather | solution.py:31
  75.9 0.4 copy.24
  76.3 0.1 copy.36
  76.3 0.6 multiply_reduce_fusion
  76.9 0.6 multiply_bitcast_fusion
  77.5 0.8 fusion
  78.3 0.6 bitcast_add_fusion
  78.9 9.8 %all-gather.1 = bf16[384,1,1024]{2,0,1:T(8,128)(2,1)S(1)} all-gather(bf16[192,1,1024]{2,0,1:T(8,128)(2,1)S(1)} %get-tuple-element.20), channel_id=3, replica_groups=mesh['req'=2,'seq'=4,'branch'=2,'tp'=2] {'tp'}, dimensions={0}, use_global_device_ids=true | all-gather | bytes 1179648 | tf_op jit(solution)/shard_map/all_gather | solution.py:32
  88.8 1.2 %copy.27 = bf16[384,1,1024]{0,2,1:T(8,128)(2,1)} copy(bf16[384,1,1024]{2,0,1:T(8,128)(2,1)S(1)} %all-gather.1) | data formatting | bytes 1572864 | tf_op jit(solution)/shard_map/all_gather | solution.py:32
  89.9 0.0 copy-start
  89.9 0.0 copy-start.1
  89.9 2.3 %fusion.5 = bf16[8,24,8,128]{3,2,1,0:T(8,128)(2,1)S(1)} fusion(bf16[384,8,128]{0,2,1:T(8,128)(2,1)} %bitcast.53, f32[8,192,384]{2,1,0:T(8,128)S(1)} %get-tuple-element.32, f32[8,192]{1,0:T(8,128)S(1)} %get-tuple-element.30, f32[192,8]{0,1:T(8,128)} %bitcast_add_fusion, f32[192,8]{0,1:T(8,128)} %multiply_bitcast_fusion), kind=kOutput, calls=%fused_computation.9 | convolution fusion | flops 153354240 | bytes 3557376 | tf_op jit(solution)/shard_map/while/body/eval_jaxpr/hqk,khd->hqd/dot_general | solution.py:50
  92.2 0.1 copy.42
  92.4 1.3 %collective-permute-start = (bf16[192,1024]{1,0:T(8,128)(2,1)S(1)}, bf16[192,1024]{1,0:T(8,128)(2,1)S(1)}, u32[]{:S(2)}, u32[]{:S(2)}) collective-permute-start(bf16[192,1024]{1,0:T(8,128)(2,1)S(1)} %bitcast.50), channel_id=1, source_target_pairs={{2,0},{3,1},{6,4},{7,5},{10,8},{11,9},{14,12},{15,13},{18,16},{19,... | collective-permute-start | bytes 1179656 | tf_op jit(solution)/shard_map/ppermute | solution.py:17
  93.7 0.0 copy-done
  93.7 0.0 copy-done.1
  93.7 0.1 add.75
  93.8 0.1 squeeze.29
  93.8 0.0 dynamic-slice-start
  93.9 2.1 %collective-permute-done = bf16[192,1024]{1,0:T(8,128)(2,1)S(1)} collective-permute-done((bf16[192,1024]{1,0:T(8,128)(2,1)S(1)}, bf16[192,1024]{1,0:T(8,128)(2,1)S(1)}, u32[]{:S(2)}, u32[]{:S(2)}) %collective-permute-start) | collective-permute-done | bytes 393248 | tf_op jit(solution)/shard_map/ppermute | solution.py:17
  96.0 1.0 gather_fusion
  97.0 0.0 dynamic-slice-done
  97.0 0.3 fusion.9
  97.3 14.7 %all_to_all.34 = bf16[4,48,1024]{2,1,0:T(8,128)(2,1)S(1)} all-to-all(bf16[4,48,1024]{2,1,0:T(8,128)(2,1)S(1)} %bitcast.52), channel_id=1, replica_groups=mesh['req'=2,'seq'=4,'branch'=2,'tp'=2] {'seq'}, dimensions={0} | all-to-all | bytes 786432 | tf_op jit(solution)/shard_map/all_to_all | solution.py:65
  111.9 0.3 copy.30
  112.2 1.0 broadcast_in_dim.31
  (4 shorter events, 0.0 us)
Async XLA Ops:
  18.4 7.0 %copy-start.2 = (s32[8,48]{1,0:T(8,128)S(1)}, s32[8,48]{1,0:T(8,128)}, u32[]{:S(2)}) copy-start(s32[8,48]{1,0:T(8,128)} %param.7) | copy-start | bytes 4612
  18.4 8.3 %copy-start.3 = (s32[4]{0:T(128)S(1)}, s32[4]{0:T(128)}, u32[]{:S(2)}) copy-start(s32[4]{0:T(128)} %param.6) | copy-start | bytes 52
  18.4 35.0 %all-to-all-start = ((bf16[4,2,73728]{2,1,0:T(2,128)(2,1)}), bf16[4,2,73728]{2,1,0:T(2,128)(2,1)S(1)}, u32[]{:S(2)}, u32[]{:S(2)}) async-start(bf16[4,2,73728]{2,1,0:T(2,128)(2,1)} %reshape.89), calls=%async_computation | async-start | bytes 2359296 | tf_op jit(solution)/shard_map/all_to_all | solution.py:76
  89.9 3.7 %copy-start = (s32[192,1]{0,1:T(1,128)S(1)}, s32[192,1]{0,1:T(1,128)}, u32[]{:S(2)}) copy-start(s32[192,1]{0,1:T(1,128)} %squeeze.30) | copy-start | bytes 2308
  89.9 3.7 %copy-start.1 = (s32[192,1]{0,1:T(1,128)S(1)}, s32[192,1]{0,1:T(1,128)}, u32[]{:S(2)}) copy-start(s32[192,1]{0,1:T(1,128)} %add.80) | copy-start | bytes 2308
  92.4 3.6 %collective-permute-start = (bf16[192,1024]{1,0:T(8,128)(2,1)S(1)}, bf16[192,1024]{1,0:T(8,128)(2,1)S(1)}, u32[]{:S(2)}, u32[]{:S(2)}) collective-permute-start(bf16[192,1024]{1,0:T(8,128)(2,1)S(1)} %bitcast.50), channel_id=1, source_target_pairs={{2,0},{3,1},{6,4},{7,5},{10,8},{11,9},{14,12},{15,13},{18,16},{19,... | collective-permute-start | bytes 1179656 | tf_op jit(solution)/shard_map/ppermute | solution.py:17
  93.8 3.1 %dynamic-slice-start = ((f32[4096]{0:T(1024)}, s32[]{:T(128)}), f32[1024]{0:T(1024)S(1)}, s32[]{:S(2)}) async-start(f32[4096]{0:T(1024)} %param.5, s32[]{:T(128)} %select_n.36), calls=%async_computation.2 | async-start | bytes 8704 | tf_op jit(solution)/shard_map/dynamic_slice | solution.py:85
where the time goes:
time: 114 us; the launch traced here: 113 us
  local copies, waits for them, and re-layouts  36.8 us (32%)
  blocking collectives  35.2 us (31%)
  waiting for transfers between devices  28.1 us (25%)
  starting transfers between devices  7.74 us (7%)
  matrix products  2.87 us (3%)
  other arithmetic  2.32 us (2%)
    all_to_all x1, waiting for transfers between devices, on_device(): lax.all_to_all(projected[0], 'seq', split_axis=2, concat_axis=0, tiled=True)  26 us
    unnamed x14, local copies, waits for them, and re-layouts  24.8 us
    all_to_all x1, blocking collectives, to_tokens(): lax.all_to_all(head_rows, 'seq', split_axis=0, concat_axis=1, tiled=True)  14.7 us
    all_gather x1, blocking collectives, attend(): key_piece = lax.all_gather(key_rows, 'tp', axis=0, tiled=True)  10.8 us
    all_gather x1, blocking collectives, attend(): value_piece = lax.all_gather(value_rows, 'tp', axis=0, tiled=True)  9.82 us
    all_to_all x1, starting transfers between devices, on_device(): lax.all_to_all(projected[0], 'seq', split_axis=2, concat_axis=0, tiled=True)  6.45 us
    all_to_all x1, local copies, waits for them, and re-layouts, on_device(): lax.all_to_all(projected[0], 'seq', split_axis=2, concat_axis=0, tiled=True)  5.4 us
    dot_general x1, matrix products, update(): jnp.einsum('hqk,khd->hqd', weights.astype(jnp.bfloat16), value_now, prefe...  2.3 us
  transfers between devices with their start and end apart: 2, of which 2 were waited for; matrix products, arithmetic and copies ran while one was open for 2% of the time, Pallas kernels for 0%

commit v1 on v0

--- a/solution.py
+++ b/solution.py
@@ -1,14 +1,183 @@
+import functools
 import math
 
 import jax
 import jax.numpy as jnp
 from jax import lax
+from jax.experimental import pallas as pl
+from jax.experimental.pallas import tpu as pltpu
 from jax.sharding import PartitionSpec as P
 
 HD = 128
-
+GROUP = ("seq", "tp")
+VMEM_LIMIT = 32 * 1024 * 1024
 
 key_block = 512
+
+SHARES = (1.0,)
+
+
+def group_index():
+    return lax.axis_index("seq") * lax.axis_size("tp") + lax.axis_index("tp")
+
+
+def columns_of(group, step, width, start, size):
+    first = lax.bitwise_xor(group, step) * width + start
+    return pl.ds(pl.multiple_of(first, HD), size)
+
+
+def split_kernel(chunks, count, width, rows_ref, *refs):
+    outs, sems = refs[:-1], refs[-1]
+    me = group_index()
+    copies = []
+    for c, (start, size) in enumerate(chunks):
+        for step in range(count):
+            n = c * count + step
+            copies.append(
+                pltpu.make_async_copy(
+                    rows_ref.at[:, :, columns_of(me, step, width, start, size)],
+                    outs[n],
+                    sems.at[n],
+                )
+            )
+    for copy in copies:
+        copy.start()
+    for copy in copies:
+        copy.wait()
+
+
+def attend_kernel(count, rows, size, *refs):
+    pieces, out_ref = refs[:count], refs[count]
+    scaling = 1.0 / math.sqrt(HD)
+    for head in range(size // HD):
+        at = slice(head * HD, (head + 1) * HD)
+        queries, keys, values = (
+            jnp.concatenate([piece[n, :, at] for piece in pieces], axis=0) for n in range(3)
+        )
+        scores = lax.dot_general(
+            queries, keys, (((1,), (1,)), ((), ())), preferred_element_type=jnp.float32
+        )
+        highest = jnp.max(scores, axis=1, keepdims=True)
+        weights = jnp.exp((scores - highest) * scaling)
+        totals = jnp.sum(weights, axis=1, keepdims=True)
+        summed = jnp.dot(
+            weights.astype(jnp.bfloat16), values, preferred_element_type=jnp.float32
+        )
+        out_ref[:, :, at] = (summed / totals).astype(jnp.bfloat16).reshape(count, rows, HD)
+
+
+def join_kernel(count, rows, width, start, size, map_ref, perm_ref, gain_ref, own_ref, hint_ref, *outs):
+    me = group_index()
+    tp_count = lax.axis_size("tp")
+    gain = gain_ref[:, columns_of(me, 0, width, start, size)]
+    gain = jnp.where(lax.axis_index("branch") == 0, gain, jnp.zeros_like(gain))
+    source_row = lax.broadcasted_iota(jnp.int32, (rows, rows), 0)
+    for step in range(count):
+        block = lax.bitwise_xor(me, step)
+        source = map_ref[block // tp_count] * tp_count + block % tp_count
+        chosen = (source_row == perm_ref[pl.ds(block, 1), :]).astype(jnp.bfloat16)
+        control = lax.dot_general(
+            chosen,
+            hint_ref[lax.bitwise_xor(source, me)],
+            (((0,), (0,)), ((), ())),
+            preferred_element_type=jnp.float32,
+        )
+        outs[step][...] = (own_ref[step].astype(jnp.float32) + gain * control).astype(jnp.bfloat16)
+
+
+def merge_kernel(chunks, count, width, *refs):
+    pieces, out_ref, sems = refs[:-2], refs[-2], refs[-1]
+    me = group_index()
+    copies = []
+    for c, (start, size) in enumerate(chunks):
+        for step in range(count):
+            n = c * count + step
+            copies.append(
+                pltpu.make_async_copy(
+                    pieces[n],
+                    out_ref.at[:, columns_of(me, step, width, start, size)],
+                    sems.at[n],
+                )
+            )
+    for copy in copies:
+        copy.start()
+    for copy in copies:
+        copy.wait()
+
+
+def any_specs(number):
+    return [pl.BlockSpec(memory_space=pl.ANY)] * number
+
+
+def vmem_specs(number):
+    return [pl.BlockSpec(memory_space=pltpu.VMEM)] * number
+
+
+PARAMS = pltpu.CompilerParams(vmem_limit_bytes=VMEM_LIMIT)
+
+
+def exchange(piece, step, count):
+    if step == 0:
+        return piece
+    return lax.ppermute(piece, GROUP, [(i, i ^ step) for i in range(count)])
+
+
+def by_heads(projected, hint_gain, block_map, token_perm):
+    rows, features = projected.shape[1], projected.shape[3]
+    count = lax.axis_size("seq") * lax.axis_size("tp")
+    width = features // count
+    heads = width // HD
+    edges = [0]
+    for share in SHARES:
+        edges.append(min(heads, edges[-1] + max(1, round(share * heads))))
+    edges[-1] = heads
+    chunks = [(a * HD, (b - a) * HD) for a, b in zip(edges, edges[1:]) if b > a]
+    stacked = jnp.transpose(projected[0], (1, 0, 2))
+    sent = pl.pallas_call(
+        functools.partial(split_kernel, chunks, count, width),
+        out_shape=[
+            jax.ShapeDtypeStruct((3, rows, size), projected.dtype)
+            for start, size in chunks
+            for step in range(count)
+        ],
+        in_specs=any_specs(1),
+        out_specs=any_specs(len(chunks) * count),
+        scratch_shapes=[pltpu.SemaphoreType.DMA((len(chunks) * count,))],
+        compiler_params=PARAMS,
+        name="split",
+    )(stacked)
+    gain = hint_gain[None, :]
+    returned = []
+    for c, (start, size) in enumerate(chunks):
+        pieces = [exchange(sent[c * count + step], step, count) for step in range(count)]
+        attended = pl.pallas_call(
+            functools.partial(attend_kernel, count, rows, size),
+            out_shape=jax.ShapeDtypeStruct((count, rows, size), projected.dtype),
+            in_specs=vmem_specs(count),
+            out_specs=vmem_specs(1)[0],
+            compiler_params=PARAMS,
+            name="attend",
+        )(*pieces)
+        hint = lax.ppermute(attended, "branch", [(1, 0)])
+        joined = pl.pallas_call(
+            functools.partial(join_kernel, count, rows, width, start, size),
+            out_shape=[jax.ShapeDtypeStruct((rows, size), projected.dtype)] * count,
+            in_specs=[pl.BlockSpec(memory_space=pltpu.SMEM)] + vmem_specs(4),
+            out_specs=vmem_specs(count),
+            compiler_params=PARAMS,
+            name="join",
+        )(block_map, token_perm, gain, attended, hint)
+        returned += [exchange(joined[step], step, count) for step in range(count)]
+    result = pl.pallas_call(
+        functools.partial(merge_kernel, chunks, count, width),
+        out_shape=jax.ShapeDtypeStruct((rows, features), projected.dtype),
+        in_specs=any_specs(len(returned)),
+        out_specs=any_specs(1)[0],
+        scratch_shapes=[pltpu.SemaphoreType.DMA((len(returned),))],
+        compiler_params=PARAMS,
+        name="merge",
+    )(*returned)
+    return result[None]
 
 
 def passed_along(x, axis, by):
@@ -61,11 +230,7 @@
     return jnp.transpose(result, (1, 0, 2)).reshape(row_count, columns).astype(jnp.bfloat16)
 
 
-def to_tokens(head_rows):
-    return lax.all_to_all(head_rows, "seq", split_axis=0, concat_axis=1, tiled=True)
-
-
-def on_device(projected, hint_gain, block_map, token_perm):
+def by_heads_and_rows(projected, hint_gain, block_map, token_perm):
     block_rows = projected.shape[1]
     features = projected.shape[3]
     seq_count = lax.axis_size("seq")
@@ -84,8 +249,16 @@
     control = jnp.take(partner, picked, axis=0).astype(jnp.float32)
     gain_slice = lax.dynamic_slice_in_dim(hint_gain, seq_index * columns, columns)
     summed = (attended.astype(jnp.float32) + gain_slice * control).astype(jnp.bfloat16)
-    result = to_tokens(jnp.where(branch_index == 0, summed, attended))
-    return result[None]
+    result = jnp.where(branch_index == 0, summed, attended)
+    return lax.all_to_all(result, "seq", split_axis=0, concat_axis=1, tiled=True)[None]
+
+
+def on_device(projected, hint_gain, block_map, token_perm):
+    count = lax.axis_size("seq") * lax.axis_size("tp")
+    rows, heads = projected.shape[1], projected.shape[3] // HD
+    if heads % count == 0 and count & (count - 1) == 0 and rows % 16 == 0:
+        return by_heads(projected, hint_gain, block_map, token_perm)
+    return by_heads_and_rows(projected, hint_gain, block_map, token_perm)
 
 
 def solution(mesh):

time: 114 us -> 57.7 us (0.51)
  local copies, waits for them, and re-layouts: 36.8 us -> 1.28 us
  blocking collectives: 35.2 us -> 0 us
  starting transfers between devices: 7.74 us -> 30.4 us
  waiting for transfers between devices: 28.1 us -> 22.5 us
  Pallas kernels: 0 us -> 3.37 us
  matrix products: 2.87 us -> 0 us
  other arithmetic: 2.32 us -> 0 us
    ppermute x1 -> x15, starting transfers between devices: 1.29 us -> 30.4 us  [the longest x14 29.1 us: exchange(): return lax.ppermute(piece, GROUP, [(i, i ^ step) for i in range(count)])]
    all_to_all x1 -> x0, waiting for transfers between devices: 26 us -> none  [on_device(): lax.all_to_all(projected[0], 'seq', split_axis=2, concat_axis=0, tiled=True)]
    unnamed x14 -> x8, local copies, waits for them, and re-layouts: 24.8 us -> 1.28 us
    all_gather x2 -> x0, blocking collectives: 20.6 us -> none  [the longest x1 10.8 us: attend(): key_piece = lax.all_gather(key_rows, 'tp', axis=0, tiled=True)]
    ppermute x1 -> x15, waiting for transfers between devices: 2.09 us -> 22.5 us  [the longest x14 20.2 us: exchange(): return lax.ppermute(piece, GROUP, [(i, i ^ step) for i in range(count)])]
    all_to_all x1 -> x0, blocking collectives: 14.7 us -> none  [to_tokens(): lax.all_to_all(head_rows, 'seq', split_axis=0, concat_axis=1, tiled=True)]
    all_to_all x1 -> x0, starting transfers between devices: 6.45 us -> none  [on_device(): lax.all_to_all(projected[0], 'seq', split_axis=2, concat_axis=0, tiled=True)]
    all_to_all x2 -> x0, local copies, waits for them, and re-layouts: 5.71 us -> none  [the longest x1 5.4 us: on_device(): lax.all_to_all(projected[0], 'seq', split_axis=2, concat_axis=0, tiled=True)]
  transfers between devices with their start and end apart: 2 -> 15, of which waited for: 2 -> 6; matrix products, arithmetic and copies ran while one was open for 2% -> 0% of each run, Pallas kernels for 0% -> 0%
where the time goes in v1:
time: 57.7 us; the launch traced here: 57.6 us
  starting transfers between devices  30.4 us (53%)
  waiting for transfers between devices  22.5 us (39%)
  Pallas kernels  3.37 us (6%)
  local copies, waits for them, and re-layouts  1.28 us (2%)
    ppermute x14, starting transfers between devices, exchange(): return lax.ppermute(piece, GROUP, [(i, i ^ step) for i in range(count)])  29.1 us
    ppermute x14, waiting for transfers between devices, exchange(): return lax.ppermute(piece, GROUP, [(i, i ^ step) for i in range(count)])  20.2 us
    ppermute x1, waiting for transfers between devices, by_heads(): hint = lax.ppermute(attended, 'branch', [(1, 0)])  2.32 us
    pallas_call x1, Pallas kernels, by_heads(): pl.pallas_call(functools.partial(attend_kernel, count, rows, size), out_s...  1.47 us
    ppermute x1, starting transfers between devices, by_heads(): hint = lax.ppermute(attended, 'branch', [(1, 0)])  1.29 us
    unnamed x8, local copies, waits for them, and re-layouts  1.28 us
  transfers between devices with their start and end apart: 15, of which 6 were waited for; matrix products, arithmetic and copies ran while one was open for 0% of the time, Pallas kernels for 0%

profile of v1, /device:TPU:0, one launch (start us, length us, event | category | flops | bytes accessed | tf_op | source)
XLA Modules:
  0.0 57.6 jit_solution(14548960768725180562)
XLA Ops:
  0.0 0.0 copy-start
  0.0 1.3 %copy-done = bf16[1,48,3,4096]{3,1,2,0:T(8,128)(2,1)S(1)} copy-done((bf16[1,48,3,4096]{3,1,2,0:T(8,128)(2,1)S(1)}, bf16[1,48,3,4096]{3,1,2,0:T(8,128)(2,1)}, u32[]{:S(2)}) %copy-start) | copy-done | bytes 1179672
  1.3 0.0 copy-start.1
  1.3 0.0 copy-start.2
  1.3 0.0 copy-start.3
  1.3 0.3 split.1
  1.5 3.0 %collective-permute-start = (bf16[3,48,512]{2,1,0:T(8,128)(2,1)S(1)}, bf16[3,48,512]{2,1,0:T(8,128)(2,1)S(1)}, u32[]{:S(2)}, u32[]{:S(2)}) collective-permute-start(bf16[3,48,512]{2,1,0:T(8,128)(2,1)S(1)} %get-tuple-element.22), channel_id=1, source_target_pairs={{0,1},{1,0},{4,5},{5,4},{8,9},{9,8},{12,13},{13,12},{2,3},{3,2},{6... | collective-permute-start | bytes 442376 | tf_op jit(solution)/shard_map/ppermute | solution.py:122
  4.5 1.6 %collective-permute-start.1 = (bf16[3,48,512]{2,1,0:T(8,128)(2,1)S(1)}, bf16[3,48,512]{2,1,0:T(8,128)(2,1)S(1)}, u32[]{:S(2)}, u32[]{:S(2)}) collective-permute-start(bf16[3,48,512]{2,1,0:T(8,128)(2,1)S(1)} %get-tuple-element.23), channel_id=1, source_target_pairs={{0,4},{1,5},{4,0},{5,1},{8,12},{9,13},{12,8},{13,9},{2,6},{3,7},{6... | collective-permute-start | bytes 442376 | tf_op jit(solution)/shard_map/ppermute | solution.py:122
  6.1 0.0 collective-permute-start.2
  6.1 3.0 %collective-permute-start.3 = (bf16[3,48,512]{2,1,0:T(8,128)(2,1)S(1)}, bf16[3,48,512]{2,1,0:T(8,128)(2,1)S(1)}, u32[]{:S(2)}, u32[]{:S(2)}) collective-permute-start(bf16[3,48,512]{2,1,0:T(8,128)(2,1)S(1)} %get-tuple-element.25), channel_id=1, source_target_pairs={{0,8},{1,9},{4,12},{5,13},{8,0},{9,1},{12,4},{13,5},{2,10},{3,11},... | collective-permute-start | bytes 442376 | tf_op jit(solution)/shard_map/ppermute | solution.py:122
  9.1 1.3 %collective-permute-start.4 = (bf16[3,48,512]{2,1,0:T(8,128)(2,1)S(1)}, bf16[3,48,512]{2,1,0:T(8,128)(2,1)S(1)}, u32[]{:S(2)}, u32[]{:S(2)}) collective-permute-start(bf16[3,48,512]{2,1,0:T(8,128)(2,1)S(1)} %get-tuple-element.26), channel_id=1, source_target_pairs={{0,9},{1,8},{4,13},{5,12},{8,1},{9,0},{12,5},{13,4},{2,11},{3,10},... | collective-permute-start | bytes 442376 | tf_op jit(solution)/shard_map/ppermute | solution.py:122
  10.4 0.0 collective-permute-done.refs_1_
  10.4 3.6 %collective-permute-start.5 = (bf16[3,48,512]{2,1,0:T(8,128)(2,1)S(1)}, bf16[3,48,512]{2,1,0:T(8,128)(2,1)S(1)}, u32[]{:S(2)}, u32[]{:S(2)}) collective-permute-start(bf16[3,48,512]{2,1,0:T(8,128)(2,1)S(1)} %get-tuple-element.27), channel_id=1, source_target_pairs={{0,12},{1,13},{4,8},{5,9},{8,4},{9,5},{12,0},{13,1},{2,14},{3,15},... | collective-permute-start | bytes 442376 | tf_op jit(solution)/shard_map/ppermute | solution.py:122
  14.0 2.5 %collective-permute-done.1.refs_2_ = bf16[3,48,512]{2,1,0:T(8,128)(2,1)S(1)} collective-permute-done((bf16[3,48,512]{2,1,0:T(8,128)(2,1)S(1)}, bf16[3,48,512]{2,1,0:T(8,128)(2,1)S(1)}, u32[]{:S(2)}, u32[]{:S(2)}) %collective-permute-start.1) | collective-permute-done | bytes 147488 | tf_op jit(solution)/shard_map/ppermute | solution.py:122
  16.5 0.9 %collective-permute-start.6 = (bf16[3,48,512]{2,1,0:T(8,128)(2,1)S(1)}, bf16[3,48,512]{2,1,0:T(8,128)(2,1)S(1)}, u32[]{:S(2)}, u32[]{:S(2)}) collective-permute-start(bf16[3,48,512]{2,1,0:T(8,128)(2,1)S(1)} %get-tuple-element.28), channel_id=1, source_target_pairs={{0,13},{1,12},{4,9},{5,8},{8,5},{9,4},{12,1},{13,0},{2,15},{3,14},... | collective-permute-start | bytes 442376 | tf_op jit(solution)/shard_map/ppermute | solution.py:122
  17.5 0.1 collective-permute-done.2.refs_3_
  17.6 0.0 collective-permute-done.3.refs_4_
  17.6 13.0 %collective-permute-done.4.refs_5_ = bf16[3,48,512]{2,1,0:T(8,128)(2,1)S(1)} collective-permute-done((bf16[3,48,512]{2,1,0:T(8,128)(2,1)S(1)}, bf16[3,48,512]{2,1,0:T(8,128)(2,1)S(1)}, u32[]{:S(2)}, u32[]{:S(2)}) %collective-permute-start.4) | collective-permute-done | bytes 147488 | tf_op jit(solution)/shard_map/ppermute | solution.py:122
  30.6 0.0 collective-permute-done.5.refs_6_
  30.6 0.0 collective-permute-done.6.refs_7_
  30.6 1.5 %attend.1.own_ref = bf16[8,48,512]{2,1,0:T(8,128)(2,1)S(1)} custom-call(bf16[3,48,512]{2,1,0:T(8,128)(2,1)S(1)} %get-tuple-element.21.refs_0_, bf16[3,48,512]{2,1,0:T(8,128)(2,1)S(1)} %collective-permute-done.refs_1_, bf16[3,48,512]{2,1,0:T(8,128)(2,1)S(1)} %collective-permute-done.1.refs_2_, bf16[3,48,512]{2,1,0:T(8,128)(2,1)S(1)} %collective-permute-done.2.refs_3_, ...), custom_call_target="tpu_custom_call" | custom-call | tf_op jit(solution)/shard_map/attend/pallas_call | solution.py:153
  32.1 1.3 %collective-permute-start.7 = (bf16[8,48,512]{2,1,0:T(8,128)(2,1)S(1)}, bf16[8,48,512]{2,1,0:T(8,128)(2,1)S(1)}, u32[]{:S(2)}, u32[]{:S(2)}) collective-permute-start(bf16[8,48,512]{2,1,0:T(8,128)(2,1)S(1)} %attend.1.own_ref), channel_id=1, source_target_pairs={{2,0},{3,1},{6,4},{7,5},{10,8},{11,9},{14,12},{15,13},{18,16},{19,... | collective-permute-start | bytes 1179656 | tf_op jit(solution)/shard_map/ppermute | solution.py:161
  33.4 2.3 %collective-permute-done.7.hint_ref = bf16[8,48,512]{2,1,0:T(8,128)(2,1)S(1)} collective-permute-done((bf16[8,48,512]{2,1,0:T(8,128)(2,1)S(1)}, bf16[8,48,512]{2,1,0:T(8,128)(2,1)S(1)}, u32[]{:S(2)}, u32[]{:S(2)}) %collective-permute-start.7) | collective-permute-done | bytes 393248 | tf_op jit(solution)/shard_map/ppermute | solution.py:161
  35.7 0.0 copy-done.1
  35.7 0.0 copy-done.2
  35.7 0.0 copy-done.3
  35.7 0.8 %join.1 = (bf16[48,512]{1,0:T(8,128)(2,1)S(1)}, bf16[48,512]{1,0:T(8,128)(2,1)S(1)}, bf16[48,512]{1,0:T(8,128)(2,1)S(1)}, bf16[48,512]{1,0:T(8,128)(2,1)S(1)}, b...) custom-call(s32[4]{0:T(128)S(1)} %copy-done.3, ...), custom_call_target="tpu_custom_call" | custom-call | tf_op jit(solution)/shard_map/join/pallas_call | solution.py:162
  36.5 0.9 %collective-permute-start.8 = (bf16[48,512]{1,0:T(8,128)(2,1)S(1)}, bf16[48,512]{1,0:T(8,128)(2,1)S(1)}, u32[]{:S(2)}, u32[]{:S(2)}) collective-permute-start(bf16[48,512]{1,0:T(8,128)(2,1)S(1)} %get-tuple-element.30), channel_id=1, source_target_pairs={{0,1},{1,0},{4,5},{5,4},{8,9},{9,8},{12,13},{13,12},{2,3},{3,2},{6... | collective-permute-start | bytes 147464 | tf_op jit(solution)/shard_map/ppermute | solution.py:122
  37.4 5.2 %collective-permute-start.9 = (bf16[48,512]{1,0:T(8,128)(2,1)S(1)}, bf16[48,512]{1,0:T(8,128)(2,1)S(1)}, u32[]{:S(2)}, u32[]{:S(2)}) collective-permute-start(bf16[48,512]{1,0:T(8,128)(2,1)S(1)} %get-tuple-element.31), channel_id=1, source_target_pairs={{0,4},{1,5},{4,0},{5,1},{8,12},{9,13},{12,8},{13,9},{2,6},{3,7},{6... | collective-permute-start | bytes 147464 | tf_op jit(solution)/shard_map/ppermute | solution.py:122
  42.7 1.0 %collective-permute-start.10 = (bf16[48,512]{1,0:T(8,128)(2,1)S(1)}, bf16[48,512]{1,0:T(8,128)(2,1)S(1)}, u32[]{:S(2)}, u32[]{:S(2)}) collective-permute-start(bf16[48,512]{1,0:T(8,128)(2,1)S(1)} %get-tuple-element.32), channel_id=1, source_target_pairs={{0,5},{1,4},{4,1},{5,0},{8,13},{9,12},{12,9},{13,8},{2,7},{3,6},{6... | collective-permute-start | bytes 147464 | tf_op jit(solution)/shard_map/ppermute | solution.py:122
  43.7 3.8 %collective-permute-start.11 = (bf16[48,512]{1,0:T(8,128)(2,1)S(1)}, bf16[48,512]{1,0:T(8,128)(2,1)S(1)}, u32[]{:S(2)}, u32[]{:S(2)}) collective-permute-start(bf16[48,512]{1,0:T(8,128)(2,1)S(1)} %get-tuple-element.33), channel_id=1, source_target_pairs={{0,8},{1,9},{4,12},{5,13},{8,0},{9,1},{12,4},{13,5},{2,10},{3,11},... | collective-permute-start | bytes 147464 | tf_op jit(solution)/shard_map/ppermute | solution.py:122
  47.5 0.0 collective-permute-start.12
  47.5 0.0 collective-permute-done.8.refs_1_
  47.5 2.4 %collective-permute-start.13 = (bf16[48,512]{1,0:T(8,128)(2,1)S(1)}, bf16[48,512]{1,0:T(8,128)(2,1)S(1)}, u32[]{:S(2)}, u32[]{:S(2)}) collective-permute-start(bf16[48,512]{1,0:T(8,128)(2,1)S(1)} %get-tuple-element.35), channel_id=1, source_target_pairs={{0,12},{1,13},{4,8},{5,9},{8,4},{9,5},{12,0},{13,1},{2,14},{3,15},... | collective-permute-start | bytes 147464 | tf_op jit(solution)/shard_map/ppermute | solution.py:122
  49.9 0.0 collective-permute-done.9.refs_2_
  49.9 2.4 %collective-permute-start.14 = (bf16[48,512]{1,0:T(8,128)(2,1)S(1)}, bf16[48,512]{1,0:T(8,128)(2,1)S(1)}, u32[]{:S(2)}, u32[]{:S(2)}) collective-permute-start(bf16[48,512]{1,0:T(8,128)(2,1)S(1)} %get-tuple-element.36), channel_id=1, source_target_pairs={{0,13},{1,12},{4,9},{5,8},{8,5},{9,4},{12,1},{13,0},{2,15},{3,14},... | collective-permute-start | bytes 147464 | tf_op jit(solution)/shard_map/ppermute | solution.py:122
  52.2 0.0 collective-permute-done.10.refs_3_
  52.2 0.0 collective-permute-done.11.refs_4_
  52.2 2.9 %collective-permute-done.12.refs_5_ = bf16[48,512]{1,0:T(8,128)(2,1)S(1)} collective-permute-done((bf16[48,512]{1,0:T(8,128)(2,1)S(1)}, bf16[48,512]{1,0:T(8,128)(2,1)S(1)}, u32[]{:S(2)}, u32[]{:S(2)}) %collective-permute-start.12) | collective-permute-done | bytes 49184 | tf_op jit(solution)/shard_map/ppermute | solution.py:122
  55.1 0.0 collective-permute-done.13.refs_6_
  55.1 1.6 %collective-permute-done.14.refs_7_ = bf16[48,512]{1,0:T(8,128)(2,1)S(1)} collective-permute-done((bf16[48,512]{1,0:T(8,128)(2,1)S(1)}, bf16[48,512]{1,0:T(8,128)(2,1)S(1)}, u32[]{:S(2)}, u32[]{:S(2)}) %collective-permute-start.14) | collective-permute-done | bytes 49184 | tf_op jit(solution)/shard_map/ppermute | solution.py:122
  56.8 0.8 %merge.1 = bf16[48,4096]{1,0:T(8,128)(2,1)} custom-call(bf16[48,512]{1,0:T(8,128)(2,1)S(1)} %get-tuple-element.29.refs_0_, bf16[48,512]{1,0:T(8,128)(2,1)S(1)} %collective-permute-done.8.refs_1_, bf16[48,512]{1,0:T(8,128)(2,1)S(1)} %collective-permute-done.9.refs_2_, bf16[48,512]{1,0:T(8,128)(2,1)S(1)} %collective-permute-done.10.refs_3_, ...), custom_call_target="tpu_custom_call" | custom-call | tf_op jit(solution)/shard_map/merge/pallas_call | solution.py:171
Async XLA Ops:
  0.0 1.3 %copy-start = (bf16[1,48,3,4096]{3,1,2,0:T(8,128)(2,1)S(1)}, bf16[1,48,3,4096]{3,1,2,0:T(8,128)(2,1)}, u32[]{:S(2)}) copy-start(bf16[1,48,3,4096]{3,1,2,0:T(8,128)(2,1)} %param.4) | copy-start | bytes 3538948
  1.3 34.4 %copy-start.1 = (f32[4096]{0:T(1024)S(1)}, f32[4096]{0:T(1024)}, u32[]{:S(2)}) copy-start(f32[4096]{0:T(1024)} %param.5) | copy-start | bytes 49156
  1.3 34.4 %copy-start.2 = (s32[8,48]{1,0:T(8,128)S(1)}, s32[8,48]{1,0:T(8,128)}, u32[]{:S(2)}) copy-start(s32[8,48]{1,0:T(8,128)} %perm_ref.1) | copy-start | bytes 4612
  1.3 34.4 %copy-start.3 = (s32[4]{0:T(128)S(1)}, s32[4]{0:T(128)}, u32[]{:S(2)}) copy-start(s32[4]{0:T(128)} %map_ref.1) | copy-start | bytes 52
  1.5 8.9 %collective-permute-start = (bf16[3,48,512]{2,1,0:T(8,128)(2,1)S(1)}, bf16[3,48,512]{2,1,0:T(8,128)(2,1)S(1)}, u32[]{:S(2)}, u32[]{:S(2)}) collective-permute-start(bf16[3,48,512]{2,1,0:T(8,128)(2,1)S(1)} %get-tuple-element.22), channel_id=1, source_target_pairs={{0,1},{1,0},{4,5},{5,4},{8,9},{9,8},{12,13},{13,12},{2,3},{3,2},{6... | collective-permute-start | bytes 442376 | tf_op jit(solution)/shard_map/ppermute | solution.py:122
  4.5 12.0 %collective-permute-start.1 = (bf16[3,48,512]{2,1,0:T(8,128)(2,1)S(1)}, bf16[3,48,512]{2,1,0:T(8,128)(2,1)S(1)}, u32[]{:S(2)}, u32[]{:S(2)}) collective-permute-start(bf16[3,48,512]{2,1,0:T(8,128)(2,1)S(1)} %get-tuple-element.23), channel_id=1, source_target_pairs={{0,4},{1,5},{4,0},{5,1},{8,12},{9,13},{12,8},{13,9},{2,6},{3,7},{6... | collective-permute-start | bytes 442376 | tf_op jit(solution)/shard_map/ppermute | solution.py:122
  6.1 11.5 %collective-permute-start.2 = (bf16[3,48,512]{2,1,0:T(8,128)(2,1)S(1)}, bf16[3,48,512]{2,1,0:T(8,128)(2,1)S(1)}, u32[]{:S(2)}, u32[]{:S(2)}) collective-permute-start(bf16[3,48,512]{2,1,0:T(8,128)(2,1)S(1)} %get-tuple-element.24), channel_id=1, source_target_pairs={{0,5},{1,4},{4,1},{5,0},{8,13},{9,12},{12,9},{13,8},{2,7},{3,6},{6... | collective-permute-start | bytes 442376 | tf_op jit(solution)/shard_map/ppermute | solution.py:122
  6.1 11.5 %collective-permute-start.3 = (bf16[3,48,512]{2,1,0:T(8,128)(2,1)S(1)}, bf16[3,48,512]{2,1,0:T(8,128)(2,1)S(1)}, u32[]{:S(2)}, u32[]{:S(2)}) collective-permute-start(bf16[3,48,512]{2,1,0:T(8,128)(2,1)S(1)} %get-tuple-element.25), channel_id=1, source_target_pairs={{0,8},{1,9},{4,12},{5,13},{8,0},{9,1},{12,4},{13,5},{2,10},{3,11},... | collective-permute-start | bytes 442376 | tf_op jit(solution)/shard_map/ppermute | solution.py:122
  9.1 21.5 %collective-permute-start.4 = (bf16[3,48,512]{2,1,0:T(8,128)(2,1)S(1)}, bf16[3,48,512]{2,1,0:T(8,128)(2,1)S(1)}, u32[]{:S(2)}, u32[]{:S(2)}) collective-permute-start(bf16[3,48,512]{2,1,0:T(8,128)(2,1)S(1)} %get-tuple-element.26), channel_id=1, source_target_pairs={{0,9},{1,8},{4,13},{5,12},{8,1},{9,0},{12,5},{13,4},{2,11},{3,10},... | collective-permute-start | bytes 442376 | tf_op jit(solution)/shard_map/ppermute | solution.py:122
  10.4 20.2 %collective-permute-start.5 = (bf16[3,48,512]{2,1,0:T(8,128)(2,1)S(1)}, bf16[3,48,512]{2,1,0:T(8,128)(2,1)S(1)}, u32[]{:S(2)}, u32[]{:S(2)}) collective-permute-start(bf16[3,48,512]{2,1,0:T(8,128)(2,1)S(1)} %get-tuple-element.27), channel_id=1, source_target_pairs={{0,12},{1,13},{4,8},{5,9},{8,4},{9,5},{12,0},{13,1},{2,14},{3,15},... | collective-permute-start | bytes 442376 | tf_op jit(solution)/shard_map/ppermute | solution.py:122
  16.5 14.1 %collective-permute-start.6 = (bf16[3,48,512]{2,1,0:T(8,128)(2,1)S(1)}, bf16[3,48,512]{2,1,0:T(8,128)(2,1)S(1)}, u32[]{:S(2)}, u32[]{:S(2)}) collective-permute-start(bf16[3,48,512]{2,1,0:T(8,128)(2,1)S(1)} %get-tuple-element.28), channel_id=1, source_target_pairs={{0,13},{1,12},{4,9},{5,8},{8,5},{9,4},{12,1},{13,0},{2,15},{3,14},... | collective-permute-start | bytes 442376 | tf_op jit(solution)/shard_map/ppermute | solution.py:122
  32.1 3.6 %collective-permute-start.7 = (bf16[8,48,512]{2,1,0:T(8,128)(2,1)S(1)}, bf16[8,48,512]{2,1,0:T(8,128)(2,1)S(1)}, u32[]{:S(2)}, u32[]{:S(2)}) collective-permute-start(bf16[8,48,512]{2,1,0:T(8,128)(2,1)S(1)} %attend.1.own_ref), channel_id=1, source_target_pairs={{2,0},{3,1},{6,4},{7,5},{10,8},{11,9},{14,12},{15,13},{18,16},{19,... | collective-permute-start | bytes 1179656 | tf_op jit(solution)/shard_map/ppermute | solution.py:161
  36.5 11.0 %collective-permute-start.8 = (bf16[48,512]{1,0:T(8,128)(2,1)S(1)}, bf16[48,512]{1,0:T(8,128)(2,1)S(1)}, u32[]{:S(2)}, u32[]{:S(2)}) collective-permute-start(bf16[48,512]{1,0:T(8,128)(2,1)S(1)} %get-tuple-element.30), channel_id=1, source_target_pairs={{0,1},{1,0},{4,5},{5,4},{8,9},{9,8},{12,13},{13,12},{2,3},{3,2},{6... | collective-permute-start | bytes 147464 | tf_op jit(solution)/shard_map/ppermute | solution.py:122
  37.4 12.5 %collective-permute-start.9 = (bf16[48,512]{1,0:T(8,128)(2,1)S(1)}, bf16[48,512]{1,0:T(8,128)(2,1)S(1)}, u32[]{:S(2)}, u32[]{:S(2)}) collective-permute-start(bf16[48,512]{1,0:T(8,128)(2,1)S(1)} %get-tuple-element.31), channel_id=1, source_target_pairs={{0,4},{1,5},{4,0},{5,1},{8,12},{9,13},{12,8},{13,9},{2,6},{3,7},{6... | collective-permute-start | bytes 147464 | tf_op jit(solution)/shard_map/ppermute | solution.py:122
  42.7 9.6 %collective-permute-start.10 = (bf16[48,512]{1,0:T(8,128)(2,1)S(1)}, bf16[48,512]{1,0:T(8,128)(2,1)S(1)}, u32[]{:S(2)}, u32[]{:S(2)}) collective-permute-start(bf16[48,512]{1,0:T(8,128)(2,1)S(1)} %get-tuple-element.32), channel_id=1, source_target_pairs={{0,5},{1,4},{4,1},{5,0},{8,13},{9,12},{12,9},{13,8},{2,7},{3,6},{6... | collective-permute-start | bytes 147464 | tf_op jit(solution)/shard_map/ppermute | solution.py:122
  43.7 8.6 %collective-permute-start.11 = (bf16[48,512]{1,0:T(8,128)(2,1)S(1)}, bf16[48,512]{1,0:T(8,128)(2,1)S(1)}, u32[]{:S(2)}, u32[]{:S(2)}) collective-permute-start(bf16[48,512]{1,0:T(8,128)(2,1)S(1)} %get-tuple-element.33), channel_id=1, source_target_pairs={{0,8},{1,9},{4,12},{5,13},{8,0},{9,1},{12,4},{13,5},{2,10},{3,11},... | collective-permute-start | bytes 147464 | tf_op jit(solution)/shard_map/ppermute | solution.py:122
  47.5 7.6 %collective-permute-start.12 = (bf16[48,512]{1,0:T(8,128)(2,1)S(1)}, bf16[48,512]{1,0:T(8,128)(2,1)S(1)}, u32[]{:S(2)}, u32[]{:S(2)}) collective-permute-start(bf16[48,512]{1,0:T(8,128)(2,1)S(1)} %get-tuple-element.34), channel_id=1, source_target_pairs={{0,9},{1,8},{4,13},{5,12},{8,1},{9,0},{12,5},{13,4},{2,11},{3,10},... | collective-permute-start | bytes 147464 | tf_op jit(solution)/shard_map/ppermute | solution.py:122
  47.5 7.6 %collective-permute-start.13 = (bf16[48,512]{1,0:T(8,128)(2,1)S(1)}, bf16[48,512]{1,0:T(8,128)(2,1)S(1)}, u32[]{:S(2)}, u32[]{:S(2)}) collective-permute-start(bf16[48,512]{1,0:T(8,128)(2,1)S(1)} %get-tuple-element.35), channel_id=1, source_target_pairs={{0,12},{1,13},{4,8},{5,9},{8,4},{9,5},{12,0},{13,1},{2,14},{3,15},... | collective-permute-start | bytes 147464 | tf_op jit(solution)/shard_map/ppermute | solution.py:122
  49.9 6.9 %collective-permute-start.14 = (bf16[48,512]{1,0:T(8,128)(2,1)S(1)}, bf16[48,512]{1,0:T(8,128)(2,1)S(1)}, u32[]{:S(2)}, u32[]{:S(2)}) collective-permute-start(bf16[48,512]{1,0:T(8,128)(2,1)S(1)} %get-tuple-element.36), channel_id=1, source_target_pairs={{0,13},{1,12},{4,9},{5,8},{8,5},{9,4},{12,1},{13,0},{2,15},{3,14},... | collective-permute-start | bytes 147464 | tf_op jit(solution)/shard_map/ppermute | solution.py:122

commit v2 on v0

--- a/solution.py
+++ b/solution.py
@@ -1,14 +1,164 @@
+import functools
 import math
 
 import jax
 import jax.numpy as jnp
 from jax import lax
+from jax.experimental import pallas as pl
+from jax.experimental.pallas import tpu as pltpu
 from jax.sharding import PartitionSpec as P
 
 HD = 128
-
+GROUP = ("seq", "tp")
+VMEM_LIMIT = 32 * 1024 * 1024
 
 key_block = 512
+
+ORDER_IN = (4, 2, 6, 5, 3, 7, 1)
+ORDER_BACK = (4, 6, 5, 7, 2, 3, 1)
+
+
+def group_index():
+    return lax.axis_index("seq") * lax.axis_size("tp") + lax.axis_index("tp")
+
+
+def columns_of(group, step, width):
+    return pl.ds(pl.multiple_of(lax.bitwise_xor(group, step) * width, HD), width)
+
+
+def split_kernel(order, width, rows_ref, *refs):
+    outs, sems = refs[:-1], refs[-1]
+    me = group_index()
+    copies = [
+        pltpu.make_async_copy(
+            rows_ref.at[:, :, columns_of(me, step, width)], outs[n], sems.at[n]
+        )
+        for n, step in enumerate(order)
+    ]
+    for copy in copies:
+        copy.start()
+    for copy in copies:
+        copy.wait()
+
+
+def attend_kernel(count, rows, width, *refs):
+    pieces, out_ref = refs[:count], refs[count]
+    scaling = 1.0 / math.sqrt(HD)
+    for head in range(width // HD):
+        at = slice(head * HD, (head + 1) * HD)
+        queries, keys, values = (
+            jnp.concatenate([piece[n, :, at] for piece in pieces], axis=0) for n in range(3)
+        )
+        scores = lax.dot_general(
+            queries, keys, (((1,), (1,)), ((), ())), preferred_element_type=jnp.float32
+        )
+        highest = jnp.max(scores, axis=1, keepdims=True)
+        weights = jnp.exp((scores - highest) * scaling)
+        totals = jnp.sum(weights, axis=1, keepdims=True)
+        summed = jnp.dot(
+            weights.astype(jnp.bfloat16), values, preferred_element_type=jnp.float32
+        )
+        out_ref[:, :, at] = (summed / totals).astype(jnp.bfloat16).reshape(count, rows, HD)
+
+
+def join_kernel(order_in, order, rows, width, map_ref, perm_ref, gain_ref, own_ref, hint_ref, *outs):
+    me = group_index()
+    tp_count = lax.axis_size("tp")
+    gain = gain_ref[:, columns_of(me, 0, width)]
+    gain = jnp.where(lax.axis_index("branch") == 0, gain, jnp.zeros_like(gain))
+    source_row = lax.broadcasted_iota(jnp.int32, (rows, rows), 0)
+    for n, step in enumerate(order):
+        block = lax.bitwise_xor(me, step)
+        source = map_ref[block // tp_count] * tp_count + block % tp_count
+        distance = lax.bitwise_xor(source, me)
+        place = sum(jnp.where(distance == far, at, 0) for at, far in enumerate(order_in))
+        chosen = (source_row == perm_ref[pl.ds(block, 1), :]).astype(jnp.bfloat16)
+        control = lax.dot_general(
+            chosen, hint_ref[place], (((0,), (0,)), ((), ())), preferred_element_type=jnp.float32
+        )
+        own = own_ref[order_in.index(step)].astype(jnp.float32)
+        outs[n][...] = (own + gain * control).astype(jnp.bfloat16)
+
+
+def merge_kernel(order, width, *refs):
+    pieces, out_ref, sems = refs[:-2], refs[-2], refs[-1]
+    me = group_index()
+    copies = [
+        pltpu.make_async_copy(piece, out_ref.at[:, columns_of(me, step, width)], sems.at[n])
+        for n, (step, piece) in enumerate(zip(order, pieces))
+    ]
+    for copy in copies:
+        copy.start()
+    for copy in copies:
+        copy.wait()
+
+
+def any_specs(number):
+    return [pl.BlockSpec(memory_space=pl.ANY)] * number
+
+
+def vmem_specs(number):
+    return [pl.BlockSpec(memory_space=pltpu.VMEM)] * number
+
+
+PARAMS = pltpu.CompilerParams(vmem_limit_bytes=VMEM_LIMIT)
+
+
+def in_order(order, count):
+    first = [step for step in order if step < count]
+    return first + [step for step in range(1, count) if step not in first] + [0]
+
+
+def exchange(pieces, order):
+    pairs = lambda step: [(i, i ^ step) for i in range(len(order))]
+    return [
+        lax.ppermute(piece, GROUP, pairs(step)) if step else piece
+        for step, piece in zip(order, pieces)
+    ]
+
+
+def by_heads(projected, hint_gain, block_map, token_perm):
+    rows, features = projected.shape[1], projected.shape[3]
+    count = lax.axis_size("seq") * lax.axis_size("tp")
+    width = features // count
+    order_in, order_back = in_order(ORDER_IN, count), in_order(ORDER_BACK, count)
+    dtype = projected.dtype
+    sent = pl.pallas_call(
+        functools.partial(split_kernel, order_in, width),
+        out_shape=[jax.ShapeDtypeStruct((3, rows, width), dtype)] * count,
+        in_specs=any_specs(1),
+        out_specs=any_specs(count),
+        scratch_shapes=[pltpu.SemaphoreType.DMA((count,))],
+        compiler_params=PARAMS,
+        name="split",
+    )(jnp.transpose(projected[0], (1, 0, 2)))
+    attended = pl.pallas_call(
+        functools.partial(attend_kernel, count, rows, width),
+        out_shape=jax.ShapeDtypeStruct((count, rows, width), dtype),
+        in_specs=vmem_specs(count),
+        out_specs=vmem_specs(1)[0],
+        compiler_params=PARAMS,
+        name="attend",
+    )(*exchange(sent, order_in))
+    other = lax.ppermute(attended, "branch", [(0, 1), (1, 0)])
+    joined = pl.pallas_call(
+        functools.partial(join_kernel, order_in, order_back, rows, width),
+        out_shape=[jax.ShapeDtypeStruct((rows, width), dtype)] * count,
+        in_specs=[pl.BlockSpec(memory_space=pltpu.SMEM)] + vmem_specs(4),
+        out_specs=vmem_specs(count),
+        compiler_params=PARAMS,
+        name="join",
+    )(block_map, token_perm, hint_gain[None, :], attended, other)
+    result = pl.pallas_call(
+        functools.partial(merge_kernel, order_back, width),
+        out_shape=jax.ShapeDtypeStruct((rows, features), dtype),
+        in_specs=any_specs(count),
+        out_specs=any_specs(1)[0],
+        scratch_shapes=[pltpu.SemaphoreType.DMA((count,))],
+        compiler_params=PARAMS,
+        name="merge",
+    )(*exchange(joined, order_back))
+    return result[None]
 
 
 def passed_along(x, axis, by):
@@ -61,11 +211,7 @@
     return jnp.transpose(result, (1, 0, 2)).reshape(row_count, columns).astype(jnp.bfloat16)
 
 
-def to_tokens(head_rows):
-    return lax.all_to_all(head_rows, "seq", split_axis=0, concat_axis=1, tiled=True)
-
-
-def on_device(projected, hint_gain, block_map, token_perm):
+def by_heads_and_rows(projected, hint_gain, block_map, token_perm):
     block_rows = projected.shape[1]
     features = projected.shape[3]
     seq_count = lax.axis_size("seq")
@@ -84,8 +230,16 @@
     control = jnp.take(partner, picked, axis=0).astype(jnp.float32)
     gain_slice = lax.dynamic_slice_in_dim(hint_gain, seq_index * columns, columns)
     summed = (attended.astype(jnp.float32) + gain_slice * control).astype(jnp.bfloat16)
-    result = to_tokens(jnp.where(branch_index == 0, summed, attended))
-    return result[None]
+    result = jnp.where(branch_index == 0, summed, attended)
+    return lax.all_to_all(result, "seq", split_axis=0, concat_axis=1, tiled=True)[None]
+
+
+def on_device(projected, hint_gain, block_map, token_perm):
+    count = lax.axis_size("seq") * lax.axis_size("tp")
+    rows, heads = projected.shape[1], projected.shape[3] // HD
+    if heads % count == 0 and count & (count - 1) == 0 and rows % 16 == 0:
+        return by_heads(projected, hint_gain, block_map, token_perm)
+    return by_heads_and_rows(projected, hint_gain, block_map, token_perm)
 
 
 def solution(mesh):

time: 114 us -> 51.2 us (0.45)
  local copies, waits for them, and re-layouts: 36.8 us -> 1.28 us
  blocking collectives: 35.2 us -> 0 us
  starting transfers between devices: 7.74 us -> 31.5 us
  waiting for transfers between devices: 28.1 us -> 14.9 us
  Pallas kernels: 0 us -> 3.37 us
  matrix products: 2.87 us -> 0 us
  other arithmetic: 2.32 us -> 0 us
    ppermute x1 -> x15, starting transfers between devices: 1.29 us -> 31.5 us  [the longest x14 31.4 us: exchange(): lax.ppermute(piece, GROUP, pairs(step))]
    all_to_all x1 -> x0, waiting for transfers between devices: 26 us -> none  [on_device(): lax.all_to_all(projected[0], 'seq', split_axis=2, concat_axis=0, tiled=True)]
    unnamed x14 -> x8, local copies, waits for them, and re-layouts: 24.8 us -> 1.28 us
    all_gather x2 -> x0, blocking collectives: 20.6 us -> none  [the longest x1 10.8 us: attend(): key_piece = lax.all_gather(key_rows, 'tp', axis=0, tiled=True)]
    all_to_all x1 -> x0, blocking collectives: 14.7 us -> none  [to_tokens(): lax.all_to_all(head_rows, 'seq', split_axis=0, concat_axis=1, tiled=True)]
    ppermute x1 -> x15, waiting for transfers between devices: 2.09 us -> 14.9 us  [the longest x14 13.2 us: exchange(): lax.ppermute(piece, GROUP, pairs(step))]
    all_to_all x1 -> x0, starting transfers between devices: 6.45 us -> none  [on_device(): lax.all_to_all(projected[0], 'seq', split_axis=2, concat_axis=0, tiled=True)]
    all_to_all x2 -> x0, local copies, waits for them, and re-layouts: 5.71 us -> none  [the longest x1 5.4 us: on_device(): lax.all_to_all(projected[0], 'seq', split_axis=2, concat_axis=0, tiled=True)]
  transfers between devices with their start and end apart: 2 -> 15, of which waited for: 2 -> 8; matrix products, arithmetic and copies ran while one was open for 2% -> 0% of each run, Pallas kernels for 0% -> 0%
where the time goes in v2:
time: 51.2 us; the launch traced here: 51.1 us
  starting transfers between devices  31.5 us (62%)
  waiting for transfers between devices  14.9 us (29%)
  Pallas kernels  3.37 us (7%)
  local copies, waits for them, and re-layouts  1.28 us (2%)
    ppermute x14, starting transfers between devices, exchange(): lax.ppermute(piece, GROUP, pairs(step))  31.4 us
    ppermute x14, waiting for transfers between devices, exchange(): lax.ppermute(piece, GROUP, pairs(step))  13.2 us
    ppermute x1, waiting for transfers between devices, by_heads(): other = lax.ppermute(attended, 'branch', [(0, 1), (1, 0)])  1.71 us
    pallas_call x1, Pallas kernels, by_heads(): pl.pallas_call(functools.partial(attend_kernel, count, rows, width), out_...  1.46 us
    unnamed x8, local copies, waits for them, and re-layouts  1.28 us
  transfers between devices with their start and end apart: 15, of which 8 were waited for; matrix products, arithmetic and copies ran while one was open for 0% of the time, Pallas kernels for 0%

profile of v2, /device:TPU:0, one launch (start us, length us, event | category | flops | bytes accessed | tf_op | source)
XLA Modules:
  0.0 51.1 jit_solution(15271810384505560733)
XLA Ops:
  0.0 0.0 copy-start
  0.0 1.3 %copy-done = bf16[1,48,3,4096]{3,1,2,0:T(8,128)(2,1)S(1)} copy-done((bf16[1,48,3,4096]{3,1,2,0:T(8,128)(2,1)S(1)}, bf16[1,48,3,4096]{3,1,2,0:T(8,128)(2,1)}, u32[]{:S(2)}) %copy-start) | copy-done | bytes 1179672
  1.3 0.0 copy-start.1
  1.3 0.0 copy-start.2
  1.3 0.0 copy-start.3
  1.3 0.3 split.1
  1.5 4.1 %collective-permute-start = (bf16[3,48,512]{2,1,0:T(8,128)(2,1)S(1)}, bf16[3,48,512]{2,1,0:T(8,128)(2,1)S(1)}, u32[]{:S(2)}, u32[]{:S(2)}) collective-permute-start(bf16[3,48,512]{2,1,0:T(8,128)(2,1)S(1)} %get-tuple-element.21), channel_id=1, source_target_pairs={{0,8},{1,9},{4,12},{5,13},{8,0},{9,1},{12,4},{13,5},{2,10},{3,11},... | collective-permute-start | bytes 442376 | tf_op jit(solution)/shard_map/ppermute | solution.py:115
  5.6 1.6 %collective-permute-start.1 = (bf16[3,48,512]{2,1,0:T(8,128)(2,1)S(1)}, bf16[3,48,512]{2,1,0:T(8,128)(2,1)S(1)}, u32[]{:S(2)}, u32[]{:S(2)}) collective-permute-start(bf16[3,48,512]{2,1,0:T(8,128)(2,1)S(1)} %get-tuple-element.22), channel_id=1, source_target_pairs={{0,4},{1,5},{4,0},{5,1},{8,12},{9,13},{12,8},{13,9},{2,6},{3,7},{6... | collective-permute-start | bytes 442376 | tf_op jit(solution)/shard_map/ppermute | solution.py:115
  7.2 0.0 collective-permute-start.2
  7.2 2.8 %collective-permute-start.3 = (bf16[3,48,512]{2,1,0:T(8,128)(2,1)S(1)}, bf16[3,48,512]{2,1,0:T(8,128)(2,1)S(1)}, u32[]{:S(2)}, u32[]{:S(2)}) collective-permute-start(bf16[3,48,512]{2,1,0:T(8,128)(2,1)S(1)} %get-tuple-element.24), channel_id=1, source_target_pairs={{0,9},{1,8},{4,13},{5,12},{8,1},{9,0},{12,5},{13,4},{2,11},{3,10},... | collective-permute-start | bytes 442376 | tf_op jit(solution)/shard_map/ppermute | solution.py:115
  10.1 2.4 %collective-permute-start.4 = (bf16[3,48,512]{2,1,0:T(8,128)(2,1)S(1)}, bf16[3,48,512]{2,1,0:T(8,128)(2,1)S(1)}, u32[]{:S(2)}, u32[]{:S(2)}) collective-permute-start(bf16[3,48,512]{2,1,0:T(8,128)(2,1)S(1)} %get-tuple-element.25), channel_id=1, source_target_pairs={{0,5},{1,4},{4,1},{5,0},{8,13},{9,12},{12,9},{13,8},{2,7},{3,6},{6... | collective-permute-start | bytes 442376 | tf_op jit(solution)/shard_map/ppermute | solution.py:115
  12.5 1.8 %collective-permute-done.refs_0_ = bf16[3,48,512]{2,1,0:T(8,128)(2,1)S(1)} collective-permute-done((bf16[3,48,512]{2,1,0:T(8,128)(2,1)S(1)}, bf16[3,48,512]{2,1,0:T(8,128)(2,1)S(1)}, u32[]{:S(2)}, u32[]{:S(2)}) %collective-permute-start) | collective-permute-done | bytes 147488 | tf_op jit(solution)/shard_map/ppermute | solution.py:115
  14.3 8.3 %collective-permute-start.5 = (bf16[3,48,512]{2,1,0:T(8,128)(2,1)S(1)}, bf16[3,48,512]{2,1,0:T(8,128)(2,1)S(1)}, u32[]{:S(2)}, u32[]{:S(2)}) collective-permute-start(bf16[3,48,512]{2,1,0:T(8,128)(2,1)S(1)} %get-tuple-element.26), channel_id=1, source_target_pairs={{0,13},{1,12},{4,9},{5,8},{8,5},{9,4},{12,1},{13,0},{2,15},{3,14},... | collective-permute-start | bytes 442376 | tf_op jit(solution)/shard_map/ppermute | solution.py:115
  22.6 0.0 collective-permute-done.1.refs_1_
  22.6 0.5 collective-permute-start.6
  23.1 0.0 collective-permute-done.2.refs_2_
  23.1 7.5 %collective-permute-done.3.refs_3_ = bf16[3,48,512]{2,1,0:T(8,128)(2,1)S(1)} collective-permute-done((bf16[3,48,512]{2,1,0:T(8,128)(2,1)S(1)}, bf16[3,48,512]{2,1,0:T(8,128)(2,1)S(1)}, u32[]{:S(2)}, u32[]{:S(2)}) %collective-permute-start.3) | collective-permute-done | bytes 147488 | tf_op jit(solution)/shard_map/ppermute | solution.py:115
  30.6 0.0 collective-permute-done.4.refs_4_
  30.6 0.0 collective-permute-done.5.refs_5_
  30.6 0.4 collective-permute-done.6.refs_6_
  31.0 1.5 %attend.1.own_ref = bf16[8,48,512]{2,1,0:T(8,128)(2,1)S(1)} custom-call(bf16[3,48,512]{2,1,0:T(8,128)(2,1)S(1)} %collective-permute-done.refs_0_, bf16[3,48,512]{2,1,0:T(8,128)(2,1)S(1)} %collective-permute-done.1.refs_1_, bf16[3,48,512]{2,1,0:T(8,128)(2,1)S(1)} %collective-permute-done.2.refs_2_, bf16[3,48,512]{2,1,0:T(8,128)(2,1)S(1)} %collective-permute-done.3.refs_3_, ...), custom_call_target="tpu_custom_call" | custom-call | tf_op jit(solution)/shard_map/attend/pallas_call | solution.py:135
  32.5 0.1 collective-permute-start.7
  32.6 1.7 %collective-permute-done.7.hint_ref = bf16[8,48,512]{2,1,0:T(8,128)(2,1)S(1)} collective-permute-done((bf16[8,48,512]{2,1,0:T(8,128)(2,1)S(1)}, bf16[8,48,512]{2,1,0:T(8,128)(2,1)S(1)}, u32[]{:S(2)}, u32[]{:S(2)}) %collective-permute-start.7) | collective-permute-done | bytes 393248 | tf_op jit(solution)/shard_map/ppermute | solution.py:143
  34.3 0.0 copy-done.1
  34.3 0.0 copy-done.2
  34.3 0.0 copy-done.3
  34.3 0.8 %join.1 = (bf16[48,512]{1,0:T(8,128)(2,1)S(1)}, bf16[48,512]{1,0:T(8,128)(2,1)S(1)}, bf16[48,512]{1,0:T(8,128)(2,1)S(1)}, bf16[48,512]{1,0:T(8,128)(2,1)S(1)}, b...) custom-call(s32[4]{0:T(128)S(1)} %copy-done.3, ...), custom_call_target="tpu_custom_call" | custom-call | tf_op jit(solution)/shard_map/join/pallas_call | solution.py:144
  35.1 4.3 %collective-permute-start.8 = (bf16[48,512]{1,0:T(8,128)(2,1)S(1)}, bf16[48,512]{1,0:T(8,128)(2,1)S(1)}, u32[]{:S(2)}, u32[]{:S(2)}) collective-permute-start(bf16[48,512]{1,0:T(8,128)(2,1)S(1)} %get-tuple-element.29), channel_id=1, source_target_pairs={{0,8},{1,9},{4,12},{5,13},{8,0},{9,1},{12,4},{13,5},{2,10},{3,11},... | collective-permute-start | bytes 147464 | tf_op jit(solution)/shard_map/ppermute | solution.py:115
  39.4 0.3 collective-permute-start.9
  39.7 0.2 collective-permute-start.10
  39.9 3.4 %collective-permute-start.11 = (bf16[48,512]{1,0:T(8,128)(2,1)S(1)}, bf16[48,512]{1,0:T(8,128)(2,1)S(1)}, u32[]{:S(2)}, u32[]{:S(2)}) collective-permute-start(bf16[48,512]{1,0:T(8,128)(2,1)S(1)} %get-tuple-element.32), channel_id=1, source_target_pairs={{0,13},{1,12},{4,9},{5,8},{8,5},{9,4},{12,1},{13,0},{2,15},{3,14},... | collective-permute-start | bytes 147464 | tf_op jit(solution)/shard_map/ppermute | solution.py:115
  43.3 0.8 %collective-permute-start.12 = (bf16[48,512]{1,0:T(8,128)(2,1)S(1)}, bf16[48,512]{1,0:T(8,128)(2,1)S(1)}, u32[]{:S(2)}, u32[]{:S(2)}) collective-permute-start(bf16[48,512]{1,0:T(8,128)(2,1)S(1)} %get-tuple-element.33), channel_id=1, source_target_pairs={{0,4},{1,5},{4,0},{5,1},{8,12},{9,13},{12,8},{13,9},{2,6},{3,7},{6... | collective-permute-start | bytes 147464 | tf_op jit(solution)/shard_map/ppermute | solution.py:115
  44.1 0.0 collective-permute-done.8.refs_0_
  44.1 2.1 %collective-permute-start.13 = (bf16[48,512]{1,0:T(8,128)(2,1)S(1)}, bf16[48,512]{1,0:T(8,128)(2,1)S(1)}, u32[]{:S(2)}, u32[]{:S(2)}) collective-permute-start(bf16[48,512]{1,0:T(8,128)(2,1)S(1)} %get-tuple-element.34), channel_id=1, source_target_pairs={{0,5},{1,4},{4,1},{5,0},{8,13},{9,12},{12,9},{13,8},{2,7},{3,6},{6... | collective-permute-start | bytes 147464 | tf_op jit(solution)/shard_map/ppermute | solution.py:115
  46.2 0.0 collective-permute-done.9.refs_1_
  46.2 0.6 %collective-permute-start.14 = (bf16[48,512]{1,0:T(8,128)(2,1)S(1)}, bf16[48,512]{1,0:T(8,128)(2,1)S(1)}, u32[]{:S(2)}, u32[]{:S(2)}) collective-permute-start(bf16[48,512]{1,0:T(8,128)(2,1)S(1)} %get-tuple-element.35), channel_id=1, source_target_pairs={{0,1},{1,0},{4,5},{5,4},{8,9},{9,8},{12,13},{13,12},{2,3},{3,2},{6... | collective-permute-start | bytes 147464 | tf_op jit(solution)/shard_map/ppermute | solution.py:115
  46.8 1.2 %collective-permute-done.10.refs_2_ = bf16[48,512]{1,0:T(8,128)(2,1)S(1)} collective-permute-done((bf16[48,512]{1,0:T(8,128)(2,1)S(1)}, bf16[48,512]{1,0:T(8,128)(2,1)S(1)}, u32[]{:S(2)}, u32[]{:S(2)}) %collective-permute-start.10) | collective-permute-done | bytes 49184 | tf_op jit(solution)/shard_map/ppermute | solution.py:115
  48.0 0.0 collective-permute-done.11.refs_3_
  48.0 0.8 %collective-permute-done.12.refs_4_ = bf16[48,512]{1,0:T(8,128)(2,1)S(1)} collective-permute-done((bf16[48,512]{1,0:T(8,128)(2,1)S(1)}, bf16[48,512]{1,0:T(8,128)(2,1)S(1)}, u32[]{:S(2)}, u32[]{:S(2)}) %collective-permute-start.12) | collective-permute-done | bytes 49184 | tf_op jit(solution)/shard_map/ppermute | solution.py:115
  48.8 0.8 %collective-permute-done.13.refs_5_ = bf16[48,512]{1,0:T(8,128)(2,1)S(1)} collective-permute-done((bf16[48,512]{1,0:T(8,128)(2,1)S(1)}, bf16[48,512]{1,0:T(8,128)(2,1)S(1)}, u32[]{:S(2)}, u32[]{:S(2)}) %collective-permute-start.13) | collective-permute-done | bytes 49184 | tf_op jit(solution)/shard_map/ppermute | solution.py:115
  49.6 0.7 %collective-permute-done.14.refs_6_ = bf16[48,512]{1,0:T(8,128)(2,1)S(1)} collective-permute-done((bf16[48,512]{1,0:T(8,128)(2,1)S(1)}, bf16[48,512]{1,0:T(8,128)(2,1)S(1)}, u32[]{:S(2)}, u32[]{:S(2)}) %collective-permute-start.14) | collective-permute-done | bytes 49184 | tf_op jit(solution)/shard_map/ppermute | solution.py:115
  50.3 0.8 %merge.1 = bf16[48,4096]{1,0:T(8,128)(2,1)} custom-call(bf16[48,512]{1,0:T(8,128)(2,1)S(1)} %collective-permute-done.8.refs_0_, bf16[48,512]{1,0:T(8,128)(2,1)S(1)} %collective-permute-done.9.refs_1_, bf16[48,512]{1,0:T(8,128)(2,1)S(1)} %collective-permute-done.10.refs_2_, bf16[48,512]{1,0:T(8,128)(2,1)S(1)} %collective-permute-done.11.refs_3_, ...), custom_call_target="tpu_custom_call" | custom-call | tf_op jit(solution)/shard_map/merge/pallas_call | solution.py:152
Async XLA Ops:
  0.0 1.3 %copy-start = (bf16[1,48,3,4096]{3,1,2,0:T(8,128)(2,1)S(1)}, bf16[1,48,3,4096]{3,1,2,0:T(8,128)(2,1)}, u32[]{:S(2)}) copy-start(bf16[1,48,3,4096]{3,1,2,0:T(8,128)(2,1)} %param.4) | copy-start | bytes 3538948
  1.3 33.0 %copy-start.1 = (f32[4096]{0:T(1024)S(1)}, f32[4096]{0:T(1024)}, u32[]{:S(2)}) copy-start(f32[4096]{0:T(1024)} %param.5) | copy-start | bytes 49156
  1.3 33.0 %copy-start.2 = (s32[8,48]{1,0:T(8,128)S(1)}, s32[8,48]{1,0:T(8,128)}, u32[]{:S(2)}) copy-start(s32[8,48]{1,0:T(8,128)} %perm_ref.1) | copy-start | bytes 4612
  1.3 33.0 %copy-start.3 = (s32[4]{0:T(128)S(1)}, s32[4]{0:T(128)}, u32[]{:S(2)}) copy-start(s32[4]{0:T(128)} %map_ref.1) | copy-start | bytes 52
  1.5 12.8 %collective-permute-start = (bf16[3,48,512]{2,1,0:T(8,128)(2,1)S(1)}, bf16[3,48,512]{2,1,0:T(8,128)(2,1)S(1)}, u32[]{:S(2)}, u32[]{:S(2)}) collective-permute-start(bf16[3,48,512]{2,1,0:T(8,128)(2,1)S(1)} %get-tuple-element.21), channel_id=1, source_target_pairs={{0,8},{1,9},{4,12},{5,13},{8,0},{9,1},{12,4},{13,5},{2,10},{3,11},... | collective-permute-start | bytes 442376 | tf_op jit(solution)/shard_map/ppermute | solution.py:115
  5.6 17.0 %collective-permute-start.1 = (bf16[3,48,512]{2,1,0:T(8,128)(2,1)S(1)}, bf16[3,48,512]{2,1,0:T(8,128)(2,1)S(1)}, u32[]{:S(2)}, u32[]{:S(2)}) collective-permute-start(bf16[3,48,512]{2,1,0:T(8,128)(2,1)S(1)} %get-tuple-element.22), channel_id=1, source_target_pairs={{0,4},{1,5},{4,0},{5,1},{8,12},{9,13},{12,8},{13,9},{2,6},{3,7},{6... | collective-permute-start | bytes 442376 | tf_op jit(solution)/shard_map/ppermute | solution.py:115
  7.2 15.8 %collective-permute-start.2 = (bf16[3,48,512]{2,1,0:T(8,128)(2,1)S(1)}, bf16[3,48,512]{2,1,0:T(8,128)(2,1)S(1)}, u32[]{:S(2)}, u32[]{:S(2)}) collective-permute-start(bf16[3,48,512]{2,1,0:T(8,128)(2,1)S(1)} %get-tuple-element.23), channel_id=1, source_target_pairs={{0,12},{1,13},{4,8},{5,9},{8,4},{9,5},{12,0},{13,1},{2,14},{3,15},... | collective-permute-start | bytes 442376 | tf_op jit(solution)/shard_map/ppermute | solution.py:115
  7.2 23.3 %collective-permute-start.3 = (bf16[3,48,512]{2,1,0:T(8,128)(2,1)S(1)}, bf16[3,48,512]{2,1,0:T(8,128)(2,1)S(1)}, u32[]{:S(2)}, u32[]{:S(2)}) collective-permute-start(bf16[3,48,512]{2,1,0:T(8,128)(2,1)S(1)} %get-tuple-element.24), channel_id=1, source_target_pairs={{0,9},{1,8},{4,13},{5,12},{8,1},{9,0},{12,5},{13,4},{2,11},{3,10},... | collective-permute-start | bytes 442376 | tf_op jit(solution)/shard_map/ppermute | solution.py:115
  10.1 20.5 %collective-permute-start.4 = (bf16[3,48,512]{2,1,0:T(8,128)(2,1)S(1)}, bf16[3,48,512]{2,1,0:T(8,128)(2,1)S(1)}, u32[]{:S(2)}, u32[]{:S(2)}) collective-permute-start(bf16[3,48,512]{2,1,0:T(8,128)(2,1)S(1)} %get-tuple-element.25), channel_id=1, source_target_pairs={{0,5},{1,4},{4,1},{5,0},{8,13},{9,12},{12,9},{13,8},{2,7},{3,6},{6... | collective-permute-start | bytes 442376 | tf_op jit(solution)/shard_map/ppermute | solution.py:115
  14.3 16.3 %collective-permute-start.5 = (bf16[3,48,512]{2,1,0:T(8,128)(2,1)S(1)}, bf16[3,48,512]{2,1,0:T(8,128)(2,1)S(1)}, u32[]{:S(2)}, u32[]{:S(2)}) collective-permute-start(bf16[3,48,512]{2,1,0:T(8,128)(2,1)S(1)} %get-tuple-element.26), channel_id=1, source_target_pairs={{0,13},{1,12},{4,9},{5,8},{8,5},{9,4},{12,1},{13,0},{2,15},{3,14},... | collective-permute-start | bytes 442376 | tf_op jit(solution)/shard_map/ppermute | solution.py:115
  22.6 8.4 %collective-permute-start.6 = (bf16[3,48,512]{2,1,0:T(8,128)(2,1)S(1)}, bf16[3,48,512]{2,1,0:T(8,128)(2,1)S(1)}, u32[]{:S(2)}, u32[]{:S(2)}) collective-permute-start(bf16[3,48,512]{2,1,0:T(8,128)(2,1)S(1)} %get-tuple-element.27), channel_id=1, source_target_pairs={{0,1},{1,0},{4,5},{5,4},{8,9},{9,8},{12,13},{13,12},{2,3},{3,2},{6... | collective-permute-start | bytes 442376 | tf_op jit(solution)/shard_map/ppermute | solution.py:115
  32.5 1.8 %collective-permute-start.7 = (bf16[8,48,512]{2,1,0:T(8,128)(2,1)S(1)}, bf16[8,48,512]{2,1,0:T(8,128)(2,1)S(1)}, u32[]{:S(2)}, u32[]{:S(2)}) collective-permute-start(bf16[8,48,512]{2,1,0:T(8,128)(2,1)S(1)} %attend.1.own_ref), channel_id=1, source_target_pairs={{0,2},{2,0},{1,3},{3,1},{4,6},{6,4},{5,7},{7,5},{8,10},{10,8},{9,1... | collective-permute-start | bytes 1179656 | tf_op jit(solution)/shard_map/ppermute | solution.py:143
  35.1 9.0 %collective-permute-start.8 = (bf16[48,512]{1,0:T(8,128)(2,1)S(1)}, bf16[48,512]{1,0:T(8,128)(2,1)S(1)}, u32[]{:S(2)}, u32[]{:S(2)}) collective-permute-start(bf16[48,512]{1,0:T(8,128)(2,1)S(1)} %get-tuple-element.29), channel_id=1, source_target_pairs={{0,8},{1,9},{4,12},{5,13},{8,0},{9,1},{12,4},{13,5},{2,10},{3,11},... | collective-permute-start | bytes 147464 | tf_op jit(solution)/shard_map/ppermute | solution.py:115
  39.4 6.8 %collective-permute-start.9 = (bf16[48,512]{1,0:T(8,128)(2,1)S(1)}, bf16[48,512]{1,0:T(8,128)(2,1)S(1)}, u32[]{:S(2)}, u32[]{:S(2)}) collective-permute-start(bf16[48,512]{1,0:T(8,128)(2,1)S(1)} %get-tuple-element.30), channel_id=1, source_target_pairs={{0,12},{1,13},{4,8},{5,9},{8,4},{9,5},{12,0},{13,1},{2,14},{3,15},... | collective-permute-start | bytes 147464 | tf_op jit(solution)/shard_map/ppermute | solution.py:115
  39.7 8.3 %collective-permute-start.10 = (bf16[48,512]{1,0:T(8,128)(2,1)S(1)}, bf16[48,512]{1,0:T(8,128)(2,1)S(1)}, u32[]{:S(2)}, u32[]{:S(2)}) collective-permute-start(bf16[48,512]{1,0:T(8,128)(2,1)S(1)} %get-tuple-element.31), channel_id=1, source_target_pairs={{0,9},{1,8},{4,13},{5,12},{8,1},{9,0},{12,5},{13,4},{2,11},{3,10},... | collective-permute-start | bytes 147464 | tf_op jit(solution)/shard_map/ppermute | solution.py:115
  39.9 8.1 %collective-permute-start.11 = (bf16[48,512]{1,0:T(8,128)(2,1)S(1)}, bf16[48,512]{1,0:T(8,128)(2,1)S(1)}, u32[]{:S(2)}, u32[]{:S(2)}) collective-permute-start(bf16[48,512]{1,0:T(8,128)(2,1)S(1)} %get-tuple-element.32), channel_id=1, source_target_pairs={{0,13},{1,12},{4,9},{5,8},{8,5},{9,4},{12,1},{13,0},{2,15},{3,14},... | collective-permute-start | bytes 147464 | tf_op jit(solution)/shard_map/ppermute | solution.py:115
  43.3 5.5 %collective-permute-start.12 = (bf16[48,512]{1,0:T(8,128)(2,1)S(1)}, bf16[48,512]{1,0:T(8,128)(2,1)S(1)}, u32[]{:S(2)}, u32[]{:S(2)}) collective-permute-start(bf16[48,512]{1,0:T(8,128)(2,1)S(1)} %get-tuple-element.33), channel_id=1, source_target_pairs={{0,4},{1,5},{4,0},{5,1},{8,12},{9,13},{12,8},{13,9},{2,6},{3,7},{6... | collective-permute-start | bytes 147464 | tf_op jit(solution)/shard_map/ppermute | solution.py:115
  44.1 5.5 %collective-permute-start.13 = (bf16[48,512]{1,0:T(8,128)(2,1)S(1)}, bf16[48,512]{1,0:T(8,128)(2,1)S(1)}, u32[]{:S(2)}, u32[]{:S(2)}) collective-permute-start(bf16[48,512]{1,0:T(8,128)(2,1)S(1)} %get-tuple-element.34), channel_id=1, source_target_pairs={{0,5},{1,4},{4,1},{5,0},{8,13},{9,12},{12,9},{13,8},{2,7},{3,6},{6... | collective-permute-start | bytes 147464 | tf_op jit(solution)/shard_map/ppermute | solution.py:115
  46.2 4.1 %collective-permute-start.14 = (bf16[48,512]{1,0:T(8,128)(2,1)S(1)}, bf16[48,512]{1,0:T(8,128)(2,1)S(1)}, u32[]{:S(2)}, u32[]{:S(2)}) collective-permute-start(bf16[48,512]{1,0:T(8,128)(2,1)S(1)} %get-tuple-element.35), channel_id=1, source_target_pairs={{0,1},{1,0},{4,5},{5,4},{8,9},{9,8},{12,13},{13,12},{2,3},{3,2},{6... | collective-permute-start | bytes 147464 | tf_op jit(solution)/shard_map/ppermute | solution.py:115

commit v3 on v2

--- a/solution.py
+++ b/solution.py
@@ -14,8 +14,8 @@
 
 key_block = 512
 
-ORDER_IN = (4, 2, 6, 5, 3, 7, 1)
-ORDER_BACK = (4, 6, 5, 7, 2, 3, 1)
+ORDER_IN = (6, 3, 2, 5, 4, 7, 1)
+ORDER_BACK = (7, 6, 4, 5, 3, 2, 1)
 
 
 def group_index():
@@ -44,40 +44,69 @@
 def attend_kernel(count, rows, width, *refs):
     pieces, out_ref = refs[:count], refs[count]
     scaling = 1.0 / math.sqrt(HD)
-    for head in range(width // HD):
-        at = slice(head * HD, (head + 1) * HD)
-        queries, keys, values = (
-            jnp.concatenate([piece[n, :, at] for piece in pieces], axis=0) for n in range(3)
-        )
-        scores = lax.dot_general(
-            queries, keys, (((1,), (1,)), ((), ())), preferred_element_type=jnp.float32
-        )
-        highest = jnp.max(scores, axis=1, keepdims=True)
-        weights = jnp.exp((scores - highest) * scaling)
-        totals = jnp.sum(weights, axis=1, keepdims=True)
-        summed = jnp.dot(
-            weights.astype(jnp.bfloat16), values, preferred_element_type=jnp.float32
-        )
+    heads = [slice(first, first + HD) for first in range(0, width, HD)]
+    joined = lambda n, at: jnp.concatenate([piece[n, :, at] for piece in pieces], axis=0)
+    scores = [
+        lax.dot_general(
+            joined(0, at),
+            joined(1, at),
+            (((1,), (1,)), ((), ())),
+            preferred_element_type=jnp.float32,
+        )
+        for at in heads
+    ]
+    weighted = []
+    for score in scores:
+        highest = jnp.max(score, axis=1, keepdims=True)
+        weights = jnp.exp((score - highest) * scaling)
+        weighted.append((weights.astype(jnp.bfloat16), jnp.sum(weights, axis=1, keepdims=True)))
+    for at, (probs, totals) in zip(heads, weighted):
+        summed = jnp.dot(probs, joined(2, at), preferred_element_type=jnp.float32)
         out_ref[:, :, at] = (summed / totals).astype(jnp.bfloat16).reshape(count, rows, HD)
 
 
-def join_kernel(order_in, order, rows, width, map_ref, perm_ref, gain_ref, own_ref, hint_ref, *outs):
+def choose_kernel(order_in, order, rows, map_ref, perm_ref, out_ref):
     me = group_index()
     tp_count = lax.axis_size("tp")
-    gain = gain_ref[:, columns_of(me, 0, width)]
-    gain = jnp.where(lax.axis_index("branch") == 0, gain, jnp.zeros_like(gain))
-    source_row = lax.broadcasted_iota(jnp.int32, (rows, rows), 0)
+    tokens = len(order) * rows
+    lane = lax.broadcasted_iota(jnp.int32, (1, tokens), 1)
+    row_of = jnp.zeros((1, tokens), jnp.int32)
+    first_of = jnp.zeros((1, tokens), jnp.int32)
     for n, step in enumerate(order):
         block = lax.bitwise_xor(me, step)
         source = map_ref[block // tp_count] * tp_count + block % tp_count
         distance = lax.bitwise_xor(source, me)
         place = sum(jnp.where(distance == far, at, 0) for at, far in enumerate(order_in))
-        chosen = (source_row == perm_ref[pl.ds(block, 1), :]).astype(jnp.bfloat16)
-        control = lax.dot_general(
-            chosen, hint_ref[place], (((0,), (0,)), ((), ())), preferred_element_type=jnp.float32
-        )
+        here = (lane >= n * rows) & (lane < (n + 1) * rows)
+        row_of = jnp.where(here, block, row_of)
+        first_of = jnp.where(here, place * rows, first_of)
+    within = lax.broadcasted_iota(jnp.int32, (rows, tokens), 0)
+    repeat = sum((within + n * rows == lane).astype(jnp.float32) for n in range(len(order)))
+    perms = jnp.dot(
+        perm_ref[...].astype(jnp.float32),
+        repeat,
+        precision=lax.Precision.HIGHEST,
+        preferred_element_type=jnp.float32,
+    )
+    number = lax.broadcasted_iota(jnp.int32, perms.shape, 0)
+    perm = jnp.sum(jnp.where(number == row_of, perms, 0.0), axis=0, keepdims=True)
+    source_token = first_of.astype(jnp.float32) + perm
+    column = lax.broadcasted_iota(jnp.int32, (tokens, tokens), 0).astype(jnp.float32)
+    out_ref[...] = (column == source_token).astype(jnp.float32).T.astype(out_ref.dtype)
+
+
+def join_kernel(order_in, order, rows, width, chosen_ref, gain_ref, own_ref, hint_ref, *outs):
+    gain = gain_ref[:, columns_of(group_index(), 0, width)]
+    gain = jnp.where(lax.axis_index("branch") == 0, gain, jnp.zeros_like(gain))
+    control = jnp.dot(
+        chosen_ref[...],
+        hint_ref[...].reshape(len(order) * rows, width),
+        preferred_element_type=jnp.float32,
+    )
+    for n, step in enumerate(order):
         own = own_ref[order_in.index(step)].astype(jnp.float32)
-        outs[n][...] = (own + gain * control).astype(jnp.bfloat16)
+        added = gain * control[n * rows : (n + 1) * rows]
+        outs[n][...] = (own + added).astype(jnp.bfloat16)
 
 
 def merge_kernel(order, width, *refs):
@@ -132,6 +161,7 @@
         compiler_params=PARAMS,
         name="split",
     )(jnp.transpose(projected[0], (1, 0, 2)))
+    arrived = exchange(sent, order_in)
     attended = pl.pallas_call(
         functools.partial(attend_kernel, count, rows, width),
         out_shape=jax.ShapeDtypeStruct((count, rows, width), dtype),
@@ -139,16 +169,26 @@
         out_specs=vmem_specs(1)[0],
         compiler_params=PARAMS,
         name="attend",
-    )(*exchange(sent, order_in))
+    )(*arrived)
     other = lax.ppermute(attended, "branch", [(0, 1), (1, 0)])
+    block_map, attended = lax.optimization_barrier((block_map, attended))
+    tokens = count * rows
+    chosen = pl.pallas_call(
+        functools.partial(choose_kernel, order_in, order_back, rows),
+        out_shape=jax.ShapeDtypeStruct((tokens, tokens), dtype),
+        in_specs=[pl.BlockSpec(memory_space=pltpu.SMEM)] + vmem_specs(1),
+        out_specs=vmem_specs(1)[0],
+        compiler_params=PARAMS,
+        name="choose",
+    )(block_map, token_perm)
     joined = pl.pallas_call(
         functools.partial(join_kernel, order_in, order_back, rows, width),
         out_shape=[jax.ShapeDtypeStruct((rows, width), dtype)] * count,
-        in_specs=[pl.BlockSpec(memory_space=pltpu.SMEM)] + vmem_specs(4),
+        in_specs=vmem_specs(4),
         out_specs=vmem_specs(count),
         compiler_params=PARAMS,
         name="join",
-    )(block_map, token_perm, hint_gain[None, :], attended, other)
+    )(chosen, hint_gain[None, :], attended, other)
     result = pl.pallas_call(
         functools.partial(merge_kernel, order_back, width),
         out_shape=jax.ShapeDtypeStruct((rows, features), dtype),

time: 51.2 us -> 49.2 us (0.961)
  starting transfers between devices: 31.5 us -> 28.4 us
  waiting for transfers between devices: 14.9 us -> 15.9 us
    ppermute x14, starting transfers between devices: 31.4 us -> 28.3 us  [exchange(): lax.ppermute(piece, GROUP, pairs(step))]
    ppermute x14, waiting for transfers between devices: 13.2 us -> 15.1 us  [exchange(): lax.ppermute(piece, GROUP, pairs(step))]
    ppermute x1, waiting for transfers between devices: 1.71 us -> 0.78 us  [by_heads(): other = lax.ppermute(attended, 'branch', [(0, 1), (1, 0)])]
    pallas_call x0 -> x1, Pallas kernels: none -> 0.9 us  [by_heads(): pl.pallas_call(functools.partial(choose_kernel, order_in, order_back, row...]
  transfers between devices with their start and end apart: 15 -> 15, of which waited for: 8 -> 10; matrix products, arithmetic and copies ran while one was open for 0% -> 0% of each run, Pallas kernels for 0% -> 2%
where the time goes in v3:
time: 49.2 us; the launch traced here: 49 us
  starting transfers between devices  28.4 us (58%)
  waiting for transfers between devices  15.9 us (32%)
  Pallas kernels  3.36 us (7%)
  local copies, waits for them, and re-layouts  1.28 us (3%)
    ppermute x14, starting transfers between devices, exchange(): lax.ppermute(piece, GROUP, pairs(step))  28.3 us
    ppermute x14, waiting for transfers between devices, exchange(): lax.ppermute(piece, GROUP, pairs(step))  15.1 us
    unnamed x8, local copies, waits for them, and re-layouts  1.28 us
    pallas_call x1, Pallas kernels, by_heads(): pl.pallas_call(functools.partial(attend_kernel, count, rows, width), out_...  1.03 us
  transfers between devices with their start and end apart: 15, of which 10 were waited for; matrix products, arithmetic and copies ran while one was open for 0% of the time, Pallas kernels for 2%

profile of v3, /device:TPU:0, one launch (start us, length us, event | category | flops | bytes accessed | tf_op | source)
XLA Modules:
  0.0 49.0 jit_solution(17675529678918506379)
XLA Ops:
  0.0 0.0 copy-start
  0.0 1.3 %copy-done = bf16[1,48,3,4096]{3,1,2,0:T(8,128)(2,1)S(1)} copy-done((bf16[1,48,3,4096]{3,1,2,0:T(8,128)(2,1)S(1)}, bf16[1,48,3,4096]{3,1,2,0:T(8,128)(2,1)}, u32[]{:S(2)}) %copy-start) | copy-done | bytes 1179672
  1.3 0.0 copy-start.2
  1.3 0.0 copy-start.3
  1.3 0.3 split.1
  1.5 0.0 copy-start.1
  1.6 5.1 %collective-permute-start = (bf16[3,48,512]{2,1,0:T(8,128)(2,1)S(1)}, bf16[3,48,512]{2,1,0:T(8,128)(2,1)S(1)}, u32[]{:S(2)}, u32[]{:S(2)}) collective-permute-start(bf16[3,48,512]{2,1,0:T(8,128)(2,1)S(1)} %get-tuple-element.23), channel_id=1, source_target_pairs={{0,12},{1,13},{4,8},{5,9},{8,4},{9,5},{12,0},{13,1},{2,14},{3,15},... | collective-permute-start | bytes 442376 | tf_op jit(solution)/shard_map/ppermute | solution.py:144
  6.7 0.5 collective-permute-start.1
  7.1 2.5 %collective-permute-start.2 = (bf16[3,48,512]{2,1,0:T(8,128)(2,1)S(1)}, bf16[3,48,512]{2,1,0:T(8,128)(2,1)S(1)}, u32[]{:S(2)}, u32[]{:S(2)}) collective-permute-start(bf16[3,48,512]{2,1,0:T(8,128)(2,1)S(1)} %get-tuple-element.25), channel_id=1, source_target_pairs={{0,4},{1,5},{4,0},{5,1},{8,12},{9,13},{12,8},{13,9},{2,6},{3,7},{6... | collective-permute-start | bytes 442376 | tf_op jit(solution)/shard_map/ppermute | solution.py:144
  9.6 0.0 collective-permute-start.3
  9.6 2.9 %collective-permute-start.4 = (bf16[3,48,512]{2,1,0:T(8,128)(2,1)S(1)}, bf16[3,48,512]{2,1,0:T(8,128)(2,1)S(1)}, u32[]{:S(2)}, u32[]{:S(2)}) collective-permute-start(bf16[3,48,512]{2,1,0:T(8,128)(2,1)S(1)} %get-tuple-element.27), channel_id=1, source_target_pairs={{0,8},{1,9},{4,12},{5,13},{8,0},{9,1},{12,4},{13,5},{2,10},{3,11},... | collective-permute-start | bytes 442376 | tf_op jit(solution)/shard_map/ppermute | solution.py:144
  12.5 0.0 collective-permute-done.refs_0_
  12.5 3.6 %collective-permute-start.5 = (bf16[3,48,512]{2,1,0:T(8,128)(2,1)S(1)}, bf16[3,48,512]{2,1,0:T(8,128)(2,1)S(1)}, u32[]{:S(2)}, u32[]{:S(2)}) collective-permute-start(bf16[3,48,512]{2,1,0:T(8,128)(2,1)S(1)} %get-tuple-element.28), channel_id=1, source_target_pairs={{0,13},{1,12},{4,9},{5,8},{8,5},{9,4},{12,1},{13,0},{2,15},{3,14},... | collective-permute-start | bytes 442376 | tf_op jit(solution)/shard_map/ppermute | solution.py:144
  16.1 3.0 %collective-permute-done.1.refs_1_ = bf16[3,48,512]{2,1,0:T(8,128)(2,1)S(1)} collective-permute-done((bf16[3,48,512]{2,1,0:T(8,128)(2,1)S(1)}, bf16[3,48,512]{2,1,0:T(8,128)(2,1)S(1)}, u32[]{:S(2)}, u32[]{:S(2)}) %collective-permute-start.1) | collective-permute-done | bytes 147488 | tf_op jit(solution)/shard_map/ppermute | solution.py:144
  19.1 1.0 %collective-permute-start.6 = (bf16[3,48,512]{2,1,0:T(8,128)(2,1)S(1)}, bf16[3,48,512]{2,1,0:T(8,128)(2,1)S(1)}, u32[]{:S(2)}, u32[]{:S(2)}) collective-permute-start(bf16[3,48,512]{2,1,0:T(8,128)(2,1)S(1)} %get-tuple-element.29), channel_id=1, source_target_pairs={{0,1},{1,0},{4,5},{5,4},{8,9},{9,8},{12,13},{13,12},{2,3},{3,2},{6... | collective-permute-start | bytes 442376 | tf_op jit(solution)/shard_map/ppermute | solution.py:144
  20.1 1.0 %collective-permute-done.2.refs_2_ = bf16[3,48,512]{2,1,0:T(8,128)(2,1)S(1)} collective-permute-done((bf16[3,48,512]{2,1,0:T(8,128)(2,1)S(1)}, bf16[3,48,512]{2,1,0:T(8,128)(2,1)S(1)}, u32[]{:S(2)}, u32[]{:S(2)}) %collective-permute-start.2) | collective-permute-done | bytes 147488 | tf_op jit(solution)/shard_map/ppermute | solution.py:144
  21.0 6.7 %collective-permute-done.3.refs_3_ = bf16[3,48,512]{2,1,0:T(8,128)(2,1)S(1)} collective-permute-done((bf16[3,48,512]{2,1,0:T(8,128)(2,1)S(1)}, bf16[3,48,512]{2,1,0:T(8,128)(2,1)S(1)}, u32[]{:S(2)}, u32[]{:S(2)}) %collective-permute-start.3) | collective-permute-done | bytes 147488 | tf_op jit(solution)/shard_map/ppermute | solution.py:144
  27.7 2.2 %collective-permute-done.4.refs_4_ = bf16[3,48,512]{2,1,0:T(8,128)(2,1)S(1)} collective-permute-done((bf16[3,48,512]{2,1,0:T(8,128)(2,1)S(1)}, bf16[3,48,512]{2,1,0:T(8,128)(2,1)S(1)}, u32[]{:S(2)}, u32[]{:S(2)}) %collective-permute-start.4) | collective-permute-done | bytes 147488 | tf_op jit(solution)/shard_map/ppermute | solution.py:144
  30.0 0.0 collective-permute-done.5.refs_5_
  30.0 0.0 collective-permute-done.6.refs_6_
  30.0 1.0 %attend.1.own_ref = bf16[8,48,512]{2,1,0:T(8,128)(2,1)S(1)} custom-call(bf16[3,48,512]{2,1,0:T(8,128)(2,1)S(1)} %collective-permute-done.refs_0_, bf16[3,48,512]{2,1,0:T(8,128)(2,1)S(1)} %collective-permute-done.1.refs_1_, bf16[3,48,512]{2,1,0:T(8,128)(2,1)S(1)} %collective-permute-done.2.refs_2_, bf16[3,48,512]{2,1,0:T(8,128)(2,1)S(1)} %collective-permute-done.3.refs_3_, ...), custom_call_target="tpu_custom_call" | custom-call | tf_op jit(solution)/shard_map/attend/pallas_call | solution.py:165
  31.0 0.1 collective-permute-start.7
  31.1 0.0 copy-done.2
  31.1 0.0 copy-done.3
  31.1 0.9 %choose.1.chosen_ref = bf16[384,384]{1,0:T(8,128)(2,1)S(1)} custom-call(s32[4]{0:T(128)S(1)} %copy-done.3, s32[8,48]{1,0:T(8,128)S(1)} %copy-done.2), custom_call_target="tpu_custom_call" | custom-call | tf_op jit(solution)/shard_map/choose/pallas_call | solution.py:176
  32.0 0.8 %collective-permute-done.7.hint_ref = bf16[8,48,512]{2,1,0:T(8,128)(2,1)S(1)} collective-permute-done((bf16[8,48,512]{2,1,0:T(8,128)(2,1)S(1)}, bf16[8,48,512]{2,1,0:T(8,128)(2,1)S(1)}, u32[]{:S(2)}, u32[]{:S(2)}) %collective-permute-start.7) | collective-permute-done | bytes 393248 | tf_op jit(solution)/shard_map/ppermute | solution.py:173
  32.8 0.0 copy-done.1
  32.8 0.4 join.1
  33.2 3.2 %collective-permute-start.8 = (bf16[48,512]{1,0:T(8,128)(2,1)S(1)}, bf16[48,512]{1,0:T(8,128)(2,1)S(1)}, u32[]{:S(2)}, u32[]{:S(2)}) collective-permute-start(bf16[48,512]{1,0:T(8,128)(2,1)S(1)} %get-tuple-element.33), channel_id=1, source_target_pairs={{0,13},{1,12},{4,9},{5,8},{8,5},{9,4},{12,1},{13,0},{2,15},{3,14},... | collective-permute-start | bytes 147464 | tf_op jit(solution)/shard_map/ppermute | solution.py:144
  36.4 1.6 %collective-permute-start.9 = (bf16[48,512]{1,0:T(8,128)(2,1)S(1)}, bf16[48,512]{1,0:T(8,128)(2,1)S(1)}, u32[]{:S(2)}, u32[]{:S(2)}) collective-permute-start(bf16[48,512]{1,0:T(8,128)(2,1)S(1)} %get-tuple-element.34), channel_id=1, source_target_pairs={{0,12},{1,13},{4,8},{5,9},{8,4},{9,5},{12,0},{13,1},{2,14},{3,15},... | collective-permute-start | bytes 147464 | tf_op jit(solution)/shard_map/ppermute | solution.py:144
  38.0 1.6 %collective-permute-start.10 = (bf16[48,512]{1,0:T(8,128)(2,1)S(1)}, bf16[48,512]{1,0:T(8,128)(2,1)S(1)}, u32[]{:S(2)}, u32[]{:S(2)}) collective-permute-start(bf16[48,512]{1,0:T(8,128)(2,1)S(1)} %get-tuple-element.35), channel_id=1, source_target_pairs={{0,8},{1,9},{4,12},{5,13},{8,0},{9,1},{12,4},{13,5},{2,10},{3,11},... | collective-permute-start | bytes 147464 | tf_op jit(solution)/shard_map/ppermute | solution.py:144
  39.6 1.3 %collective-permute-start.11 = (bf16[48,512]{1,0:T(8,128)(2,1)S(1)}, bf16[48,512]{1,0:T(8,128)(2,1)S(1)}, u32[]{:S(2)}, u32[]{:S(2)}) collective-permute-start(bf16[48,512]{1,0:T(8,128)(2,1)S(1)} %get-tuple-element.36), channel_id=1, source_target_pairs={{0,9},{1,8},{4,13},{5,12},{8,1},{9,0},{12,5},{13,4},{2,11},{3,10},... | collective-permute-start | bytes 147464 | tf_op jit(solution)/shard_map/ppermute | solution.py:144
  40.9 1.5 %collective-permute-start.12 = (bf16[48,512]{1,0:T(8,128)(2,1)S(1)}, bf16[48,512]{1,0:T(8,128)(2,1)S(1)}, u32[]{:S(2)}, u32[]{:S(2)}) collective-permute-start(bf16[48,512]{1,0:T(8,128)(2,1)S(1)} %get-tuple-element.37), channel_id=1, source_target_pairs={{0,5},{1,4},{4,1},{5,0},{8,13},{9,12},{12,9},{13,8},{2,7},{3,6},{6... | collective-permute-start | bytes 147464 | tf_op jit(solution)/shard_map/ppermute | solution.py:144
  42.4 0.0 collective-permute-done.8.refs_0_
  42.4 1.4 %collective-permute-start.13 = (bf16[48,512]{1,0:T(8,128)(2,1)S(1)}, bf16[48,512]{1,0:T(8,128)(2,1)S(1)}, u32[]{:S(2)}, u32[]{:S(2)}) collective-permute-start(bf16[48,512]{1,0:T(8,128)(2,1)S(1)} %get-tuple-element.38), channel_id=1, source_target_pairs={{0,4},{1,5},{4,0},{5,1},{8,12},{9,13},{12,8},{13,9},{2,6},{3,7},{6... | collective-permute-start | bytes 147464 | tf_op jit(solution)/shard_map/ppermute | solution.py:144
  43.8 0.0 collective-permute-done.9.refs_1_
  43.8 2.1 %collective-permute-start.14 = (bf16[48,512]{1,0:T(8,128)(2,1)S(1)}, bf16[48,512]{1,0:T(8,128)(2,1)S(1)}, u32[]{:S(2)}, u32[]{:S(2)}) collective-permute-start(bf16[48,512]{1,0:T(8,128)(2,1)S(1)} %get-tuple-element.39), channel_id=1, source_target_pairs={{0,1},{1,0},{4,5},{5,4},{8,9},{9,8},{12,13},{13,12},{2,3},{3,2},{6... | collective-permute-start | bytes 147464 | tf_op jit(solution)/shard_map/ppermute | solution.py:144
  45.9 0.5 %collective-permute-done.10.refs_2_ = bf16[48,512]{1,0:T(8,128)(2,1)S(1)} collective-permute-done((bf16[48,512]{1,0:T(8,128)(2,1)S(1)}, bf16[48,512]{1,0:T(8,128)(2,1)S(1)}, u32[]{:S(2)}, u32[]{:S(2)}) %collective-permute-start.10) | collective-permute-done | bytes 49184 | tf_op jit(solution)/shard_map/ppermute | solution.py:144
  46.5 0.9 %collective-permute-done.11.refs_3_ = bf16[48,512]{1,0:T(8,128)(2,1)S(1)} collective-permute-done((bf16[48,512]{1,0:T(8,128)(2,1)S(1)}, bf16[48,512]{1,0:T(8,128)(2,1)S(1)}, u32[]{:S(2)}, u32[]{:S(2)}) %collective-permute-start.11) | collective-permute-done | bytes 49184 | tf_op jit(solution)/shard_map/ppermute | solution.py:144
  47.4 0.3 collective-permute-done.12.refs_4_
  47.7 0.3 collective-permute-done.13.refs_5_
  48.0 0.2 collective-permute-done.14.refs_6_
  48.2 0.8 %merge.1 = bf16[48,4096]{1,0:T(8,128)(2,1)} custom-call(bf16[48,512]{1,0:T(8,128)(2,1)S(1)} %collective-permute-done.8.refs_0_, bf16[48,512]{1,0:T(8,128)(2,1)S(1)} %collective-permute-done.9.refs_1_, bf16[48,512]{1,0:T(8,128)(2,1)S(1)} %collective-permute-done.10.refs_2_, bf16[48,512]{1,0:T(8,128)(2,1)S(1)} %collective-permute-done.11.refs_3_, ...), custom_call_target="tpu_custom_call" | custom-call | tf_op jit(solution)/shard_map/merge/pallas_call | solution.py:192
Async XLA Ops:
  0.0 1.3 %copy-start = (bf16[1,48,3,4096]{3,1,2,0:T(8,128)(2,1)S(1)}, bf16[1,48,3,4096]{3,1,2,0:T(8,128)(2,1)}, u32[]{:S(2)}) copy-start(bf16[1,48,3,4096]{3,1,2,0:T(8,128)(2,1)} %param.4) | copy-start | bytes 3538948
  1.3 29.8 %copy-start.2 = (s32[8,48]{1,0:T(8,128)S(1)}, s32[8,48]{1,0:T(8,128)}, u32[]{:S(2)}) copy-start(s32[8,48]{1,0:T(8,128)} %perm_ref.1) | copy-start | bytes 4612
  1.3 29.8 %copy-start.3 = (s32[4]{0:T(128)S(1)}, s32[4]{0:T(128)}, u32[]{:S(2)}) copy-start(s32[4]{0:T(128)} %map_ref) | copy-start | bytes 52
  1.5 31.3 %copy-start.1 = (f32[4096]{0:T(1024)S(1)}, f32[4096]{0:T(1024)}, u32[]{:S(2)}) copy-start(f32[4096]{0:T(1024)} %param.5) | copy-start | bytes 49156
  1.6 11.0 %collective-permute-start = (bf16[3,48,512]{2,1,0:T(8,128)(2,1)S(1)}, bf16[3,48,512]{2,1,0:T(8,128)(2,1)S(1)}, u32[]{:S(2)}, u32[]{:S(2)}) collective-permute-start(bf16[3,48,512]{2,1,0:T(8,128)(2,1)S(1)} %get-tuple-element.23), channel_id=1, source_target_pairs={{0,12},{1,13},{4,8},{5,9},{8,4},{9,5},{12,0},{13,1},{2,14},{3,15},... | collective-permute-start | bytes 442376 | tf_op jit(solution)/shard_map/ppermute | solution.py:144
  6.7 12.4 %collective-permute-start.1 = (bf16[3,48,512]{2,1,0:T(8,128)(2,1)S(1)}, bf16[3,48,512]{2,1,0:T(8,128)(2,1)S(1)}, u32[]{:S(2)}, u32[]{:S(2)}) collective-permute-start(bf16[3,48,512]{2,1,0:T(8,128)(2,1)S(1)} %get-tuple-element.24), channel_id=1, source_target_pairs={{0,5},{1,4},{4,1},{5,0},{8,13},{9,12},{12,9},{13,8},{2,7},{3,6},{6... | collective-permute-start | bytes 442376 | tf_op jit(solution)/shard_map/ppermute | solution.py:144
  7.1 13.9 %collective-permute-start.2 = (bf16[3,48,512]{2,1,0:T(8,128)(2,1)S(1)}, bf16[3,48,512]{2,1,0:T(8,128)(2,1)S(1)}, u32[]{:S(2)}, u32[]{:S(2)}) collective-permute-start(bf16[3,48,512]{2,1,0:T(8,128)(2,1)S(1)} %get-tuple-element.25), channel_id=1, source_target_pairs={{0,4},{1,5},{4,0},{5,1},{8,12},{9,13},{12,8},{13,9},{2,6},{3,7},{6... | collective-permute-start | bytes 442376 | tf_op jit(solution)/shard_map/ppermute | solution.py:144
  9.6 18.1 %collective-permute-start.3 = (bf16[3,48,512]{2,1,0:T(8,128)(2,1)S(1)}, bf16[3,48,512]{2,1,0:T(8,128)(2,1)S(1)}, u32[]{:S(2)}, u32[]{:S(2)}) collective-permute-start(bf16[3,48,512]{2,1,0:T(8,128)(2,1)S(1)} %get-tuple-element.26), channel_id=1, source_target_pairs={{0,9},{1,8},{4,13},{5,12},{8,1},{9,0},{12,5},{13,4},{2,11},{3,10},... | collective-permute-start | bytes 442376 | tf_op jit(solution)/shard_map/ppermute | solution.py:144
  9.6 20.3 %collective-permute-start.4 = (bf16[3,48,512]{2,1,0:T(8,128)(2,1)S(1)}, bf16[3,48,512]{2,1,0:T(8,128)(2,1)S(1)}, u32[]{:S(2)}, u32[]{:S(2)}) collective-permute-start(bf16[3,48,512]{2,1,0:T(8,128)(2,1)S(1)} %get-tuple-element.27), channel_id=1, source_target_pairs={{0,8},{1,9},{4,12},{5,13},{8,0},{9,1},{12,4},{13,5},{2,10},{3,11},... | collective-permute-start | bytes 442376 | tf_op jit(solution)/shard_map/ppermute | solution.py:144
  12.5 17.4 %collective-permute-start.5 = (bf16[3,48,512]{2,1,0:T(8,128)(2,1)S(1)}, bf16[3,48,512]{2,1,0:T(8,128)(2,1)S(1)}, u32[]{:S(2)}, u32[]{:S(2)}) collective-permute-start(bf16[3,48,512]{2,1,0:T(8,128)(2,1)S(1)} %get-tuple-element.28), channel_id=1, source_target_pairs={{0,13},{1,12},{4,9},{5,8},{8,5},{9,4},{12,1},{13,0},{2,15},{3,14},... | collective-permute-start | bytes 442376 | tf_op jit(solution)/shard_map/ppermute | solution.py:144
  19.1 10.9 %collective-permute-start.6 = (bf16[3,48,512]{2,1,0:T(8,128)(2,1)S(1)}, bf16[3,48,512]{2,1,0:T(8,128)(2,1)S(1)}, u32[]{:S(2)}, u32[]{:S(2)}) collective-permute-start(bf16[3,48,512]{2,1,0:T(8,128)(2,1)S(1)} %get-tuple-element.29), channel_id=1, source_target_pairs={{0,1},{1,0},{4,5},{5,4},{8,9},{9,8},{12,13},{13,12},{2,3},{3,2},{6... | collective-permute-start | bytes 442376 | tf_op jit(solution)/shard_map/ppermute | solution.py:144
  31.0 1.8 %collective-permute-start.7 = (bf16[8,48,512]{2,1,0:T(8,128)(2,1)S(1)}, bf16[8,48,512]{2,1,0:T(8,128)(2,1)S(1)}, u32[]{:S(2)}, u32[]{:S(2)}) collective-permute-start(bf16[8,48,512]{2,1,0:T(8,128)(2,1)S(1)} %attend.1.own_ref), channel_id=1, source_target_pairs={{0,2},{2,0},{1,3},{3,1},{4,6},{6,4},{5,7},{7,5},{8,10},{10,8},{9,1... | collective-permute-start | bytes 1179656 | tf_op jit(solution)/shard_map/ppermute | solution.py:173
  33.2 9.2 %collective-permute-start.8 = (bf16[48,512]{1,0:T(8,128)(2,1)S(1)}, bf16[48,512]{1,0:T(8,128)(2,1)S(1)}, u32[]{:S(2)}, u32[]{:S(2)}) collective-permute-start(bf16[48,512]{1,0:T(8,128)(2,1)S(1)} %get-tuple-element.33), channel_id=1, source_target_pairs={{0,13},{1,12},{4,9},{5,8},{8,5},{9,4},{12,1},{13,0},{2,15},{3,14},... | collective-permute-start | bytes 147464 | tf_op jit(solution)/shard_map/ppermute | solution.py:144
  36.4 7.5 %collective-permute-start.9 = (bf16[48,512]{1,0:T(8,128)(2,1)S(1)}, bf16[48,512]{1,0:T(8,128)(2,1)S(1)}, u32[]{:S(2)}, u32[]{:S(2)}) collective-permute-start(bf16[48,512]{1,0:T(8,128)(2,1)S(1)} %get-tuple-element.34), channel_id=1, source_target_pairs={{0,12},{1,13},{4,8},{5,9},{8,4},{9,5},{12,0},{13,1},{2,14},{3,15},... | collective-permute-start | bytes 147464 | tf_op jit(solution)/shard_map/ppermute | solution.py:144
  38.0 8.5 %collective-permute-start.10 = (bf16[48,512]{1,0:T(8,128)(2,1)S(1)}, bf16[48,512]{1,0:T(8,128)(2,1)S(1)}, u32[]{:S(2)}, u32[]{:S(2)}) collective-permute-start(bf16[48,512]{1,0:T(8,128)(2,1)S(1)} %get-tuple-element.35), channel_id=1, source_target_pairs={{0,8},{1,9},{4,12},{5,13},{8,0},{9,1},{12,4},{13,5},{2,10},{3,11},... | collective-permute-start | bytes 147464 | tf_op jit(solution)/shard_map/ppermute | solution.py:144
  39.6 7.8 %collective-permute-start.11 = (bf16[48,512]{1,0:T(8,128)(2,1)S(1)}, bf16[48,512]{1,0:T(8,128)(2,1)S(1)}, u32[]{:S(2)}, u32[]{:S(2)}) collective-permute-start(bf16[48,512]{1,0:T(8,128)(2,1)S(1)} %get-tuple-element.36), channel_id=1, source_target_pairs={{0,9},{1,8},{4,13},{5,12},{8,1},{9,0},{12,5},{13,4},{2,11},{3,10},... | collective-permute-start | bytes 147464 | tf_op jit(solution)/shard_map/ppermute | solution.py:144
  40.9 6.8 %collective-permute-start.12 = (bf16[48,512]{1,0:T(8,128)(2,1)S(1)}, bf16[48,512]{1,0:T(8,128)(2,1)S(1)}, u32[]{:S(2)}, u32[]{:S(2)}) collective-permute-start(bf16[48,512]{1,0:T(8,128)(2,1)S(1)} %get-tuple-element.37), channel_id=1, source_target_pairs={{0,5},{1,4},{4,1},{5,0},{8,13},{9,12},{12,9},{13,8},{2,7},{3,6},{6... | collective-permute-start | bytes 147464 | tf_op jit(solution)/shard_map/ppermute | solution.py:144
  42.4 5.6 %collective-permute-start.13 = (bf16[48,512]{1,0:T(8,128)(2,1)S(1)}, bf16[48,512]{1,0:T(8,128)(2,1)S(1)}, u32[]{:S(2)}, u32[]{:S(2)}) collective-permute-start(bf16[48,512]{1,0:T(8,128)(2,1)S(1)} %get-tuple-element.38), channel_id=1, source_target_pairs={{0,4},{1,5},{4,0},{5,1},{8,12},{9,13},{12,8},{13,9},{2,6},{3,7},{6... | collective-permute-start | bytes 147464 | tf_op jit(solution)/shard_map/ppermute | solution.py:144
  43.8 4.4 %collective-permute-start.14 = (bf16[48,512]{1,0:T(8,128)(2,1)S(1)}, bf16[48,512]{1,0:T(8,128)(2,1)S(1)}, u32[]{:S(2)}, u32[]{:S(2)}) collective-permute-start(bf16[48,512]{1,0:T(8,128)(2,1)S(1)} %get-tuple-element.39), channel_id=1, source_target_pairs={{0,1},{1,0},{4,5},{5,4},{8,9},{9,8},{12,13},{13,12},{2,3},{3,2},{6... | collective-permute-start | bytes 147464 | tf_op jit(solution)/shard_map/ppermute | solution.py:144

commit v4 on v3

--- a/solution.py
+++ b/solution.py
@@ -9,13 +9,12 @@
 from jax.sharding import PartitionSpec as P
 
 HD = 128
-GROUP = ("seq", "tp")
 VMEM_LIMIT = 32 * 1024 * 1024
 
 key_block = 512
 
-ORDER_IN = (6, 3, 2, 5, 4, 7, 1)
-ORDER_BACK = (7, 6, 4, 5, 3, 2, 1)
+ORDER_IN = ((6, 3, 2, 5, 4, 7, 1), (6, 3, 2, 5, 4, 7, 1))
+ORDER_BACK = ((7, 3, 1, 0), (4, 6, 2, 5))
 
 
 def group_index():
@@ -26,15 +25,14 @@
     return pl.ds(pl.multiple_of(lax.bitwise_xor(group, step) * width, HD), width)
 
 
-def split_kernel(order, width, rows_ref, *refs):
+def split_kernel(orders, width, rows_ref, *refs):
     outs, sems = refs[:-1], refs[-1]
     me = group_index()
-    copies = [
-        pltpu.make_async_copy(
-            rows_ref.at[:, :, columns_of(me, step, width)], outs[n], sems.at[n]
-        )
-        for n, step in enumerate(order)
-    ]
+    copies = []
+    for n, steps in enumerate(zip(*orders)):
+        step = jnp.where(lax.axis_index("branch") == 0, *steps)
+        piece = rows_ref.at[:, :, columns_of(me, step, width)]
+        copies.append(pltpu.make_async_copy(piece, outs[n], sems.at[n]))
     for copy in copies:
         copy.start()
     for copy in copies:
@@ -43,7 +41,7 @@
 
 def attend_kernel(count, rows, width, *refs):
     pieces, out_ref = refs[:count], refs[count]
-    scaling = 1.0 / math.sqrt(HD)
+    scaling = math.log2(math.e) / math.sqrt(HD)
     heads = [slice(first, first + HD) for first in range(0, width, HD)]
     joined = lambda n, at: jnp.concatenate([piece[n, :, at] for piece in pieces], axis=0)
     scores = [
@@ -58,14 +56,23 @@
     weighted = []
     for score in scores:
         highest = jnp.max(score, axis=1, keepdims=True)
-        weights = jnp.exp((score - highest) * scaling)
+        weights = jnp.exp2((score - highest) * scaling)
         weighted.append((weights.astype(jnp.bfloat16), jnp.sum(weights, axis=1, keepdims=True)))
     for at, (probs, totals) in zip(heads, weighted):
         summed = jnp.dot(probs, joined(2, at), preferred_element_type=jnp.float32)
         out_ref[:, :, at] = (summed / totals).astype(jnp.bfloat16).reshape(count, rows, HD)
 
 
-def choose_kernel(order_in, order, rows, map_ref, perm_ref, out_ref):
+def on_branch(work):
+    for branch in range(2):
+        pl.when(lax.axis_index("branch") == branch)(functools.partial(work, branch))
+
+
+def choose_kernel(orders_in, orders, rows, map_ref, perm_ref, out_ref):
+    on_branch(lambda branch: choose(orders_in[1], orders[branch], rows, map_ref, perm_ref, out_ref))
+
+
+def choose(order_in, order, rows, map_ref, perm_ref, out_ref):
     me = group_index()
     tp_count = lax.axis_size("tp")
     tokens = len(order) * rows
@@ -91,35 +98,53 @@
     number = lax.broadcasted_iota(jnp.int32, perms.shape, 0)
     perm = jnp.sum(jnp.where(number == row_of, perms, 0.0), axis=0, keepdims=True)
     source_token = first_of.astype(jnp.float32) + perm
-    column = lax.broadcasted_iota(jnp.int32, (tokens, tokens), 0).astype(jnp.float32)
+    shape = (len(order_in) * rows, tokens)
+    column = lax.broadcasted_iota(jnp.int32, shape, 0).astype(jnp.float32)
     out_ref[...] = (column == source_token).astype(jnp.float32).T.astype(out_ref.dtype)
 
 
-def join_kernel(order_in, order, rows, width, chosen_ref, gain_ref, own_ref, hint_ref, *outs):
-    gain = gain_ref[:, columns_of(group_index(), 0, width)]
-    gain = jnp.where(lax.axis_index("branch") == 0, gain, jnp.zeros_like(gain))
-    control = jnp.dot(
-        chosen_ref[...],
-        hint_ref[...].reshape(len(order) * rows, width),
-        preferred_element_type=jnp.float32,
-    )
-    for n, step in enumerate(order):
-        own = own_ref[order_in.index(step)].astype(jnp.float32)
-        added = gain * control[n * rows : (n + 1) * rows]
-        outs[n][...] = (own + added).astype(jnp.bfloat16)
-
-
-def merge_kernel(order, width, *refs):
-    pieces, out_ref, sems = refs[:-2], refs[-2], refs[-1]
-    me = group_index()
-    copies = [
-        pltpu.make_async_copy(piece, out_ref.at[:, columns_of(me, step, width)], sems.at[n])
-        for n, (step, piece) in enumerate(zip(order, pieces))
-    ]
-    for copy in copies:
-        copy.start()
-    for copy in copies:
-        copy.wait()
+def join_kernel(orders_in, orders, rows, width, chosen_ref, gain_ref, own_ref, other_ref, *outs):
+    def work(branch):
+        base_ref, control_ref = (own_ref, other_ref) if branch == 0 else (other_ref, own_ref)
+        gain = gain_ref[:, columns_of(group_index(), 0, width)]
+        hint = jnp.dot(
+            chosen_ref[...],
+            control_ref[...].reshape(len(orders_in[1]) * rows, width),
+            preferred_element_type=jnp.float32,
+        )
+        for n, step in enumerate(orders[branch]):
+            base = base_ref[orders_in[0].index(step)].astype(jnp.float32)
+            added = gain * hint[n * rows : (n + 1) * rows]
+            outs[n][branch] = (base + added).astype(jnp.bfloat16)
+            outs[n][1 - branch] = control_ref[orders_in[1].index(step)]
+
+    on_branch(work)
+
+
+def take_kernel(in_ref, out_ref):
+    out_ref[...] = in_ref[1]
+
+
+def merge_kernel(orders, width, *refs):
+    out_ref, sems = refs[-2:]
+    count = len(orders[0])
+
+    def work(branch):
+        me = group_index()
+        copies = []
+        for n in range(count):
+            for piece, step in (
+                (refs[n].at[0], orders[branch][n]),
+                (refs[count + n], orders[1 - branch][n]),
+            ):
+                place = out_ref.at[:, columns_of(me, step, width)]
+                copies.append(pltpu.make_async_copy(piece, place, sems.at[len(copies)]))
+        for copy in copies:
+            copy.start()
+        for copy in copies:
+            copy.wait()
+
+    on_branch(work)
 
 
 def any_specs(number):
@@ -138,22 +163,38 @@
     return first + [step for step in range(1, count) if step not in first] + [0]
 
 
-def exchange(pieces, order):
-    pairs = lambda step: [(i, i ^ step) for i in range(len(order))]
-    return [
-        lax.ppermute(piece, GROUP, pairs(step)) if step else piece
-        for step, piece in zip(order, pieces)
-    ]
+def halves(orders, count):
+    known = [[step for step in order if step < count] for order in orders]
+    for step in range(count):
+        if step not in known[0] + known[1]:
+            min(known, key=len).append(step)
+    return known
+
+
+def exchange_by_core(pieces, orders):
+    tp_count = lax.axis_size("tp")
+    groups = range(lax.axis_size("seq") * tp_count)
+    device = lambda group, core: (group // tp_count * 2 + core) * tp_count + group % tp_count
+    arrived = []
+    for piece, steps in zip(pieces, zip(*orders)):
+        pairs = [(device(g, core), device(g ^ steps[core], core)) for g in groups for core in (0, 1)]
+        moved = any(steps)
+        arrived.append(lax.ppermute(piece, ("seq", "branch", "tp"), pairs) if moved else piece)
+    return arrived
 
 
 def by_heads(projected, hint_gain, block_map, token_perm):
     rows, features = projected.shape[1], projected.shape[3]
     count = lax.axis_size("seq") * lax.axis_size("tp")
     width = features // count
-    order_in, order_back = in_order(ORDER_IN, count), in_order(ORDER_BACK, count)
+    orders_in = [in_order(order, count) for order in ORDER_IN]
+    orders_back = halves(ORDER_BACK, count)
+    half = count // 2
+    tokens = count * rows
     dtype = projected.dtype
+    both = [(0, 1), (1, 0)]
     sent = pl.pallas_call(
-        functools.partial(split_kernel, order_in, width),
+        functools.partial(split_kernel, orders_in, width),
         out_shape=[jax.ShapeDtypeStruct((3, rows, width), dtype)] * count,
         in_specs=any_specs(1),
         out_specs=any_specs(count),
@@ -161,7 +202,6 @@
         compiler_params=PARAMS,
         name="split",
     )(jnp.transpose(projected[0], (1, 0, 2)))
-    arrived = exchange(sent, order_in)
     attended = pl.pallas_call(
         functools.partial(attend_kernel, count, rows, width),
         out_shape=jax.ShapeDtypeStruct((count, rows, width), dtype),
@@ -169,35 +209,46 @@
         out_specs=vmem_specs(1)[0],
         compiler_params=PARAMS,
         name="attend",
-    )(*arrived)
-    other = lax.ppermute(attended, "branch", [(0, 1), (1, 0)])
+    )(*exchange_by_core(sent, orders_in))
+    other = lax.ppermute(attended, "branch", both)
     block_map, attended = lax.optimization_barrier((block_map, attended))
-    tokens = count * rows
     chosen = pl.pallas_call(
-        functools.partial(choose_kernel, order_in, order_back, rows),
-        out_shape=jax.ShapeDtypeStruct((tokens, tokens), dtype),
+        functools.partial(choose_kernel, orders_in, orders_back, rows),
+        out_shape=jax.ShapeDtypeStruct((half * rows, tokens), dtype),
         in_specs=[pl.BlockSpec(memory_space=pltpu.SMEM)] + vmem_specs(1),
         out_specs=vmem_specs(1)[0],
         compiler_params=PARAMS,
         name="choose",
     )(block_map, token_perm)
     joined = pl.pallas_call(
-        functools.partial(join_kernel, order_in, order_back, rows, width),
-        out_shape=[jax.ShapeDtypeStruct((rows, width), dtype)] * count,
+        functools.partial(join_kernel, orders_in, orders_back, rows, width),
+        out_shape=[jax.ShapeDtypeStruct((2, rows, width), dtype)] * half,
         in_specs=vmem_specs(4),
-        out_specs=vmem_specs(count),
+        out_specs=vmem_specs(half),
         compiler_params=PARAMS,
         name="join",
     )(chosen, hint_gain[None, :], attended, other)
+    returned = exchange_by_core(joined, orders_back)
+    passed = []
+    for piece in returned:
+        taken = pl.pallas_call(
+            take_kernel,
+            out_shape=jax.ShapeDtypeStruct((rows, width), dtype),
+            in_specs=vmem_specs(1),
+            out_specs=vmem_specs(1)[0],
+            compiler_params=PARAMS,
+            name="take",
+        )(piece)
+        passed.append(lax.ppermute(taken, "branch", both))
     result = pl.pallas_call(
-        functools.partial(merge_kernel, order_back, width),
+        functools.partial(merge_kernel, orders_back, width),
         out_shape=jax.ShapeDtypeStruct((rows, features), dtype),
         in_specs=any_specs(count),
         out_specs=any_specs(1)[0],
         scratch_shapes=[pltpu.SemaphoreType.DMA((count,))],
         compiler_params=PARAMS,
         name="merge",
-    )(*exchange(joined, order_back))
+    )(*returned, *passed)
     return result[None]
 
 

time: 49.2 us -> 47.5 us (0.965)
  starting transfers between devices: 28.4 us -> 25.5 us
  waiting for transfers between devices: 15.9 us -> 17.2 us
    ppermute x15 -> x16, starting transfers between devices: 28.4 us -> 25.5 us  [the longest x11 22.6 us: exchange_by_core(): lax.ppermute(piece, ('seq', 'branch', 'tp'), pairs)]
    ppermute x15 -> x16, waiting for transfers between devices: 15.9 us -> 17.2 us  [the longest x11 15.5 us: exchange_by_core(): lax.ppermute(piece, ('seq', 'branch', 'tp'), pairs)]
    pallas_call x4 -> x8, Pallas kernels: 2.32 us -> 2.19 us  [the longest x1 0.85 us: by_heads(): pl.pallas_call(functools.partial(choose_kernel, orders_in, orders_back, r...]
  transfers between devices with their start and end apart: 15 -> 16, of which waited for: 10 -> 8; matrix products, arithmetic and copies ran while one was open for 0% -> 0% of each run, Pallas kernels for 2% -> 2%
where the time goes in v4:
time: 47.5 us; the launch traced here: 47.2 us
  starting transfers between devices  25.5 us (54%)
  waiting for transfers between devices  17.2 us (36%)
  Pallas kernels  3.12 us (7%)
  local copies, waits for them, and re-layouts  1.28 us (3%)
    ppermute x11, starting transfers between devices, exchange_by_core(): lax.ppermute(piece, ('seq', 'branch', 'tp'), pairs)  22.6 us
    ppermute x11, waiting for transfers between devices, exchange_by_core(): lax.ppermute(piece, ('seq', 'branch', 'tp'), pairs)  15.5 us
    ppermute x4, starting transfers between devices, by_heads(): passed.append(lax.ppermute(taken, 'branch', both))  2.79 us
    unnamed x8, local copies, waits for them, and re-layouts  1.28 us
  transfers between devices with their start and end apart: 16, of which 8 were waited for; matrix products, arithmetic and copies ran while one was open for 0% of the time, Pallas kernels for 2%

profile of v4, /device:TPU:0, one launch (start us, length us, event | category | flops | bytes accessed | tf_op | source)
XLA Modules:
  0.0 47.2 jit_solution(13087380372663814059)
XLA Ops:
  0.0 0.0 copy-start
  0.0 1.3 %copy-done = bf16[1,48,3,4096]{3,1,2,0:T(8,128)(2,1)S(1)} copy-done((bf16[1,48,3,4096]{3,1,2,0:T(8,128)(2,1)S(1)}, bf16[1,48,3,4096]{3,1,2,0:T(8,128)(2,1)}, u32[]{:S(2)}) %copy-start) | copy-done | bytes 1179672
  1.3 0.0 copy-start.2
  1.3 0.0 copy-start.3
  1.3 0.0 copy-start.1
  1.3 0.3 split.1
  1.5 5.1 %collective-permute-start = (bf16[3,48,512]{2,1,0:T(8,128)(2,1)S(1)}, bf16[3,48,512]{2,1,0:T(8,128)(2,1)S(1)}, u32[]{:S(2)}, u32[]{:S(2)}) collective-permute-start(bf16[3,48,512]{2,1,0:T(8,128)(2,1)S(1)} %get-tuple-element.19), channel_id=1, source_target_pairs={{0,12},{2,14},{1,13},{3,15},{4,8},{6,10},{5,9},{7,11},{8,4},{10,6}... | collective-permute-start | bytes 442376 | tf_op jit(solution)/shard_map/ppermute | solution.py:182
  6.7 0.5 %collective-permute-start.1 = (bf16[3,48,512]{2,1,0:T(8,128)(2,1)S(1)}, bf16[3,48,512]{2,1,0:T(8,128)(2,1)S(1)}, u32[]{:S(2)}, u32[]{:S(2)}) collective-permute-start(bf16[3,48,512]{2,1,0:T(8,128)(2,1)S(1)} %get-tuple-element.20), channel_id=1, source_target_pairs={{0,5},{2,7},{1,4},{3,6},{4,1},{6,3},{5,0},{7,2},{8,13},{10,15},{9,... | collective-permute-start | bytes 442376 | tf_op jit(solution)/shard_map/ppermute | solution.py:182
  7.1 2.5 %collective-permute-start.2 = (bf16[3,48,512]{2,1,0:T(8,128)(2,1)S(1)}, bf16[3,48,512]{2,1,0:T(8,128)(2,1)S(1)}, u32[]{:S(2)}, u32[]{:S(2)}) collective-permute-start(bf16[3,48,512]{2,1,0:T(8,128)(2,1)S(1)} %get-tuple-element.21), channel_id=1, source_target_pairs={{0,4},{2,6},{1,5},{3,7},{4,0},{6,2},{5,1},{7,3},{8,12},{10,14},{9,... | collective-permute-start | bytes 442376 | tf_op jit(solution)/shard_map/ppermute | solution.py:182
  9.6 0.0 collective-permute-start.3
  9.6 2.9 %collective-permute-start.4 = (bf16[3,48,512]{2,1,0:T(8,128)(2,1)S(1)}, bf16[3,48,512]{2,1,0:T(8,128)(2,1)S(1)}, u32[]{:S(2)}, u32[]{:S(2)}) collective-permute-start(bf16[3,48,512]{2,1,0:T(8,128)(2,1)S(1)} %get-tuple-element.23), channel_id=1, source_target_pairs={{0,8},{2,10},{1,9},{3,11},{4,12},{6,14},{5,13},{7,15},{8,0},{10,2}... | collective-permute-start | bytes 442376 | tf_op jit(solution)/shard_map/ppermute | solution.py:182
  12.5 0.0 collective-permute-done.refs_0_
  12.5 3.6 %collective-permute-start.5 = (bf16[3,48,512]{2,1,0:T(8,128)(2,1)S(1)}, bf16[3,48,512]{2,1,0:T(8,128)(2,1)S(1)}, u32[]{:S(2)}, u32[]{:S(2)}) collective-permute-start(bf16[3,48,512]{2,1,0:T(8,128)(2,1)S(1)} %get-tuple-element.24), channel_id=1, source_target_pairs={{0,13},{2,15},{1,12},{3,14},{4,9},{6,11},{5,8},{7,10},{8,5},{10,7}... | collective-permute-start | bytes 442376 | tf_op jit(solution)/shard_map/ppermute | solution.py:182
  16.1 3.0 %collective-permute-done.1.refs_1_ = bf16[3,48,512]{2,1,0:T(8,128)(2,1)S(1)} collective-permute-done((bf16[3,48,512]{2,1,0:T(8,128)(2,1)S(1)}, bf16[3,48,512]{2,1,0:T(8,128)(2,1)S(1)}, u32[]{:S(2)}, u32[]{:S(2)}) %collective-permute-start.1) | collective-permute-done | bytes 147488 | tf_op jit(solution)/shard_map/ppermute | solution.py:182
  19.1 1.0 %collective-permute-start.6 = (bf16[3,48,512]{2,1,0:T(8,128)(2,1)S(1)}, bf16[3,48,512]{2,1,0:T(8,128)(2,1)S(1)}, u32[]{:S(2)}, u32[]{:S(2)}) collective-permute-start(bf16[3,48,512]{2,1,0:T(8,128)(2,1)S(1)} %get-tuple-element.25), channel_id=1, source_target_pairs={{0,1},{2,3},{1,0},{3,2},{4,5},{6,7},{5,4},{7,6},{8,9},{10,11},{9,8... | collective-permute-start | bytes 442376 | tf_op jit(solution)/shard_map/ppermute | solution.py:182
  20.0 1.0 %collective-permute-done.2.refs_2_ = bf16[3,48,512]{2,1,0:T(8,128)(2,1)S(1)} collective-permute-done((bf16[3,48,512]{2,1,0:T(8,128)(2,1)S(1)}, bf16[3,48,512]{2,1,0:T(8,128)(2,1)S(1)}, u32[]{:S(2)}, u32[]{:S(2)}) %collective-permute-start.2) | collective-permute-done | bytes 147488 | tf_op jit(solution)/shard_map/ppermute | solution.py:182
  21.0 6.7 %collective-permute-done.3.refs_3_ = bf16[3,48,512]{2,1,0:T(8,128)(2,1)S(1)} collective-permute-done((bf16[3,48,512]{2,1,0:T(8,128)(2,1)S(1)}, bf16[3,48,512]{2,1,0:T(8,128)(2,1)S(1)}, u32[]{:S(2)}, u32[]{:S(2)}) %collective-permute-start.3) | collective-permute-done | bytes 147488 | tf_op jit(solution)/shard_map/ppermute | solution.py:182
  27.7 2.2 %collective-permute-done.4.refs_4_ = bf16[3,48,512]{2,1,0:T(8,128)(2,1)S(1)} collective-permute-done((bf16[3,48,512]{2,1,0:T(8,128)(2,1)S(1)}, bf16[3,48,512]{2,1,0:T(8,128)(2,1)S(1)}, u32[]{:S(2)}, u32[]{:S(2)}) %collective-permute-start.4) | collective-permute-done | bytes 147488 | tf_op jit(solution)/shard_map/ppermute | solution.py:182
  30.0 0.0 collective-permute-done.5.refs_5_
  30.0 0.0 collective-permute-done.6.refs_6_
  30.0 0.9 %attend.1.own_ref = bf16[8,48,512]{2,1,0:T(8,128)(2,1)S(1)} custom-call(bf16[3,48,512]{2,1,0:T(8,128)(2,1)S(1)} %collective-permute-done.refs_0_, bf16[3,48,512]{2,1,0:T(8,128)(2,1)S(1)} %collective-permute-done.1.refs_1_, bf16[3,48,512]{2,1,0:T(8,128)(2,1)S(1)} %collective-permute-done.2.refs_2_, bf16[3,48,512]{2,1,0:T(8,128)(2,1)S(1)} %collective-permute-done.3.refs_3_, ...), custom_call_target="tpu_custom_call" | custom-call | tf_op jit(solution)/shard_map/attend/pallas_call | solution.py:205
  30.9 0.1 collective-permute-start.7
  31.0 0.0 copy-done.2
  31.0 0.0 copy-done.3
  31.0 0.8 %choose.1.chosen_ref = bf16[192,384]{1,0:T(8,128)(2,1)S(1)} custom-call(s32[4]{0:T(128)S(1)} %copy-done.3, s32[8,48]{1,0:T(8,128)S(1)} %copy-done.2), custom_call_target="tpu_custom_call" | custom-call | tf_op jit(solution)/shard_map/choose/pallas_call | solution.py:215
  31.9 0.8 %collective-permute-done.7.other_ref = bf16[8,48,512]{2,1,0:T(8,128)(2,1)S(1)} collective-permute-done((bf16[8,48,512]{2,1,0:T(8,128)(2,1)S(1)}, bf16[8,48,512]{2,1,0:T(8,128)(2,1)S(1)}, u32[]{:S(2)}, u32[]{:S(2)}) %collective-permute-start.7) | collective-permute-done | bytes 393248 | tf_op jit(solution)/shard_map/ppermute | solution.py:213
  32.7 0.0 copy-done.1
  32.7 0.3 join.1
  33.0 3.2 %collective-permute-start.8 = (bf16[2,48,512]{2,1,0:T(8,128)(2,1)S(1)}, bf16[2,48,512]{2,1,0:T(8,128)(2,1)S(1)}, u32[]{:S(2)}, u32[]{:S(2)}) collective-permute-start(bf16[2,48,512]{2,1,0:T(8,128)(2,1)S(1)} %get-tuple-element.29), channel_id=1, source_target_pairs={{0,13},{2,10},{1,12},{3,11},{4,9},{6,14},{5,8},{7,15},{8,5},{10,2}... | collective-permute-start | bytes 294920 | tf_op jit(solution)/shard_map/ppermute | solution.py:182
  36.2 2.6 %collective-permute-start.9 = (bf16[2,48,512]{2,1,0:T(8,128)(2,1)S(1)}, bf16[2,48,512]{2,1,0:T(8,128)(2,1)S(1)}, u32[]{:S(2)}, u32[]{:S(2)}) collective-permute-start(bf16[2,48,512]{2,1,0:T(8,128)(2,1)S(1)} %get-tuple-element.30), channel_id=1, source_target_pairs={{0,5},{2,14},{1,4},{3,15},{4,1},{6,10},{5,0},{7,11},{8,13},{10,6},... | collective-permute-start | bytes 294920 | tf_op jit(solution)/shard_map/ppermute | solution.py:182
  38.8 0.5 %collective-permute-start.10 = (bf16[2,48,512]{2,1,0:T(8,128)(2,1)S(1)}, bf16[2,48,512]{2,1,0:T(8,128)(2,1)S(1)}, u32[]{:S(2)}, u32[]{:S(2)}) collective-permute-start(bf16[2,48,512]{2,1,0:T(8,128)(2,1)S(1)} %get-tuple-element.31), channel_id=1, source_target_pairs={{0,1},{2,6},{1,0},{3,7},{4,5},{6,2},{5,4},{7,3},{8,9},{10,14},{9,8... | collective-permute-start | bytes 294920 | tf_op jit(solution)/shard_map/ppermute | solution.py:182
  39.4 0.7 %collective-permute-start.11 = (bf16[2,48,512]{2,1,0:T(8,128)(2,1)S(1)}, bf16[2,48,512]{2,1,0:T(8,128)(2,1)S(1)}, u32[]{:S(2)}, u32[]{:S(2)}) collective-permute-start(bf16[2,48,512]{2,1,0:T(8,128)(2,1)S(1)} %get-tuple-element.32), channel_id=1, source_target_pairs={{0,0},{2,11},{1,1},{3,10},{4,4},{6,15},{5,5},{7,14},{8,8},{10,3},{... | collective-permute-start | bytes 294920 | tf_op jit(solution)/shard_map/ppermute | solution.py:182
  40.0 1.3 %collective-permute-done.8.in_ref.refs_0_ = bf16[2,48,512]{2,1,0:T(8,128)(2,1)S(1)} collective-permute-done((bf16[2,48,512]{2,1,0:T(8,128)(2,1)S(1)}, bf16[2,48,512]{2,1,0:T(8,128)(2,1)S(1)}, u32[]{:S(2)}, u32[]{:S(2)}) %collective-permute-start.8) | collective-permute-done | bytes 98336 | tf_op jit(solution)/shard_map/ppermute | solution.py:182
  41.4 1.4 %collective-permute-start.12 = (bf16[48,512]{1,0:T(8,128)(2,1)S(1)}, bf16[48,512]{1,0:T(8,128)(2,1)S(1)}, u32[]{:S(2)}, u32[]{:S(2)}) collective-permute-start(bf16[48,512]{1,0:T(8,128)(2,1)S(1)} %take.4), channel_id=1, source_target_pairs={{0,2},{2,0},{1,3},{3,1},{4,6},{6,4},{5,7},{7,5},{8,10},{10,8},{9,1... | collective-permute-start | bytes 147464 | tf_op jit(solution)/shard_map/ppermute | solution.py:242
  42.7 1.3 %collective-permute-done.9.in_ref.refs_1_ = bf16[2,48,512]{2,1,0:T(8,128)(2,1)S(1)} collective-permute-done((bf16[2,48,512]{2,1,0:T(8,128)(2,1)S(1)}, bf16[2,48,512]{2,1,0:T(8,128)(2,1)S(1)}, u32[]{:S(2)}, u32[]{:S(2)}) %collective-permute-start.9) | collective-permute-done | bytes 98336 | tf_op jit(solution)/shard_map/ppermute | solution.py:182
  44.0 0.0 collective-permute-start.13
  44.0 0.0 collective-permute-done.10.in_ref.refs_2_
  44.1 0.5 %collective-permute-start.14 = (bf16[48,512]{1,0:T(8,128)(2,1)S(1)}, bf16[48,512]{1,0:T(8,128)(2,1)S(1)}, u32[]{:S(2)}, u32[]{:S(2)}) collective-permute-start(bf16[48,512]{1,0:T(8,128)(2,1)S(1)} %take.6), channel_id=1, source_target_pairs={{0,2},{2,0},{1,3},{3,1},{4,6},{6,4},{5,7},{7,5},{8,10},{10,8},{9,1... | collective-permute-start | bytes 147464 | tf_op jit(solution)/shard_map/ppermute | solution.py:242
  44.6 0.0 collective-permute-done.11.in_ref.refs_3_
  44.6 0.9 %collective-permute-start.15 = (bf16[48,512]{1,0:T(8,128)(2,1)S(1)}, bf16[48,512]{1,0:T(8,128)(2,1)S(1)}, u32[]{:S(2)}, u32[]{:S(2)}) collective-permute-start(bf16[48,512]{1,0:T(8,128)(2,1)S(1)} %take.7), channel_id=1, source_target_pairs={{0,2},{2,0},{1,3},{3,1},{4,6},{6,4},{5,7},{7,5},{8,10},{10,8},{9,1... | collective-permute-start | bytes 147464 | tf_op jit(solution)/shard_map/ppermute | solution.py:242
  45.5 0.0 collective-permute-done.12.refs_4_
  45.5 0.0 collective-permute-done.13.refs_5_
  45.5 0.0 collective-permute-done.14.refs_6_
  45.5 0.9 %collective-permute-done.15.refs_7_ = bf16[48,512]{1,0:T(8,128)(2,1)S(1)} collective-permute-done((bf16[48,512]{1,0:T(8,128)(2,1)S(1)}, bf16[48,512]{1,0:T(8,128)(2,1)S(1)}, u32[]{:S(2)}, u32[]{:S(2)}) %collective-permute-start.15) | collective-permute-done | bytes 49184 | tf_op jit(solution)/shard_map/ppermute | solution.py:242
  46.4 0.8 %merge.1 = bf16[48,4096]{1,0:T(8,128)(2,1)} custom-call(bf16[2,48,512]{2,1,0:T(8,128)(2,1)S(1)} %collective-permute-done.8.in_ref.refs_0_, bf16[2,48,512]{2,1,0:T(8,128)(2,1)S(1)} %collective-permute-done.9.in_ref.refs_1_, bf16[2,48,512]{2,1,0:T(8,128)(2,1)S(1)} %collective-permute-done.10.in_ref.refs_2_, ...), custom_call_target="tpu_custom_call" | custom-call | tf_op jit(solution)/shard_map/merge/pallas_call | solution.py:243
  (4 shorter events, 0.0 us)
Async XLA Ops:
  0.0 1.3 %copy-start = (bf16[1,48,3,4096]{3,1,2,0:T(8,128)(2,1)S(1)}, bf16[1,48,3,4096]{3,1,2,0:T(8,128)(2,1)}, u32[]{:S(2)}) copy-start(bf16[1,48,3,4096]{3,1,2,0:T(8,128)(2,1)} %param.4) | copy-start | bytes 3538948
  1.3 29.7 %copy-start.2 = (s32[8,48]{1,0:T(8,128)S(1)}, s32[8,48]{1,0:T(8,128)}, u32[]{:S(2)}) copy-start(s32[8,48]{1,0:T(8,128)} %perm_ref.1) | copy-start | bytes 4612
  1.3 29.7 %copy-start.3 = (s32[4]{0:T(128)S(1)}, s32[4]{0:T(128)}, u32[]{:S(2)}) copy-start(s32[4]{0:T(128)} %map_ref) | copy-start | bytes 52
  1.3 31.4 %copy-start.1 = (f32[4096]{0:T(1024)S(1)}, f32[4096]{0:T(1024)}, u32[]{:S(2)}) copy-start(f32[4096]{0:T(1024)} %param.5) | copy-start | bytes 49156
  1.5 11.0 %collective-permute-start = (bf16[3,48,512]{2,1,0:T(8,128)(2,1)S(1)}, bf16[3,48,512]{2,1,0:T(8,128)(2,1)S(1)}, u32[]{:S(2)}, u32[]{:S(2)}) collective-permute-start(bf16[3,48,512]{2,1,0:T(8,128)(2,1)S(1)} %get-tuple-element.19), channel_id=1, source_target_pairs={{0,12},{2,14},{1,13},{3,15},{4,8},{6,10},{5,9},{7,11},{8,4},{10,6}... | collective-permute-start | bytes 442376 | tf_op jit(solution)/shard_map/ppermute | solution.py:182
  6.7 12.4 %collective-permute-start.1 = (bf16[3,48,512]{2,1,0:T(8,128)(2,1)S(1)}, bf16[3,48,512]{2,1,0:T(8,128)(2,1)S(1)}, u32[]{:S(2)}, u32[]{:S(2)}) collective-permute-start(bf16[3,48,512]{2,1,0:T(8,128)(2,1)S(1)} %get-tuple-element.20), channel_id=1, source_target_pairs={{0,5},{2,7},{1,4},{3,6},{4,1},{6,3},{5,0},{7,2},{8,13},{10,15},{9,... | collective-permute-start | bytes 442376 | tf_op jit(solution)/shard_map/ppermute | solution.py:182
  7.1 13.9 %collective-permute-start.2 = (bf16[3,48,512]{2,1,0:T(8,128)(2,1)S(1)}, bf16[3,48,512]{2,1,0:T(8,128)(2,1)S(1)}, u32[]{:S(2)}, u32[]{:S(2)}) collective-permute-start(bf16[3,48,512]{2,1,0:T(8,128)(2,1)S(1)} %get-tuple-element.21), channel_id=1, source_target_pairs={{0,4},{2,6},{1,5},{3,7},{4,0},{6,2},{5,1},{7,3},{8,12},{10,14},{9,... | collective-permute-start | bytes 442376 | tf_op jit(solution)/shard_map/ppermute | solution.py:182
  9.6 18.1 %collective-permute-start.3 = (bf16[3,48,512]{2,1,0:T(8,128)(2,1)S(1)}, bf16[3,48,512]{2,1,0:T(8,128)(2,1)S(1)}, u32[]{:S(2)}, u32[]{:S(2)}) collective-permute-start(bf16[3,48,512]{2,1,0:T(8,128)(2,1)S(1)} %get-tuple-element.22), channel_id=1, source_target_pairs={{0,9},{2,11},{1,8},{3,10},{4,13},{6,15},{5,12},{7,14},{8,1},{10,3}... | collective-permute-start | bytes 442376 | tf_op jit(solution)/shard_map/ppermute | solution.py:182
  9.6 20.3 %collective-permute-start.4 = (bf16[3,48,512]{2,1,0:T(8,128)(2,1)S(1)}, bf16[3,48,512]{2,1,0:T(8,128)(2,1)S(1)}, u32[]{:S(2)}, u32[]{:S(2)}) collective-permute-start(bf16[3,48,512]{2,1,0:T(8,128)(2,1)S(1)} %get-tuple-element.23), channel_id=1, source_target_pairs={{0,8},{2,10},{1,9},{3,11},{4,12},{6,14},{5,13},{7,15},{8,0},{10,2}... | collective-permute-start | bytes 442376 | tf_op jit(solution)/shard_map/ppermute | solution.py:182
  12.5 17.4 %collective-permute-start.5 = (bf16[3,48,512]{2,1,0:T(8,128)(2,1)S(1)}, bf16[3,48,512]{2,1,0:T(8,128)(2,1)S(1)}, u32[]{:S(2)}, u32[]{:S(2)}) collective-permute-start(bf16[3,48,512]{2,1,0:T(8,128)(2,1)S(1)} %get-tuple-element.24), channel_id=1, source_target_pairs={{0,13},{2,15},{1,12},{3,14},{4,9},{6,11},{5,8},{7,10},{8,5},{10,7}... | collective-permute-start | bytes 442376 | tf_op jit(solution)/shard_map/ppermute | solution.py:182
  19.1 10.9 %collective-permute-start.6 = (bf16[3,48,512]{2,1,0:T(8,128)(2,1)S(1)}, bf16[3,48,512]{2,1,0:T(8,128)(2,1)S(1)}, u32[]{:S(2)}, u32[]{:S(2)}) collective-permute-start(bf16[3,48,512]{2,1,0:T(8,128)(2,1)S(1)} %get-tuple-element.25), channel_id=1, source_target_pairs={{0,1},{2,3},{1,0},{3,2},{4,5},{6,7},{5,4},{7,6},{8,9},{10,11},{9,8... | collective-permute-start | bytes 442376 | tf_op jit(solution)/shard_map/ppermute | solution.py:182
  30.9 1.8 %collective-permute-start.7 = (bf16[8,48,512]{2,1,0:T(8,128)(2,1)S(1)}, bf16[8,48,512]{2,1,0:T(8,128)(2,1)S(1)}, u32[]{:S(2)}, u32[]{:S(2)}) collective-permute-start(bf16[8,48,512]{2,1,0:T(8,128)(2,1)S(1)} %attend.1.own_ref), channel_id=1, source_target_pairs={{0,2},{2,0},{1,3},{3,1},{4,6},{6,4},{5,7},{7,5},{8,10},{10,8},{9,1... | collective-permute-start | bytes 1179656 | tf_op jit(solution)/shard_map/ppermute | solution.py:213
  33.0 8.4 %collective-permute-start.8 = (bf16[2,48,512]{2,1,0:T(8,128)(2,1)S(1)}, bf16[2,48,512]{2,1,0:T(8,128)(2,1)S(1)}, u32[]{:S(2)}, u32[]{:S(2)}) collective-permute-start(bf16[2,48,512]{2,1,0:T(8,128)(2,1)S(1)} %get-tuple-element.29), channel_id=1, source_target_pairs={{0,13},{2,10},{1,12},{3,11},{4,9},{6,14},{5,8},{7,15},{8,5},{10,2}... | collective-permute-start | bytes 294920 | tf_op jit(solution)/shard_map/ppermute | solution.py:182
  36.2 7.9 %collective-permute-start.9 = (bf16[2,48,512]{2,1,0:T(8,128)(2,1)S(1)}, bf16[2,48,512]{2,1,0:T(8,128)(2,1)S(1)}, u32[]{:S(2)}, u32[]{:S(2)}) collective-permute-start(bf16[2,48,512]{2,1,0:T(8,128)(2,1)S(1)} %get-tuple-element.30), channel_id=1, source_target_pairs={{0,5},{2,14},{1,4},{3,15},{4,1},{6,10},{5,0},{7,11},{8,13},{10,6},... | collective-permute-start | bytes 294920 | tf_op jit(solution)/shard_map/ppermute | solution.py:182
  38.8 5.2 %collective-permute-start.10 = (bf16[2,48,512]{2,1,0:T(8,128)(2,1)S(1)}, bf16[2,48,512]{2,1,0:T(8,128)(2,1)S(1)}, u32[]{:S(2)}, u32[]{:S(2)}) collective-permute-start(bf16[2,48,512]{2,1,0:T(8,128)(2,1)S(1)} %get-tuple-element.31), channel_id=1, source_target_pairs={{0,1},{2,6},{1,0},{3,7},{4,5},{6,2},{5,4},{7,3},{8,9},{10,14},{9,8... | collective-permute-start | bytes 294920 | tf_op jit(solution)/shard_map/ppermute | solution.py:182
  39.4 5.3 %collective-permute-start.11 = (bf16[2,48,512]{2,1,0:T(8,128)(2,1)S(1)}, bf16[2,48,512]{2,1,0:T(8,128)(2,1)S(1)}, u32[]{:S(2)}, u32[]{:S(2)}) collective-permute-start(bf16[2,48,512]{2,1,0:T(8,128)(2,1)S(1)} %get-tuple-element.32), channel_id=1, source_target_pairs={{0,0},{2,11},{1,1},{3,10},{4,4},{6,15},{5,5},{7,14},{8,8},{10,3},{... | collective-permute-start | bytes 294920 | tf_op jit(solution)/shard_map/ppermute | solution.py:182
  41.4 4.1 %collective-permute-start.12 = (bf16[48,512]{1,0:T(8,128)(2,1)S(1)}, bf16[48,512]{1,0:T(8,128)(2,1)S(1)}, u32[]{:S(2)}, u32[]{:S(2)}) collective-permute-start(bf16[48,512]{1,0:T(8,128)(2,1)S(1)} %take.4), channel_id=1, source_target_pairs={{0,2},{2,0},{1,3},{3,1},{4,6},{6,4},{5,7},{7,5},{8,10},{10,8},{9,1... | collective-permute-start | bytes 147464 | tf_op jit(solution)/shard_map/ppermute | solution.py:242
  44.0 1.5 %collective-permute-start.13 = (bf16[48,512]{1,0:T(8,128)(2,1)S(1)}, bf16[48,512]{1,0:T(8,128)(2,1)S(1)}, u32[]{:S(2)}, u32[]{:S(2)}) collective-permute-start(bf16[48,512]{1,0:T(8,128)(2,1)S(1)} %take.5), channel_id=1, source_target_pairs={{0,2},{2,0},{1,3},{3,1},{4,6},{6,4},{5,7},{7,5},{8,10},{10,8},{9,1... | collective-permute-start | bytes 147464 | tf_op jit(solution)/shard_map/ppermute | solution.py:242
  44.1 1.5 %collective-permute-start.14 = (bf16[48,512]{1,0:T(8,128)(2,1)S(1)}, bf16[48,512]{1,0:T(8,128)(2,1)S(1)}, u32[]{:S(2)}, u32[]{:S(2)}) collective-permute-start(bf16[48,512]{1,0:T(8,128)(2,1)S(1)} %take.6), channel_id=1, source_target_pairs={{0,2},{2,0},{1,3},{3,1},{4,6},{6,4},{5,7},{7,5},{8,10},{10,8},{9,1... | collective-permute-start | bytes 147464 | tf_op jit(solution)/shard_map/ppermute | solution.py:242
  44.6 1.8 %collective-permute-start.15 = (bf16[48,512]{1,0:T(8,128)(2,1)S(1)}, bf16[48,512]{1,0:T(8,128)(2,1)S(1)}, u32[]{:S(2)}, u32[]{:S(2)}) collective-permute-start(bf16[48,512]{1,0:T(8,128)(2,1)S(1)} %take.7), channel_id=1, source_target_pairs={{0,2},{2,0},{1,3},{3,1},{4,6},{6,4},{5,7},{7,5},{8,10},{10,8},{9,1... | collective-permute-start | bytes 147464 | tf_op jit(solution)/shard_map/ppermute | solution.py:242

commit v5 on v4

--- a/solution.py
+++ b/solution.py
@@ -13,8 +13,10 @@
 
 key_block = 512
 
-ORDER_IN = ((6, 3, 2, 5, 4, 7, 1), (6, 3, 2, 5, 4, 7, 1))
-ORDER_BACK = ((7, 3, 1, 0), (4, 6, 2, 5))
+ORDER_IN = ((4, 3, 2, 5, 6, 7, 1), (6, 1, 2, 4, 5, 7, 3))
+ORDER_BACK = ((6, 3, 1), (7, 5, 2))
+STRAIGHT = (4,)
+STRAIGHT_FIRST = False
 
 
 def group_index():
@@ -39,10 +41,10 @@
         copy.wait()
 
 
-def attend_kernel(count, rows, width, *refs):
+def attend_kernel(count, rows, start, stop, *refs):
     pieces, out_ref = refs[:count], refs[count]
     scaling = math.log2(math.e) / math.sqrt(HD)
-    heads = [slice(first, first + HD) for first in range(0, width, HD)]
+    heads = [slice(first, first + HD) for first in range(start, stop, HD)]
     joined = lambda n, at: jnp.concatenate([piece[n, :, at] for piece in pieces], axis=0)
     scores = [
         lax.dot_general(
@@ -60,7 +62,8 @@
         weighted.append((weights.astype(jnp.bfloat16), jnp.sum(weights, axis=1, keepdims=True)))
     for at, (probs, totals) in zip(heads, weighted):
         summed = jnp.dot(probs, joined(2, at), preferred_element_type=jnp.float32)
-        out_ref[:, :, at] = (summed / totals).astype(jnp.bfloat16).reshape(count, rows, HD)
+        place = slice(at.start - start, at.stop - start)
+        out_ref[:, :, place] = (summed / totals).astype(jnp.bfloat16).reshape(count, rows, HD)
 
 
 def on_branch(work):
@@ -103,20 +106,30 @@
     out_ref[...] = (column == source_token).astype(jnp.float32).T.astype(out_ref.dtype)
 
 
-def join_kernel(orders_in, orders, rows, width, chosen_ref, gain_ref, own_ref, other_ref, *outs):
+def join_kernel(orders_in, orders, straight, rows, width, chosen_ref, gain_ref, own_refs, other_refs, *outs):
     def work(branch):
-        base_ref, control_ref = (own_ref, other_ref) if branch == 0 else (other_ref, own_ref)
-        gain = gain_ref[:, columns_of(group_index(), 0, width)]
-        hint = jnp.dot(
-            chosen_ref[...],
-            control_ref[...].reshape(len(orders_in[1]) * rows, width),
-            preferred_element_type=jnp.float32,
-        )
-        for n, step in enumerate(orders[branch]):
-            base = base_ref[orders_in[0].index(step)].astype(jnp.float32)
-            added = gain * hint[n * rows : (n + 1) * rows]
-            outs[n][branch] = (base + added).astype(jnp.bfloat16)
-            outs[n][1 - branch] = control_ref[orders_in[1].index(step)]
+        base_refs, control_refs = (own_refs, other_refs) if branch == 0 else (other_refs, own_refs)
+        start = 0
+        for base_ref, control_ref in zip(base_refs, control_refs):
+            stop = start + base_ref.shape[2]
+            at = slice(start, stop)
+            gain = gain_ref[:, at]
+            hint = jnp.dot(
+                chosen_ref[...],
+                control_ref[...].reshape(len(orders_in[1]) * rows, stop - start),
+                preferred_element_type=jnp.float32,
+            )
+            for n, step in enumerate(orders[branch] + straight + [0]):
+                control = control_ref[orders_in[1].index(step)]
+                base = base_ref[orders_in[0].index(step)].astype(jnp.float32)
+                added = gain * hint[n * rows : (n + 1) * rows]
+                joined = (base + added).astype(jnp.bfloat16)
+                if n < len(orders[branch]):
+                    outs[n][branch, :, at] = joined
+                    outs[n][1 - branch, :, at] = control
+                else:
+                    outs[n][:, at] = joined if branch == 0 else control
+            start = stop
 
     on_branch(work)
 
@@ -125,20 +138,22 @@
     out_ref[...] = in_ref[1]
 
 
-def merge_kernel(orders, width, *refs):
+def merge_kernel(orders, straight, width, *refs):
     out_ref, sems = refs[-2:]
-    count = len(orders[0])
+    if STRAIGHT_FIRST:
+        own_refs, pair_refs, passed_refs = refs[:-2]
+    else:
+        pair_refs, passed_refs, own_refs = refs[:-2]
 
     def work(branch):
         me = group_index()
+        pieces = [(ref.at[0], step) for ref, step in zip(pair_refs, orders[branch])]
+        pieces += zip(passed_refs, orders[1 - branch])
+        pieces += zip(own_refs, straight + [0])
         copies = []
-        for n in range(count):
-            for piece, step in (
-                (refs[n].at[0], orders[branch][n]),
-                (refs[count + n], orders[1 - branch][n]),
-            ):
-                place = out_ref.at[:, columns_of(me, step, width)]
-                copies.append(pltpu.make_async_copy(piece, place, sems.at[len(copies)]))
+        for n, (piece, step) in enumerate(pieces):
+            place = out_ref.at[:, columns_of(me, step, width)]
+            copies.append(pltpu.make_async_copy(piece, place, sems.at[n]))
         for copy in copies:
             copy.start()
         for copy in copies:
@@ -163,12 +178,13 @@
     return first + [step for step in range(1, count) if step not in first] + [0]
 
 
-def halves(orders, count):
-    known = [[step for step in order if step < count] for order in orders]
-    for step in range(count):
-        if step not in known[0] + known[1]:
-            min(known, key=len).append(step)
-    return known
+def back_plan(count):
+    orders, straight = [list(order) for order in ORDER_BACK], list(STRAIGHT)
+    steps = list(range(1, count))
+    if sorted(orders[0] + orders[1] + straight) != steps:
+        half = len(steps) // 2
+        orders, straight = [steps[:half], steps[half : 2 * half]], steps[2 * half :]
+    return orders, straight
 
 
 def exchange_by_core(pieces, orders):
@@ -188,9 +204,11 @@
     count = lax.axis_size("seq") * lax.axis_size("tp")
     width = features // count
     orders_in = [in_order(order, count) for order in ORDER_IN]
-    orders_back = halves(ORDER_BACK, count)
-    half = count // 2
-    tokens = count * rows
+    orders_back, straight = back_plan(count)
+    pairs = len(orders_back[0])
+    stays = len(straight) + 1
+    middle = width // HD // 2 * HD
+    parts = [(0, width)]
     dtype = projected.dtype
     both = [(0, 1), (1, 0)]
     sent = pl.pallas_call(
@@ -202,35 +220,41 @@
         compiler_params=PARAMS,
         name="split",
     )(jnp.transpose(projected[0], (1, 0, 2)))
-    attended = pl.pallas_call(
-        functools.partial(attend_kernel, count, rows, width),
-        out_shape=jax.ShapeDtypeStruct((count, rows, width), dtype),
-        in_specs=vmem_specs(count),
-        out_specs=vmem_specs(1)[0],
-        compiler_params=PARAMS,
-        name="attend",
-    )(*exchange_by_core(sent, orders_in))
-    other = lax.ppermute(attended, "branch", both)
-    block_map, attended = lax.optimization_barrier((block_map, attended))
+    arrived = exchange_by_core(sent, orders_in)
+    attended = [
+        pl.pallas_call(
+            functools.partial(attend_kernel, count, rows, start, stop),
+            out_shape=jax.ShapeDtypeStruct((count, rows, stop - start), dtype),
+            in_specs=vmem_specs(count),
+            out_specs=vmem_specs(1)[0],
+            compiler_params=PARAMS,
+            name="attend",
+        )(*arrived)
+        for start, stop in parts
+    ]
+    other = [lax.ppermute(part, "branch", both) for part in attended]
+    block_map, attended[-1] = lax.optimization_barrier((block_map, attended[-1]))
     chosen = pl.pallas_call(
-        functools.partial(choose_kernel, orders_in, orders_back, rows),
-        out_shape=jax.ShapeDtypeStruct((half * rows, tokens), dtype),
+        functools.partial(choose_kernel, orders_in, [order + straight + [0] for order in orders_back], rows),
+        out_shape=jax.ShapeDtypeStruct(((pairs + stays) * rows, count * rows), dtype),
         in_specs=[pl.BlockSpec(memory_space=pltpu.SMEM)] + vmem_specs(1),
         out_specs=vmem_specs(1)[0],
         compiler_params=PARAMS,
         name="choose",
     )(block_map, token_perm)
+    gain = lax.dynamic_slice_in_dim(hint_gain, group_index() * width, width)[None, :]
     joined = pl.pallas_call(
-        functools.partial(join_kernel, orders_in, orders_back, rows, width),
-        out_shape=[jax.ShapeDtypeStruct((2, rows, width), dtype)] * half,
-        in_specs=vmem_specs(4),
-        out_specs=vmem_specs(half),
+        functools.partial(join_kernel, orders_in, orders_back, straight, rows, width),
+        out_shape=[jax.ShapeDtypeStruct((2, rows, width), dtype)] * pairs
+        + [jax.ShapeDtypeStruct((rows, width), dtype)] * stays,
+        in_specs=vmem_specs(2) + [vmem_specs(len(parts))] * 2,
+        out_specs=vmem_specs(pairs + stays),
         compiler_params=PARAMS,
         name="join",
-    )(chosen, hint_gain[None, :], attended, other)
-    returned = exchange_by_core(joined, orders_back)
+    )(chosen, gain, attended, other)
+    returned = exchange_by_core(joined, [order + straight + [0] for order in orders_back])
     passed = []
-    for piece in returned:
+    for piece in returned[:pairs]:
         taken = pl.pallas_call(
             take_kernel,
             out_shape=jax.ShapeDtypeStruct((rows, width), dtype),
@@ -240,15 +264,17 @@
             name="take",
         )(piece)
         passed.append(lax.ppermute(taken, "branch", both))
+    groups = [returned[:pairs], passed]
+    groups.insert(0 if STRAIGHT_FIRST else 2, returned[pairs:])
     result = pl.pallas_call(
-        functools.partial(merge_kernel, orders_back, width),
+        functools.partial(merge_kernel, orders_back, straight, width),
         out_shape=jax.ShapeDtypeStruct((rows, features), dtype),
-        in_specs=any_specs(count),
+        in_specs=[any_specs(len(group)) for group in groups],
         out_specs=any_specs(1)[0],
         scratch_shapes=[pltpu.SemaphoreType.DMA((count,))],
         compiler_params=PARAMS,
         name="merge",
-    )(*returned, *passed)
+    )(*groups)
     return result[None]
 
 

time: 47.5 us -> 45.9 us (0.966)
  waiting for transfers between devices: 17.2 us -> 12.8 us
  starting transfers between devices: 25.5 us -> 27.7 us
  local copies, waits for them, and re-layouts: 1.28 us -> 2.04 us
    ppermute x11, waiting for transfers between devices: 15.5 us -> 12.8 us  [exchange_by_core(): lax.ppermute(piece, ('seq', 'branch', 'tp'), pairs)]
    ppermute x1, starting transfers between devices: 0.07 us -> 1.15 us  [by_heads(): other = [lax.ppermute(part, 'branch', both) for part in attended]]
    ppermute x11, starting transfers between devices: 22.6 us -> 23.5 us  [exchange_by_core(): lax.ppermute(piece, ('seq', 'branch', 'tp'), pairs)]
    ppermute x1, waiting for transfers between devices: 0.84 us -> 0.01 us  [by_heads(): other = [lax.ppermute(part, 'branch', both) for part in attended]]
    ppermute x4 -> x3, waiting for transfers between devices: 0.88 us -> 0.05 us  [by_heads(): passed.append(lax.ppermute(taken, 'branch', both))]
    dynamic_slice x0 -> x1, local copies, waits for them, and re-layouts: none -> 0.76 us  [by_heads(): lax.dynamic_slice_in_dim(hint_gain, group_index() * width, width)[None, :]]
    ppermute x4 -> x3, starting transfers between devices: 2.79 us -> 2.99 us  [by_heads(): passed.append(lax.ppermute(taken, 'branch', both))]
    unnamed x8 -> x6, local copies, waits for them, and re-layouts: 1.28 us -> 1.28 us
  transfers between devices with their start and end apart: 16 -> 15, of which waited for: 8 -> 5; matrix products, arithmetic and copies ran while one was open for 0% -> 2% of each run, Pallas kernels for 2% -> 2%
where the time goes in v5:
time: 45.9 us; the launch traced here: 45.7 us
  starting transfers between devices  27.7 us (60%)
  waiting for transfers between devices  12.8 us (28%)
  Pallas kernels  3.16 us (7%)
  local copies, waits for them, and re-layouts  2.04 us (4%)
    ppermute x11, starting transfers between devices, exchange_by_core(): lax.ppermute(piece, ('seq', 'branch', 'tp'), pairs)  23.5 us
    ppermute x11, waiting for transfers between devices, exchange_by_core(): lax.ppermute(piece, ('seq', 'branch', 'tp'), pairs)  12.8 us
    ppermute x3, starting transfers between devices, by_heads(): passed.append(lax.ppermute(taken, 'branch', both))  2.99 us
    unnamed x6, local copies, waits for them, and re-layouts  1.28 us
    ppermute x1, starting transfers between devices, by_heads(): other = [lax.ppermute(part, 'branch', both) for part in attended]  1.15 us
    pallas_call x1, Pallas kernels, by_heads(): pl.pallas_call(functools.partial(attend_kernel, count, rows, start, stop)...  0.94 us
  transfers between devices with their start and end apart: 15, of which 5 were waited for; matrix products, arithmetic and copies ran while one was open for 2% of the time, Pallas kernels for 2%

profile of v5, /device:TPU:0, one launch (start us, length us, event | category | flops | bytes accessed | tf_op | source)
XLA Modules:
  0.0 45.7 jit_solution(11210486825060211286)
XLA Ops:
  0.0 0.0 copy-start
  0.0 1.3 %copy-done = bf16[1,48,3,4096]{3,1,2,0:T(8,128)(2,1)S(1)} copy-done((bf16[1,48,3,4096]{3,1,2,0:T(8,128)(2,1)S(1)}, bf16[1,48,3,4096]{3,1,2,0:T(8,128)(2,1)}, u32[]{:S(2)}) %copy-start) | copy-done | bytes 1179672
  1.3 0.0 copy-start.1
  1.3 0.0 copy-start.2
  1.3 0.3 split.1
  1.5 4.1 %collective-permute-start = (bf16[3,48,512]{2,1,0:T(8,128)(2,1)S(1)}, bf16[3,48,512]{2,1,0:T(8,128)(2,1)S(1)}, u32[]{:S(2)}, u32[]{:S(2)}) collective-permute-start(bf16[3,48,512]{2,1,0:T(8,128)(2,1)S(1)} %get-tuple-element.20), channel_id=1, source_target_pairs={{0,8},{2,14},{1,9},{3,15},{4,12},{6,10},{5,13},{7,11},{8,0},{10,6}... | collective-permute-start | bytes 442376 | tf_op jit(solution)/shard_map/ppermute | solution.py:198
  5.6 2.5 %collective-permute-start.1 = (bf16[3,48,512]{2,1,0:T(8,128)(2,1)S(1)}, bf16[3,48,512]{2,1,0:T(8,128)(2,1)S(1)}, u32[]{:S(2)}, u32[]{:S(2)}) collective-permute-start(bf16[3,48,512]{2,1,0:T(8,128)(2,1)S(1)} %get-tuple-element.21), channel_id=1, source_target_pairs={{0,5},{2,3},{1,4},{3,2},{4,1},{6,7},{5,0},{7,6},{8,13},{10,11},{9,... | collective-permute-start | bytes 442376 | tf_op jit(solution)/shard_map/ppermute | solution.py:198
  8.1 0.4 collective-permute-start.2
  8.6 0.1 collective-permute-start.3
  8.6 3.9 %collective-permute-start.4 = (bf16[3,48,512]{2,1,0:T(8,128)(2,1)S(1)}, bf16[3,48,512]{2,1,0:T(8,128)(2,1)S(1)}, u32[]{:S(2)}, u32[]{:S(2)}) collective-permute-start(bf16[3,48,512]{2,1,0:T(8,128)(2,1)S(1)} %get-tuple-element.24), channel_id=1, source_target_pairs={{0,12},{2,11},{1,13},{3,10},{4,8},{6,15},{5,9},{7,14},{8,4},{10,3}... | collective-permute-start | bytes 442376 | tf_op jit(solution)/shard_map/ppermute | solution.py:198
  12.5 1.9 %collective-permute-done.refs_0_ = bf16[3,48,512]{2,1,0:T(8,128)(2,1)S(1)} collective-permute-done((bf16[3,48,512]{2,1,0:T(8,128)(2,1)S(1)}, bf16[3,48,512]{2,1,0:T(8,128)(2,1)S(1)}, u32[]{:S(2)}, u32[]{:S(2)}) %collective-permute-start) | collective-permute-done | bytes 147488 | tf_op jit(solution)/shard_map/ppermute | solution.py:198
  14.4 3.8 %collective-permute-start.5 = (bf16[3,48,512]{2,1,0:T(8,128)(2,1)S(1)}, bf16[3,48,512]{2,1,0:T(8,128)(2,1)S(1)}, u32[]{:S(2)}, u32[]{:S(2)}) collective-permute-start(bf16[3,48,512]{2,1,0:T(8,128)(2,1)S(1)} %get-tuple-element.25), channel_id=1, source_target_pairs={{0,13},{2,15},{1,12},{3,14},{4,9},{6,11},{5,8},{7,10},{8,5},{10,7}... | collective-permute-start | bytes 442376 | tf_op jit(solution)/shard_map/ppermute | solution.py:198
  18.2 0.0 collective-permute-done.1.refs_1_
  18.2 0.4 collective-permute-start.6
  18.6 1.5 %collective-permute-done.2.refs_2_ = bf16[3,48,512]{2,1,0:T(8,128)(2,1)S(1)} collective-permute-done((bf16[3,48,512]{2,1,0:T(8,128)(2,1)S(1)}, bf16[3,48,512]{2,1,0:T(8,128)(2,1)S(1)}, u32[]{:S(2)}, u32[]{:S(2)}) %collective-permute-start.2) | collective-permute-done | bytes 147488 | tf_op jit(solution)/shard_map/ppermute | solution.py:198
  20.1 7.2 %collective-permute-done.3.refs_3_ = bf16[3,48,512]{2,1,0:T(8,128)(2,1)S(1)} collective-permute-done((bf16[3,48,512]{2,1,0:T(8,128)(2,1)S(1)}, bf16[3,48,512]{2,1,0:T(8,128)(2,1)S(1)}, u32[]{:S(2)}, u32[]{:S(2)}) %collective-permute-start.3) | collective-permute-done | bytes 147488 | tf_op jit(solution)/shard_map/ppermute | solution.py:198
  27.3 0.0 collective-permute-done.4.refs_4_
  27.3 0.0 collective-permute-done.5.refs_5_
  27.3 0.0 collective-permute-done.6.refs_6_
  27.3 0.9 %attend.1.own_refs_0_ = bf16[8,48,512]{2,1,0:T(8,128)(2,1)S(1)} custom-call(bf16[3,48,512]{2,1,0:T(8,128)(2,1)S(1)} %collective-permute-done.refs_0_, bf16[3,48,512]{2,1,0:T(8,128)(2,1)S(1)} %collective-permute-done.1.refs_1_, bf16[3,48,512]{2,1,0:T(8,128)(2,1)S(1)} %collective-permute-done.2.refs_2_, ...), custom_call_target="tpu_custom_call" | custom-call | tf_op jit(solution)/shard_map/attend/pallas_call | solution.py:225
  28.3 1.1 %collective-permute-start.7 = (bf16[8,48,512]{2,1,0:T(8,128)(2,1)S(1)}, bf16[8,48,512]{2,1,0:T(8,128)(2,1)S(1)}, u32[]{:S(2)}, u32[]{:S(2)}) collective-permute-start(bf16[8,48,512]{2,1,0:T(8,128)(2,1)S(1)} %attend.1.own_refs_0_), channel_id=1, source_target_pairs={{0,2},{2,0},{1,3},{3,1},{4,6},{6,4},{5,7},{7,5},{8,10},{10,8},{9,1... | collective-permute-start | bytes 1179656 | tf_op jit(solution)/shard_map/ppermute | solution.py:235
  29.4 0.8 %dynamic_slice.3 = f32[512]{0:T(512)S(1)} dynamic-slice(f32[4096]{0:T(1024)} %param.5, s32[]{:T(128)S(6)} %select_n.3), dynamic_slice_sizes={512} | dynamic-slice | bytes 4100 | tf_op jit(solution)/shard_map/dynamic_slice | solution.py:245
  30.2 0.0 copy-done.1
  30.2 0.0 copy-done.2
  30.2 0.9 %choose.1.chosen_ref = bf16[240,384]{1,0:T(8,128)(2,1)S(1)} custom-call(s32[4]{0:T(128)S(1)} %copy-done.2, s32[8,48]{1,0:T(8,128)S(1)} %copy-done.1), custom_call_target="tpu_custom_call" | custom-call | tf_op jit(solution)/shard_map/choose/pallas_call | solution.py:237
  31.1 0.0 collective-permute-done.7.other_refs_0_
  31.1 0.3 join.1
  31.4 2.6 %collective-permute-start.8 = (bf16[2,48,512]{2,1,0:T(8,128)(2,1)S(1)}, bf16[2,48,512]{2,1,0:T(8,128)(2,1)S(1)}, u32[]{:S(2)}, u32[]{:S(2)}) collective-permute-start(bf16[2,48,512]{2,1,0:T(8,128)(2,1)S(1)} %get-tuple-element.30), channel_id=1, source_target_pairs={{0,12},{2,15},{1,13},{3,14},{4,8},{6,11},{5,9},{7,10},{8,4},{10,7}... | collective-permute-start | bytes 294920 | tf_op jit(solution)/shard_map/ppermute | solution.py:198
  34.0 4.3 %collective-permute-start.9 = (bf16[2,48,512]{2,1,0:T(8,128)(2,1)S(1)}, bf16[2,48,512]{2,1,0:T(8,128)(2,1)S(1)}, u32[]{:S(2)}, u32[]{:S(2)}) collective-permute-start(bf16[2,48,512]{2,1,0:T(8,128)(2,1)S(1)} %get-tuple-element.31), channel_id=1, source_target_pairs={{0,5},{2,11},{1,4},{3,10},{4,1},{6,15},{5,0},{7,14},{8,13},{10,3},... | collective-permute-start | bytes 294920 | tf_op jit(solution)/shard_map/ppermute | solution.py:198
  38.2 1.5 %collective-permute-start.10 = (bf16[2,48,512]{2,1,0:T(8,128)(2,1)S(1)}, bf16[2,48,512]{2,1,0:T(8,128)(2,1)S(1)}, u32[]{:S(2)}, u32[]{:S(2)}) collective-permute-start(bf16[2,48,512]{2,1,0:T(8,128)(2,1)S(1)} %get-tuple-element.32), channel_id=1, source_target_pairs={{0,1},{2,6},{1,0},{3,7},{4,5},{6,2},{5,4},{7,3},{8,9},{10,14},{9,8... | collective-permute-start | bytes 294920 | tf_op jit(solution)/shard_map/ppermute | solution.py:198
  39.7 0.0 collective-permute-start.14
  39.7 0.0 collective-permute-done.8.in_ref.refs_0__0_
  39.8 1.7 %collective-permute-start.11 = (bf16[48,512]{1,0:T(8,128)(2,1)S(1)}, bf16[48,512]{1,0:T(8,128)(2,1)S(1)}, u32[]{:S(2)}, u32[]{:S(2)}) collective-permute-start(bf16[48,512]{1,0:T(8,128)(2,1)S(1)} %take.3), channel_id=1, source_target_pairs={{0,2},{2,0},{1,3},{3,1},{4,6},{6,4},{5,7},{7,5},{8,10},{10,8},{9,1... | collective-permute-start | bytes 147464 | tf_op jit(solution)/shard_map/ppermute | solution.py:266
  41.5 0.0 collective-permute-done.9.in_ref.refs_0__1_
  41.5 1.3 %collective-permute-start.12 = (bf16[48,512]{1,0:T(8,128)(2,1)S(1)}, bf16[48,512]{1,0:T(8,128)(2,1)S(1)}, u32[]{:S(2)}, u32[]{:S(2)}) collective-permute-start(bf16[48,512]{1,0:T(8,128)(2,1)S(1)} %take.4), channel_id=1, source_target_pairs={{0,2},{2,0},{1,3},{3,1},{4,6},{6,4},{5,7},{7,5},{8,10},{10,8},{9,1... | collective-permute-start | bytes 147464 | tf_op jit(solution)/shard_map/ppermute | solution.py:266
  42.7 0.9 %collective-permute-done.10.in_ref.refs_0__2_ = bf16[2,48,512]{2,1,0:T(8,128)(2,1)S(1)} collective-permute-done((bf16[2,48,512]{2,1,0:T(8,128)(2,1)S(1)}, bf16[2,48,512]{2,1,0:T(8,128)(2,1)S(1)}, u32[]{:S(2)}, u32[]{:S(2)}) %collective-permute-start.10) | collective-permute-done | bytes 98336 | tf_op jit(solution)/shard_map/ppermute | solution.py:198
  43.7 0.0 collective-permute-start.13
  43.7 1.2 %collective-permute-done.14.refs_2__0_ = bf16[48,512]{1,0:T(8,128)(2,1)S(1)} collective-permute-done((bf16[48,512]{1,0:T(8,128)(2,1)S(1)}, bf16[48,512]{1,0:T(8,128)(2,1)S(1)}, u32[]{:S(2)}, u32[]{:S(2)}) %collective-permute-start.14) | collective-permute-done | bytes 49184 | tf_op jit(solution)/shard_map/ppermute | solution.py:198
  44.9 0.0 collective-permute-done.11.refs_1__0_
  44.9 0.0 collective-permute-done.12.refs_1__1_
  44.9 0.0 collective-permute-done.13.refs_1__2_
  44.9 0.8 %merge.1 = bf16[48,4096]{1,0:T(8,128)(2,1)} custom-call(bf16[2,48,512]{2,1,0:T(8,128)(2,1)S(1)} %collective-permute-done.8.in_ref.refs_0__0_, bf16[2,48,512]{2,1,0:T(8,128)(2,1)S(1)} %collective-permute-done.9.in_ref.refs_0__1_, bf16[2,48,512]{2,1,0:T(8,128)(2,1)S(1)} %collective-permute-done.10.in_ref.refs_0__2_, ...), custom_call_target="tpu_custom_call" | custom-call | tf_op jit(solution)/shard_map/merge/pallas_call | solution.py:269
  (3 shorter events, 0.0 us)
Async XLA Ops:
  0.0 1.3 %copy-start = (bf16[1,48,3,4096]{3,1,2,0:T(8,128)(2,1)S(1)}, bf16[1,48,3,4096]{3,1,2,0:T(8,128)(2,1)}, u32[]{:S(2)}) copy-start(bf16[1,48,3,4096]{3,1,2,0:T(8,128)(2,1)} %param.4) | copy-start | bytes 3538948
  1.3 28.9 %copy-start.1 = (s32[8,48]{1,0:T(8,128)S(1)}, s32[8,48]{1,0:T(8,128)}, u32[]{:S(2)}) copy-start(s32[8,48]{1,0:T(8,128)} %perm_ref.1) | copy-start | bytes 4612
  1.3 28.9 %copy-start.2 = (s32[4]{0:T(128)S(1)}, s32[4]{0:T(128)}, u32[]{:S(2)}) copy-start(s32[4]{0:T(128)} %map_ref) | copy-start | bytes 52
  1.5 12.8 %collective-permute-start = (bf16[3,48,512]{2,1,0:T(8,128)(2,1)S(1)}, bf16[3,48,512]{2,1,0:T(8,128)(2,1)S(1)}, u32[]{:S(2)}, u32[]{:S(2)}) collective-permute-start(bf16[3,48,512]{2,1,0:T(8,128)(2,1)S(1)} %get-tuple-element.20), channel_id=1, source_target_pairs={{0,8},{2,14},{1,9},{3,15},{4,12},{6,10},{5,13},{7,11},{8,0},{10,6}... | collective-permute-start | bytes 442376 | tf_op jit(solution)/shard_map/ppermute | solution.py:198
  5.6 12.5 %collective-permute-start.1 = (bf16[3,48,512]{2,1,0:T(8,128)(2,1)S(1)}, bf16[3,48,512]{2,1,0:T(8,128)(2,1)S(1)}, u32[]{:S(2)}, u32[]{:S(2)}) collective-permute-start(bf16[3,48,512]{2,1,0:T(8,128)(2,1)S(1)} %get-tuple-element.21), channel_id=1, source_target_pairs={{0,5},{2,3},{1,4},{3,2},{4,1},{6,7},{5,0},{7,6},{8,13},{10,11},{9,... | collective-permute-start | bytes 442376 | tf_op jit(solution)/shard_map/ppermute | solution.py:198
  8.1 12.0 %collective-permute-start.2 = (bf16[3,48,512]{2,1,0:T(8,128)(2,1)S(1)}, bf16[3,48,512]{2,1,0:T(8,128)(2,1)S(1)}, u32[]{:S(2)}, u32[]{:S(2)}) collective-permute-start(bf16[3,48,512]{2,1,0:T(8,128)(2,1)S(1)} %get-tuple-element.22), channel_id=1, source_target_pairs={{0,4},{2,6},{1,5},{3,7},{4,0},{6,2},{5,1},{7,3},{8,12},{10,14},{9,... | collective-permute-start | bytes 442376 | tf_op jit(solution)/shard_map/ppermute | solution.py:198
  8.6 18.7 %collective-permute-start.3 = (bf16[3,48,512]{2,1,0:T(8,128)(2,1)S(1)}, bf16[3,48,512]{2,1,0:T(8,128)(2,1)S(1)}, u32[]{:S(2)}, u32[]{:S(2)}) collective-permute-start(bf16[3,48,512]{2,1,0:T(8,128)(2,1)S(1)} %get-tuple-element.23), channel_id=1, source_target_pairs={{0,9},{2,10},{1,8},{3,11},{4,13},{6,14},{5,12},{7,15},{8,1},{10,2}... | collective-permute-start | bytes 442376 | tf_op jit(solution)/shard_map/ppermute | solution.py:198
  8.6 18.7 %collective-permute-start.4 = (bf16[3,48,512]{2,1,0:T(8,128)(2,1)S(1)}, bf16[3,48,512]{2,1,0:T(8,128)(2,1)S(1)}, u32[]{:S(2)}, u32[]{:S(2)}) collective-permute-start(bf16[3,48,512]{2,1,0:T(8,128)(2,1)S(1)} %get-tuple-element.24), channel_id=1, source_target_pairs={{0,12},{2,11},{1,13},{3,10},{4,8},{6,15},{5,9},{7,14},{8,4},{10,3}... | collective-permute-start | bytes 442376 | tf_op jit(solution)/shard_map/ppermute | solution.py:198
  14.4 13.0 %collective-permute-start.5 = (bf16[3,48,512]{2,1,0:T(8,128)(2,1)S(1)}, bf16[3,48,512]{2,1,0:T(8,128)(2,1)S(1)}, u32[]{:S(2)}, u32[]{:S(2)}) collective-permute-start(bf16[3,48,512]{2,1,0:T(8,128)(2,1)S(1)} %get-tuple-element.25), channel_id=1, source_target_pairs={{0,13},{2,15},{1,12},{3,14},{4,9},{6,11},{5,8},{7,10},{8,5},{10,7}... | collective-permute-start | bytes 442376 | tf_op jit(solution)/shard_map/ppermute | solution.py:198
  18.2 9.2 %collective-permute-start.6 = (bf16[3,48,512]{2,1,0:T(8,128)(2,1)S(1)}, bf16[3,48,512]{2,1,0:T(8,128)(2,1)S(1)}, u32[]{:S(2)}, u32[]{:S(2)}) collective-permute-start(bf16[3,48,512]{2,1,0:T(8,128)(2,1)S(1)} %get-tuple-element.26), channel_id=1, source_target_pairs={{0,1},{2,7},{1,0},{3,6},{4,5},{6,3},{5,4},{7,2},{8,9},{10,15},{9,8... | collective-permute-start | bytes 442376 | tf_op jit(solution)/shard_map/ppermute | solution.py:198
  28.3 2.8 %collective-permute-start.7 = (bf16[8,48,512]{2,1,0:T(8,128)(2,1)S(1)}, bf16[8,48,512]{2,1,0:T(8,128)(2,1)S(1)}, u32[]{:S(2)}, u32[]{:S(2)}) collective-permute-start(bf16[8,48,512]{2,1,0:T(8,128)(2,1)S(1)} %attend.1.own_refs_0_), channel_id=1, source_target_pairs={{0,2},{2,0},{1,3},{3,1},{4,6},{6,4},{5,7},{7,5},{8,10},{10,8},{9,1... | collective-permute-start | bytes 1179656 | tf_op jit(solution)/shard_map/ppermute | solution.py:235
  31.4 8.4 %collective-permute-start.8 = (bf16[2,48,512]{2,1,0:T(8,128)(2,1)S(1)}, bf16[2,48,512]{2,1,0:T(8,128)(2,1)S(1)}, u32[]{:S(2)}, u32[]{:S(2)}) collective-permute-start(bf16[2,48,512]{2,1,0:T(8,128)(2,1)S(1)} %get-tuple-element.30), channel_id=1, source_target_pairs={{0,12},{2,15},{1,13},{3,14},{4,8},{6,11},{5,9},{7,10},{8,4},{10,7}... | collective-permute-start | bytes 294920 | tf_op jit(solution)/shard_map/ppermute | solution.py:198
  34.0 7.5 %collective-permute-start.9 = (bf16[2,48,512]{2,1,0:T(8,128)(2,1)S(1)}, bf16[2,48,512]{2,1,0:T(8,128)(2,1)S(1)}, u32[]{:S(2)}, u32[]{:S(2)}) collective-permute-start(bf16[2,48,512]{2,1,0:T(8,128)(2,1)S(1)} %get-tuple-element.31), channel_id=1, source_target_pairs={{0,5},{2,11},{1,4},{3,10},{4,1},{6,15},{5,0},{7,14},{8,13},{10,3},... | collective-permute-start | bytes 294920 | tf_op jit(solution)/shard_map/ppermute | solution.py:198
  38.2 5.4 %collective-permute-start.10 = (bf16[2,48,512]{2,1,0:T(8,128)(2,1)S(1)}, bf16[2,48,512]{2,1,0:T(8,128)(2,1)S(1)}, u32[]{:S(2)}, u32[]{:S(2)}) collective-permute-start(bf16[2,48,512]{2,1,0:T(8,128)(2,1)S(1)} %get-tuple-element.32), channel_id=1, source_target_pairs={{0,1},{2,6},{1,0},{3,7},{4,5},{6,2},{5,4},{7,3},{8,9},{10,14},{9,8... | collective-permute-start | bytes 294920 | tf_op jit(solution)/shard_map/ppermute | solution.py:198
  39.7 5.1 %collective-permute-start.14 = (bf16[48,512]{1,0:T(8,128)(2,1)S(1)}, bf16[48,512]{1,0:T(8,128)(2,1)S(1)}, u32[]{:S(2)}, u32[]{:S(2)}) collective-permute-start(bf16[48,512]{1,0:T(8,128)(2,1)S(1)} %get-tuple-element.33), channel_id=1, source_target_pairs={{0,8},{2,10},{1,9},{3,11},{4,12},{6,14},{5,13},{7,15},{8,0},{10,2}... | collective-permute-start | bytes 147464 | tf_op jit(solution)/shard_map/ppermute | solution.py:198
  39.8 5.1 %collective-permute-start.11 = (bf16[48,512]{1,0:T(8,128)(2,1)S(1)}, bf16[48,512]{1,0:T(8,128)(2,1)S(1)}, u32[]{:S(2)}, u32[]{:S(2)}) collective-permute-start(bf16[48,512]{1,0:T(8,128)(2,1)S(1)} %take.3), channel_id=1, source_target_pairs={{0,2},{2,0},{1,3},{3,1},{4,6},{6,4},{5,7},{7,5},{8,10},{10,8},{9,1... | collective-permute-start | bytes 147464 | tf_op jit(solution)/shard_map/ppermute | solution.py:266
  41.5 3.4 %collective-permute-start.12 = (bf16[48,512]{1,0:T(8,128)(2,1)S(1)}, bf16[48,512]{1,0:T(8,128)(2,1)S(1)}, u32[]{:S(2)}, u32[]{:S(2)}) collective-permute-start(bf16[48,512]{1,0:T(8,128)(2,1)S(1)} %take.4), channel_id=1, source_target_pairs={{0,2},{2,0},{1,3},{3,1},{4,6},{6,4},{5,7},{7,5},{8,10},{10,8},{9,1... | collective-permute-start | bytes 147464 | tf_op jit(solution)/shard_map/ppermute | solution.py:266
  43.7 1.2 %collective-permute-start.13 = (bf16[48,512]{1,0:T(8,128)(2,1)S(1)}, bf16[48,512]{1,0:T(8,128)(2,1)S(1)}, u32[]{:S(2)}, u32[]{:S(2)}) collective-permute-start(bf16[48,512]{1,0:T(8,128)(2,1)S(1)} %take.5), channel_id=1, source_target_pairs={{0,2},{2,0},{1,3},{3,1},{4,6},{6,4},{5,7},{7,5},{8,10},{10,8},{9,1... | collective-permute-start | bytes 147464 | tf_op jit(solution)/shard_map/ppermute | solution.py:266

commit v6 on v5

--- a/solution.py
+++ b/solution.py
@@ -13,7 +13,7 @@
 
 key_block = 512
 
-ORDER_IN = ((4, 3, 2, 5, 6, 7, 1), (6, 1, 2, 4, 5, 7, 3))
+ORDER_IN = ((4, 3, 2, 5, 7, 6, 1), (6, 1, 2, 4, 5, 7, 3))
 ORDER_BACK = ((6, 3, 1), (7, 5, 2))
 STRAIGHT = (4,)
 STRAIGHT_FIRST = False

time: 45.9 us -> 45.5 us (level)
  starting transfers between devices: 27.7 us -> 27.2 us
    ppermute x3, starting transfers between devices: 2.99 us -> 2.37 us  [by_heads(): passed.append(lax.ppermute(taken, 'branch', both))]
  transfers between devices with their start and end apart: 15 -> 15, of which waited for: 5 -> 7; matrix products, arithmetic and copies ran while one was open for 2% -> 2% of each run, Pallas kernels for 2% -> 2%
where the time goes in v6:
time: 45.5 us; the launch traced here: 45.3 us
  starting transfers between devices  27.2 us (60%)
  waiting for transfers between devices  12.9 us (28%)
  Pallas kernels  3.16 us (7%)
  local copies, waits for them, and re-layouts  2.04 us (4%)
    ppermute x11, starting transfers between devices, exchange_by_core(): lax.ppermute(piece, ('seq', 'branch', 'tp'), pairs)  23.7 us
    ppermute x11, waiting for transfers between devices, exchange_by_core(): lax.ppermute(piece, ('seq', 'branch', 'tp'), pairs)  12.6 us
    ppermute x3, starting transfers between devices, by_heads(): passed.append(lax.ppermute(taken, 'branch', both))  2.37 us
    unnamed x6, local copies, waits for them, and re-layouts  1.28 us
    ppermute x1, starting transfers between devices, by_heads(): other = [lax.ppermute(part, 'branch', both) for part in attended]  1.15 us
    pallas_call x1, Pallas kernels, by_heads(): pl.pallas_call(functools.partial(attend_kernel, count, rows, start, stop)...  0.94 us
  transfers between devices with their start and end apart: 15, of which 7 were waited for; matrix products, arithmetic and copies ran while one was open for 2% of the time, Pallas kernels for 2%

profile of v6, /device:TPU:0, one launch (start us, length us, event | category | flops | bytes accessed | tf_op | source)
XLA Modules:
  0.0 45.3 jit_solution(2193224122445481706)
XLA Ops:
  0.0 0.0 copy-start
  0.0 1.3 %copy-done = bf16[1,48,3,4096]{3,1,2,0:T(8,128)(2,1)S(1)} copy-done((bf16[1,48,3,4096]{3,1,2,0:T(8,128)(2,1)S(1)}, bf16[1,48,3,4096]{3,1,2,0:T(8,128)(2,1)}, u32[]{:S(2)}) %copy-start) | copy-done | bytes 1179672
  1.3 0.0 copy-start.1
  1.3 0.0 copy-start.2
  1.3 0.3 split.1
  1.5 4.1 %collective-permute-start = (bf16[3,48,512]{2,1,0:T(8,128)(2,1)S(1)}, bf16[3,48,512]{2,1,0:T(8,128)(2,1)S(1)}, u32[]{:S(2)}, u32[]{:S(2)}) collective-permute-start(bf16[3,48,512]{2,1,0:T(8,128)(2,1)S(1)} %get-tuple-element.20), channel_id=1, source_target_pairs={{0,8},{2,14},{1,9},{3,15},{4,12},{6,10},{5,13},{7,11},{8,0},{10,6}... | collective-permute-start | bytes 442376 | tf_op jit(solution)/shard_map/ppermute | solution.py:198
  5.6 2.5 %collective-permute-start.1 = (bf16[3,48,512]{2,1,0:T(8,128)(2,1)S(1)}, bf16[3,48,512]{2,1,0:T(8,128)(2,1)S(1)}, u32[]{:S(2)}, u32[]{:S(2)}) collective-permute-start(bf16[3,48,512]{2,1,0:T(8,128)(2,1)S(1)} %get-tuple-element.21), channel_id=1, source_target_pairs={{0,5},{2,3},{1,4},{3,2},{4,1},{6,7},{5,0},{7,6},{8,13},{10,11},{9,... | collective-permute-start | bytes 442376 | tf_op jit(solution)/shard_map/ppermute | solution.py:198
  8.1 0.4 collective-permute-start.2
  8.6 0.1 collective-permute-start.3
  8.6 4.8 %collective-permute-start.4 = (bf16[3,48,512]{2,1,0:T(8,128)(2,1)S(1)}, bf16[3,48,512]{2,1,0:T(8,128)(2,1)S(1)}, u32[]{:S(2)}, u32[]{:S(2)}) collective-permute-start(bf16[3,48,512]{2,1,0:T(8,128)(2,1)S(1)} %get-tuple-element.24), channel_id=1, source_target_pairs={{0,13},{2,11},{1,12},{3,10},{4,9},{6,15},{5,8},{7,14},{8,5},{10,3}... | collective-permute-start | bytes 442376 | tf_op jit(solution)/shard_map/ppermute | solution.py:198
  13.4 0.9 %collective-permute-done.refs_0_ = bf16[3,48,512]{2,1,0:T(8,128)(2,1)S(1)} collective-permute-done((bf16[3,48,512]{2,1,0:T(8,128)(2,1)S(1)}, bf16[3,48,512]{2,1,0:T(8,128)(2,1)S(1)}, u32[]{:S(2)}, u32[]{:S(2)}) %collective-permute-start) | collective-permute-done | bytes 147488 | tf_op jit(solution)/shard_map/ppermute | solution.py:198
  14.4 2.7 %collective-permute-start.5 = (bf16[3,48,512]{2,1,0:T(8,128)(2,1)S(1)}, bf16[3,48,512]{2,1,0:T(8,128)(2,1)S(1)}, u32[]{:S(2)}, u32[]{:S(2)}) collective-permute-start(bf16[3,48,512]{2,1,0:T(8,128)(2,1)S(1)} %get-tuple-element.25), channel_id=1, source_target_pairs={{0,12},{2,15},{1,13},{3,14},{4,8},{6,11},{5,9},{7,10},{8,4},{10,7}... | collective-permute-start | bytes 442376 | tf_op jit(solution)/shard_map/ppermute | solution.py:198
  17.1 0.0 collective-permute-done.1.refs_1_
  17.1 1.6 %collective-permute-start.6 = (bf16[3,48,512]{2,1,0:T(8,128)(2,1)S(1)}, bf16[3,48,512]{2,1,0:T(8,128)(2,1)S(1)}, u32[]{:S(2)}, u32[]{:S(2)}) collective-permute-start(bf16[3,48,512]{2,1,0:T(8,128)(2,1)S(1)} %get-tuple-element.26), channel_id=1, source_target_pairs={{0,1},{2,7},{1,0},{3,6},{4,5},{6,3},{5,4},{7,2},{8,9},{10,15},{9,8... | collective-permute-start | bytes 442376 | tf_op jit(solution)/shard_map/ppermute | solution.py:198
  18.7 1.4 %collective-permute-done.2.refs_2_ = bf16[3,48,512]{2,1,0:T(8,128)(2,1)S(1)} collective-permute-done((bf16[3,48,512]{2,1,0:T(8,128)(2,1)S(1)}, bf16[3,48,512]{2,1,0:T(8,128)(2,1)S(1)}, u32[]{:S(2)}, u32[]{:S(2)}) %collective-permute-start.2) | collective-permute-done | bytes 147488 | tf_op jit(solution)/shard_map/ppermute | solution.py:198
  20.1 7.2 %collective-permute-done.3.refs_3_ = bf16[3,48,512]{2,1,0:T(8,128)(2,1)S(1)} collective-permute-done((bf16[3,48,512]{2,1,0:T(8,128)(2,1)S(1)}, bf16[3,48,512]{2,1,0:T(8,128)(2,1)S(1)}, u32[]{:S(2)}, u32[]{:S(2)}) %collective-permute-start.3) | collective-permute-done | bytes 147488 | tf_op jit(solution)/shard_map/ppermute | solution.py:198
  27.3 0.0 collective-permute-done.4.refs_4_
  27.3 0.0 collective-permute-done.5.refs_5_
  27.3 0.0 collective-permute-done.6.refs_6_
  27.3 0.9 %attend.1.own_refs_0_ = bf16[8,48,512]{2,1,0:T(8,128)(2,1)S(1)} custom-call(bf16[3,48,512]{2,1,0:T(8,128)(2,1)S(1)} %collective-permute-done.refs_0_, bf16[3,48,512]{2,1,0:T(8,128)(2,1)S(1)} %collective-permute-done.1.refs_1_, bf16[3,48,512]{2,1,0:T(8,128)(2,1)S(1)} %collective-permute-done.2.refs_2_, ...), custom_call_target="tpu_custom_call" | custom-call | tf_op jit(solution)/shard_map/attend/pallas_call | solution.py:225
  28.3 1.1 %collective-permute-start.7 = (bf16[8,48,512]{2,1,0:T(8,128)(2,1)S(1)}, bf16[8,48,512]{2,1,0:T(8,128)(2,1)S(1)}, u32[]{:S(2)}, u32[]{:S(2)}) collective-permute-start(bf16[8,48,512]{2,1,0:T(8,128)(2,1)S(1)} %attend.1.own_refs_0_), channel_id=1, source_target_pairs={{0,2},{2,0},{1,3},{3,1},{4,6},{6,4},{5,7},{7,5},{8,10},{10,8},{9,1... | collective-permute-start | bytes 1179656 | tf_op jit(solution)/shard_map/ppermute | solution.py:235
  29.4 0.8 %dynamic_slice.3 = f32[512]{0:T(512)S(1)} dynamic-slice(f32[4096]{0:T(1024)} %param.5, s32[]{:T(128)S(6)} %select_n.3), dynamic_slice_sizes={512} | dynamic-slice | bytes 4100 | tf_op jit(solution)/shard_map/dynamic_slice | solution.py:245
  30.2 0.0 copy-done.1
  30.2 0.0 copy-done.2
  30.2 0.9 %choose.1.chosen_ref = bf16[240,384]{1,0:T(8,128)(2,1)S(1)} custom-call(s32[4]{0:T(128)S(1)} %copy-done.2, s32[8,48]{1,0:T(8,128)S(1)} %copy-done.1), custom_call_target="tpu_custom_call" | custom-call | tf_op jit(solution)/shard_map/choose/pallas_call | solution.py:237
  31.1 0.0 collective-permute-done.7.other_refs_0_
  31.1 0.3 join.1
  31.4 2.3 %collective-permute-start.8 = (bf16[2,48,512]{2,1,0:T(8,128)(2,1)S(1)}, bf16[2,48,512]{2,1,0:T(8,128)(2,1)S(1)}, u32[]{:S(2)}, u32[]{:S(2)}) collective-permute-start(bf16[2,48,512]{2,1,0:T(8,128)(2,1)S(1)} %get-tuple-element.30), channel_id=1, source_target_pairs={{0,12},{2,15},{1,13},{3,14},{4,8},{6,11},{5,9},{7,10},{8,4},{10,7}... | collective-permute-start | bytes 294920 | tf_op jit(solution)/shard_map/ppermute | solution.py:198
  33.6 4.6 %collective-permute-start.9 = (bf16[2,48,512]{2,1,0:T(8,128)(2,1)S(1)}, bf16[2,48,512]{2,1,0:T(8,128)(2,1)S(1)}, u32[]{:S(2)}, u32[]{:S(2)}) collective-permute-start(bf16[2,48,512]{2,1,0:T(8,128)(2,1)S(1)} %get-tuple-element.31), channel_id=1, source_target_pairs={{0,5},{2,11},{1,4},{3,10},{4,1},{6,15},{5,0},{7,14},{8,13},{10,3},... | collective-permute-start | bytes 294920 | tf_op jit(solution)/shard_map/ppermute | solution.py:198
  38.3 0.5 %collective-permute-start.10 = (bf16[2,48,512]{2,1,0:T(8,128)(2,1)S(1)}, bf16[2,48,512]{2,1,0:T(8,128)(2,1)S(1)}, u32[]{:S(2)}, u32[]{:S(2)}) collective-permute-start(bf16[2,48,512]{2,1,0:T(8,128)(2,1)S(1)} %get-tuple-element.32), channel_id=1, source_target_pairs={{0,1},{2,6},{1,0},{3,7},{4,5},{6,2},{5,4},{7,3},{8,9},{10,14},{9,8... | collective-permute-start | bytes 294920 | tf_op jit(solution)/shard_map/ppermute | solution.py:198
  38.8 0.0 collective-permute-start.14
  38.8 0.0 collective-permute-done.8.in_ref.refs_0__0_
  38.8 1.7 %collective-permute-start.11 = (bf16[48,512]{1,0:T(8,128)(2,1)S(1)}, bf16[48,512]{1,0:T(8,128)(2,1)S(1)}, u32[]{:S(2)}, u32[]{:S(2)}) collective-permute-start(bf16[48,512]{1,0:T(8,128)(2,1)S(1)} %take.3), channel_id=1, source_target_pairs={{0,2},{2,0},{1,3},{3,1},{4,6},{6,4},{5,7},{7,5},{8,10},{10,8},{9,1... | collective-permute-start | bytes 147464 | tf_op jit(solution)/shard_map/ppermute | solution.py:266
  40.5 0.9 %collective-permute-done.9.in_ref.refs_0__1_ = bf16[2,48,512]{2,1,0:T(8,128)(2,1)S(1)} collective-permute-done((bf16[2,48,512]{2,1,0:T(8,128)(2,1)S(1)}, bf16[2,48,512]{2,1,0:T(8,128)(2,1)S(1)}, u32[]{:S(2)}, u32[]{:S(2)}) %collective-permute-start.9) | collective-permute-done | bytes 98336 | tf_op jit(solution)/shard_map/ppermute | solution.py:198
  41.5 0.7 %collective-permute-start.12 = (bf16[48,512]{1,0:T(8,128)(2,1)S(1)}, bf16[48,512]{1,0:T(8,128)(2,1)S(1)}, u32[]{:S(2)}, u32[]{:S(2)}) collective-permute-start(bf16[48,512]{1,0:T(8,128)(2,1)S(1)} %take.4), channel_id=1, source_target_pairs={{0,2},{2,0},{1,3},{3,1},{4,6},{6,4},{5,7},{7,5},{8,10},{10,8},{9,1... | collective-permute-start | bytes 147464 | tf_op jit(solution)/shard_map/ppermute | solution.py:266
  42.1 1.2 %collective-permute-done.10.in_ref.refs_0__2_ = bf16[2,48,512]{2,1,0:T(8,128)(2,1)S(1)} collective-permute-done((bf16[2,48,512]{2,1,0:T(8,128)(2,1)S(1)}, bf16[2,48,512]{2,1,0:T(8,128)(2,1)S(1)}, u32[]{:S(2)}, u32[]{:S(2)}) %collective-permute-start.10) | collective-permute-done | bytes 98336 | tf_op jit(solution)/shard_map/ppermute | solution.py:198
  43.3 0.0 collective-permute-start.13
  43.3 1.0 %collective-permute-done.14.refs_2__0_ = bf16[48,512]{1,0:T(8,128)(2,1)S(1)} collective-permute-done((bf16[48,512]{1,0:T(8,128)(2,1)S(1)}, bf16[48,512]{1,0:T(8,128)(2,1)S(1)}, u32[]{:S(2)}, u32[]{:S(2)}) %collective-permute-start.14) | collective-permute-done | bytes 49184 | tf_op jit(solution)/shard_map/ppermute | solution.py:198
  44.3 0.0 collective-permute-done.11.refs_1__0_
  44.3 0.0 collective-permute-done.12.refs_1__1_
  44.3 0.2 collective-permute-done.13.refs_1__2_
  44.5 0.8 %merge.1 = bf16[48,4096]{1,0:T(8,128)(2,1)} custom-call(bf16[2,48,512]{2,1,0:T(8,128)(2,1)S(1)} %collective-permute-done.8.in_ref.refs_0__0_, bf16[2,48,512]{2,1,0:T(8,128)(2,1)S(1)} %collective-permute-done.9.in_ref.refs_0__1_, bf16[2,48,512]{2,1,0:T(8,128)(2,1)S(1)} %collective-permute-done.10.in_ref.refs_0__2_, ...), custom_call_target="tpu_custom_call" | custom-call | tf_op jit(solution)/shard_map/merge/pallas_call | solution.py:269
  (3 shorter events, 0.0 us)
Async XLA Ops:
  0.0 1.3 %copy-start = (bf16[1,48,3,4096]{3,1,2,0:T(8,128)(2,1)S(1)}, bf16[1,48,3,4096]{3,1,2,0:T(8,128)(2,1)}, u32[]{:S(2)}) copy-start(bf16[1,48,3,4096]{3,1,2,0:T(8,128)(2,1)} %param.4) | copy-start | bytes 3538948
  1.3 28.9 %copy-start.1 = (s32[8,48]{1,0:T(8,128)S(1)}, s32[8,48]{1,0:T(8,128)}, u32[]{:S(2)}) copy-start(s32[8,48]{1,0:T(8,128)} %perm_ref.1) | copy-start | bytes 4612
  1.3 28.9 %copy-start.2 = (s32[4]{0:T(128)S(1)}, s32[4]{0:T(128)}, u32[]{:S(2)}) copy-start(s32[4]{0:T(128)} %map_ref) | copy-start | bytes 52
  1.5 12.8 %collective-permute-start = (bf16[3,48,512]{2,1,0:T(8,128)(2,1)S(1)}, bf16[3,48,512]{2,1,0:T(8,128)(2,1)S(1)}, u32[]{:S(2)}, u32[]{:S(2)}) collective-permute-start(bf16[3,48,512]{2,1,0:T(8,128)(2,1)S(1)} %get-tuple-element.20), channel_id=1, source_target_pairs={{0,8},{2,14},{1,9},{3,15},{4,12},{6,10},{5,13},{7,11},{8,0},{10,6}... | collective-permute-start | bytes 442376 | tf_op jit(solution)/shard_map/ppermute | solution.py:198
  5.6 11.5 %collective-permute-start.1 = (bf16[3,48,512]{2,1,0:T(8,128)(2,1)S(1)}, bf16[3,48,512]{2,1,0:T(8,128)(2,1)S(1)}, u32[]{:S(2)}, u32[]{:S(2)}) collective-permute-start(bf16[3,48,512]{2,1,0:T(8,128)(2,1)S(1)} %get-tuple-element.21), channel_id=1, source_target_pairs={{0,5},{2,3},{1,4},{3,2},{4,1},{6,7},{5,0},{7,6},{8,13},{10,11},{9,... | collective-permute-start | bytes 442376 | tf_op jit(solution)/shard_map/ppermute | solution.py:198
  8.1 12.0 %collective-permute-start.2 = (bf16[3,48,512]{2,1,0:T(8,128)(2,1)S(1)}, bf16[3,48,512]{2,1,0:T(8,128)(2,1)S(1)}, u32[]{:S(2)}, u32[]{:S(2)}) collective-permute-start(bf16[3,48,512]{2,1,0:T(8,128)(2,1)S(1)} %get-tuple-element.22), channel_id=1, source_target_pairs={{0,4},{2,6},{1,5},{3,7},{4,0},{6,2},{5,1},{7,3},{8,12},{10,14},{9,... | collective-permute-start | bytes 442376 | tf_op jit(solution)/shard_map/ppermute | solution.py:198
  8.6 18.7 %collective-permute-start.3 = (bf16[3,48,512]{2,1,0:T(8,128)(2,1)S(1)}, bf16[3,48,512]{2,1,0:T(8,128)(2,1)S(1)}, u32[]{:S(2)}, u32[]{:S(2)}) collective-permute-start(bf16[3,48,512]{2,1,0:T(8,128)(2,1)S(1)} %get-tuple-element.23), channel_id=1, source_target_pairs={{0,9},{2,10},{1,8},{3,11},{4,13},{6,14},{5,12},{7,15},{8,1},{10,2}... | collective-permute-start | bytes 442376 | tf_op jit(solution)/shard_map/ppermute | solution.py:198
  8.6 18.7 %collective-permute-start.4 = (bf16[3,48,512]{2,1,0:T(8,128)(2,1)S(1)}, bf16[3,48,512]{2,1,0:T(8,128)(2,1)S(1)}, u32[]{:S(2)}, u32[]{:S(2)}) collective-permute-start(bf16[3,48,512]{2,1,0:T(8,128)(2,1)S(1)} %get-tuple-element.24), channel_id=1, source_target_pairs={{0,13},{2,11},{1,12},{3,10},{4,9},{6,15},{5,8},{7,14},{8,5},{10,3}... | collective-permute-start | bytes 442376 | tf_op jit(solution)/shard_map/ppermute | solution.py:198
  14.4 13.0 %collective-permute-start.5 = (bf16[3,48,512]{2,1,0:T(8,128)(2,1)S(1)}, bf16[3,48,512]{2,1,0:T(8,128)(2,1)S(1)}, u32[]{:S(2)}, u32[]{:S(2)}) collective-permute-start(bf16[3,48,512]{2,1,0:T(8,128)(2,1)S(1)} %get-tuple-element.25), channel_id=1, source_target_pairs={{0,12},{2,15},{1,13},{3,14},{4,8},{6,11},{5,9},{7,10},{8,4},{10,7}... | collective-permute-start | bytes 442376 | tf_op jit(solution)/shard_map/ppermute | solution.py:198
  17.1 10.2 %collective-permute-start.6 = (bf16[3,48,512]{2,1,0:T(8,128)(2,1)S(1)}, bf16[3,48,512]{2,1,0:T(8,128)(2,1)S(1)}, u32[]{:S(2)}, u32[]{:S(2)}) collective-permute-start(bf16[3,48,512]{2,1,0:T(8,128)(2,1)S(1)} %get-tuple-element.26), channel_id=1, source_target_pairs={{0,1},{2,7},{1,0},{3,6},{4,5},{6,3},{5,4},{7,2},{8,9},{10,15},{9,8... | collective-permute-start | bytes 442376 | tf_op jit(solution)/shard_map/ppermute | solution.py:198
  28.3 2.8 %collective-permute-start.7 = (bf16[8,48,512]{2,1,0:T(8,128)(2,1)S(1)}, bf16[8,48,512]{2,1,0:T(8,128)(2,1)S(1)}, u32[]{:S(2)}, u32[]{:S(2)}) collective-permute-start(bf16[8,48,512]{2,1,0:T(8,128)(2,1)S(1)} %attend.1.own_refs_0_), channel_id=1, source_target_pairs={{0,2},{2,0},{1,3},{3,1},{4,6},{6,4},{5,7},{7,5},{8,10},{10,8},{9,1... | collective-permute-start | bytes 1179656 | tf_op jit(solution)/shard_map/ppermute | solution.py:235
  31.4 7.4 %collective-permute-start.8 = (bf16[2,48,512]{2,1,0:T(8,128)(2,1)S(1)}, bf16[2,48,512]{2,1,0:T(8,128)(2,1)S(1)}, u32[]{:S(2)}, u32[]{:S(2)}) collective-permute-start(bf16[2,48,512]{2,1,0:T(8,128)(2,1)S(1)} %get-tuple-element.30), channel_id=1, source_target_pairs={{0,12},{2,15},{1,13},{3,14},{4,8},{6,11},{5,9},{7,10},{8,4},{10,7}... | collective-permute-start | bytes 294920 | tf_op jit(solution)/shard_map/ppermute | solution.py:198
  33.6 7.8 %collective-permute-start.9 = (bf16[2,48,512]{2,1,0:T(8,128)(2,1)S(1)}, bf16[2,48,512]{2,1,0:T(8,128)(2,1)S(1)}, u32[]{:S(2)}, u32[]{:S(2)}) collective-permute-start(bf16[2,48,512]{2,1,0:T(8,128)(2,1)S(1)} %get-tuple-element.31), channel_id=1, source_target_pairs={{0,5},{2,11},{1,4},{3,10},{4,1},{6,15},{5,0},{7,14},{8,13},{10,3},... | collective-permute-start | bytes 294920 | tf_op jit(solution)/shard_map/ppermute | solution.py:198
  38.3 5.0 %collective-permute-start.10 = (bf16[2,48,512]{2,1,0:T(8,128)(2,1)S(1)}, bf16[2,48,512]{2,1,0:T(8,128)(2,1)S(1)}, u32[]{:S(2)}, u32[]{:S(2)}) collective-permute-start(bf16[2,48,512]{2,1,0:T(8,128)(2,1)S(1)} %get-tuple-element.32), channel_id=1, source_target_pairs={{0,1},{2,6},{1,0},{3,7},{4,5},{6,2},{5,4},{7,3},{8,9},{10,14},{9,8... | collective-permute-start | bytes 294920 | tf_op jit(solution)/shard_map/ppermute | solution.py:198
  38.8 5.5 %collective-permute-start.14 = (bf16[48,512]{1,0:T(8,128)(2,1)S(1)}, bf16[48,512]{1,0:T(8,128)(2,1)S(1)}, u32[]{:S(2)}, u32[]{:S(2)}) collective-permute-start(bf16[48,512]{1,0:T(8,128)(2,1)S(1)} %get-tuple-element.33), channel_id=1, source_target_pairs={{0,8},{2,10},{1,9},{3,11},{4,12},{6,14},{5,13},{7,15},{8,0},{10,2}... | collective-permute-start | bytes 147464 | tf_op jit(solution)/shard_map/ppermute | solution.py:198
  38.8 5.5 %collective-permute-start.11 = (bf16[48,512]{1,0:T(8,128)(2,1)S(1)}, bf16[48,512]{1,0:T(8,128)(2,1)S(1)}, u32[]{:S(2)}, u32[]{:S(2)}) collective-permute-start(bf16[48,512]{1,0:T(8,128)(2,1)S(1)} %take.3), channel_id=1, source_target_pairs={{0,2},{2,0},{1,3},{3,1},{4,6},{6,4},{5,7},{7,5},{8,10},{10,8},{9,1... | collective-permute-start | bytes 147464 | tf_op jit(solution)/shard_map/ppermute | solution.py:266
  41.5 2.9 %collective-permute-start.12 = (bf16[48,512]{1,0:T(8,128)(2,1)S(1)}, bf16[48,512]{1,0:T(8,128)(2,1)S(1)}, u32[]{:S(2)}, u32[]{:S(2)}) collective-permute-start(bf16[48,512]{1,0:T(8,128)(2,1)S(1)} %take.4), channel_id=1, source_target_pairs={{0,2},{2,0},{1,3},{3,1},{4,6},{6,4},{5,7},{7,5},{8,10},{10,8},{9,1... | collective-permute-start | bytes 147464 | tf_op jit(solution)/shard_map/ppermute | solution.py:266
  43.3 1.2 %collective-permute-start.13 = (bf16[48,512]{1,0:T(8,128)(2,1)S(1)}, bf16[48,512]{1,0:T(8,128)(2,1)S(1)}, u32[]{:S(2)}, u32[]{:S(2)}) collective-permute-start(bf16[48,512]{1,0:T(8,128)(2,1)S(1)} %take.5), channel_id=1, source_target_pairs={{0,2},{2,0},{1,3},{3,1},{4,6},{6,4},{5,7},{7,5},{8,10},{10,8},{9,1... | collective-permute-start | bytes 147464 | tf_op jit(solution)/shard_map/ppermute | solution.py:266

commit v7 on v6

--- a/solution.py
+++ b/solution.py
@@ -113,7 +113,8 @@
         for base_ref, control_ref in zip(base_refs, control_refs):
             stop = start + base_ref.shape[2]
             at = slice(start, stop)
-            gain = gain_ref[:, at]
+            first = pl.multiple_of(group_index() * width + start, HD)
+            gain = gain_ref[:, pl.ds(first, stop - start)]
             hint = jnp.dot(
                 chosen_ref[...],
                 control_ref[...].reshape(len(orders_in[1]) * rows, stop - start),
@@ -242,7 +243,6 @@
         compiler_params=PARAMS,
         name="choose",
     )(block_map, token_perm)
-    gain = lax.dynamic_slice_in_dim(hint_gain, group_index() * width, width)[None, :]
     joined = pl.pallas_call(
         functools.partial(join_kernel, orders_in, orders_back, straight, rows, width),
         out_shape=[jax.ShapeDtypeStruct((2, rows, width), dtype)] * pairs
@@ -251,7 +251,7 @@
         out_specs=vmem_specs(pairs + stays),
         compiler_params=PARAMS,
         name="join",
-    )(chosen, gain, attended, other)
+    )(chosen, hint_gain[None, :], attended, other)
     returned = exchange_by_core(joined, [order + straight + [0] for order in orders_back])
     passed = []
     for piece in returned[:pairs]:

time: 45.5 us -> 45.6 us (level)
  starting transfers between devices: 27.2 us -> 28.4 us
  local copies, waits for them, and re-layouts: 2.04 us -> 1.28 us
    ppermute x3, starting transfers between devices: 2.37 us -> 3.31 us  [by_heads(): passed.append(lax.ppermute(taken, 'branch', both))]
    ppermute x11, waiting for transfers between devices: 12.6 us -> 11.7 us  [exchange_by_core(): lax.ppermute(piece, ('seq', 'branch', 'tp'), pairs)]
    dynamic_slice x1 -> x0, local copies, waits for them, and re-layouts: 0.76 us -> none  [by_heads(): lax.dynamic_slice_in_dim(hint_gain, group_index() * width, width)[None, :]]
    ppermute x1, waiting for transfers between devices: 0.01 us -> 0.48 us  [by_heads(): other = [lax.ppermute(part, 'branch', both) for part in attended]]
    unnamed x6 -> x8, local copies, waits for them, and re-layouts: 1.28 us -> 1.28 us
  transfers between devices with their start and end apart: 15 -> 15, of which waited for: 7 -> 7; matrix products, arithmetic and copies ran while one was open for 2% -> 0% of each run, Pallas kernels for 2% -> 2%
where the time goes in v7:
time: 45.6 us; the launch traced here: 45.4 us
  starting transfers between devices  28.4 us (62%)
  waiting for transfers between devices  12.5 us (27%)
  Pallas kernels  3.16 us (7%)
  local copies, waits for them, and re-layouts  1.28 us (3%)
    ppermute x11, starting transfers between devices, exchange_by_core(): lax.ppermute(piece, ('seq', 'branch', 'tp'), pairs)  24 us
    ppermute x11, waiting for transfers between devices, exchange_by_core(): lax.ppermute(piece, ('seq', 'branch', 'tp'), pairs)  11.7 us
    ppermute x3, starting transfers between devices, by_heads(): passed.append(lax.ppermute(taken, 'branch', both))  3.31 us
    unnamed x8, local copies, waits for them, and re-layouts  1.28 us
    ppermute x1, starting transfers between devices, by_heads(): other = [lax.ppermute(part, 'branch', both) for part in attended]  1.14 us
    pallas_call x1, Pallas kernels, by_heads(): pl.pallas_call(functools.partial(attend_kernel, count, rows, start, stop)...  0.94 us
  transfers between devices with their start and end apart: 15, of which 7 were waited for; matrix products, arithmetic and copies ran while one was open for 0% of the time, Pallas kernels for 2%

profile of v7, /device:TPU:0, one launch (start us, length us, event | category | flops | bytes accessed | tf_op | source)
XLA Modules:
  0.0 45.4 jit_solution(12324962747665533572)
XLA Ops:
  0.0 0.0 copy-start
  0.0 1.3 %copy-done = bf16[1,48,3,4096]{3,1,2,0:T(8,128)(2,1)S(1)} copy-done((bf16[1,48,3,4096]{3,1,2,0:T(8,128)(2,1)S(1)}, bf16[1,48,3,4096]{3,1,2,0:T(8,128)(2,1)}, u32[]{:S(2)}) %copy-start) | copy-done | bytes 1179672
  1.3 0.0 copy-start.2
  1.3 0.0 copy-start.3
  1.3 0.3 split.1
  1.5 0.0 copy-start.1
  1.6 4.1 %collective-permute-start = (bf16[3,48,512]{2,1,0:T(8,128)(2,1)S(1)}, bf16[3,48,512]{2,1,0:T(8,128)(2,1)S(1)}, u32[]{:S(2)}, u32[]{:S(2)}) collective-permute-start(bf16[3,48,512]{2,1,0:T(8,128)(2,1)S(1)} %get-tuple-element.20), channel_id=1, source_target_pairs={{0,8},{2,14},{1,9},{3,15},{4,12},{6,10},{5,13},{7,11},{8,0},{10,6}... | collective-permute-start | bytes 442376 | tf_op jit(solution)/shard_map/ppermute | solution.py:199
  5.7 2.5 %collective-permute-start.1 = (bf16[3,48,512]{2,1,0:T(8,128)(2,1)S(1)}, bf16[3,48,512]{2,1,0:T(8,128)(2,1)S(1)}, u32[]{:S(2)}, u32[]{:S(2)}) collective-permute-start(bf16[3,48,512]{2,1,0:T(8,128)(2,1)S(1)} %get-tuple-element.21), channel_id=1, source_target_pairs={{0,5},{2,3},{1,4},{3,2},{4,1},{6,7},{5,0},{7,6},{8,13},{10,11},{9,... | collective-permute-start | bytes 442376 | tf_op jit(solution)/shard_map/ppermute | solution.py:199
  8.2 0.4 collective-permute-start.2
  8.6 0.1 collective-permute-start.3
  8.7 4.8 %collective-permute-start.4 = (bf16[3,48,512]{2,1,0:T(8,128)(2,1)S(1)}, bf16[3,48,512]{2,1,0:T(8,128)(2,1)S(1)}, u32[]{:S(2)}, u32[]{:S(2)}) collective-permute-start(bf16[3,48,512]{2,1,0:T(8,128)(2,1)S(1)} %get-tuple-element.24), channel_id=1, source_target_pairs={{0,13},{2,11},{1,12},{3,10},{4,9},{6,15},{5,8},{7,14},{8,5},{10,3}... | collective-permute-start | bytes 442376 | tf_op jit(solution)/shard_map/ppermute | solution.py:199
  13.4 0.9 %collective-permute-done.refs_0_ = bf16[3,48,512]{2,1,0:T(8,128)(2,1)S(1)} collective-permute-done((bf16[3,48,512]{2,1,0:T(8,128)(2,1)S(1)}, bf16[3,48,512]{2,1,0:T(8,128)(2,1)S(1)}, u32[]{:S(2)}, u32[]{:S(2)}) %collective-permute-start) | collective-permute-done | bytes 147488 | tf_op jit(solution)/shard_map/ppermute | solution.py:199
  14.4 2.7 %collective-permute-start.5 = (bf16[3,48,512]{2,1,0:T(8,128)(2,1)S(1)}, bf16[3,48,512]{2,1,0:T(8,128)(2,1)S(1)}, u32[]{:S(2)}, u32[]{:S(2)}) collective-permute-start(bf16[3,48,512]{2,1,0:T(8,128)(2,1)S(1)} %get-tuple-element.25), channel_id=1, source_target_pairs={{0,12},{2,15},{1,13},{3,14},{4,8},{6,11},{5,9},{7,10},{8,4},{10,7}... | collective-permute-start | bytes 442376 | tf_op jit(solution)/shard_map/ppermute | solution.py:199
  17.1 0.0 collective-permute-done.1.refs_1_
  17.1 1.6 %collective-permute-start.6 = (bf16[3,48,512]{2,1,0:T(8,128)(2,1)S(1)}, bf16[3,48,512]{2,1,0:T(8,128)(2,1)S(1)}, u32[]{:S(2)}, u32[]{:S(2)}) collective-permute-start(bf16[3,48,512]{2,1,0:T(8,128)(2,1)S(1)} %get-tuple-element.26), channel_id=1, source_target_pairs={{0,1},{2,7},{1,0},{3,6},{4,5},{6,3},{5,4},{7,2},{8,9},{10,15},{9,8... | collective-permute-start | bytes 442376 | tf_op jit(solution)/shard_map/ppermute | solution.py:199
  18.7 1.4 %collective-permute-done.2.refs_2_ = bf16[3,48,512]{2,1,0:T(8,128)(2,1)S(1)} collective-permute-done((bf16[3,48,512]{2,1,0:T(8,128)(2,1)S(1)}, bf16[3,48,512]{2,1,0:T(8,128)(2,1)S(1)}, u32[]{:S(2)}, u32[]{:S(2)}) %collective-permute-start.2) | collective-permute-done | bytes 147488 | tf_op jit(solution)/shard_map/ppermute | solution.py:199
  20.1 7.2 %collective-permute-done.3.refs_3_ = bf16[3,48,512]{2,1,0:T(8,128)(2,1)S(1)} collective-permute-done((bf16[3,48,512]{2,1,0:T(8,128)(2,1)S(1)}, bf16[3,48,512]{2,1,0:T(8,128)(2,1)S(1)}, u32[]{:S(2)}, u32[]{:S(2)}) %collective-permute-start.3) | collective-permute-done | bytes 147488 | tf_op jit(solution)/shard_map/ppermute | solution.py:199
  27.3 0.0 collective-permute-done.4.refs_4_
  27.3 0.0 collective-permute-done.5.refs_5_
  27.3 0.0 collective-permute-done.6.refs_6_
  27.3 0.9 %attend.1.own_refs_0_ = bf16[8,48,512]{2,1,0:T(8,128)(2,1)S(1)} custom-call(bf16[3,48,512]{2,1,0:T(8,128)(2,1)S(1)} %collective-permute-done.refs_0_, bf16[3,48,512]{2,1,0:T(8,128)(2,1)S(1)} %collective-permute-done.1.refs_1_, bf16[3,48,512]{2,1,0:T(8,128)(2,1)S(1)} %collective-permute-done.2.refs_2_, ...), custom_call_target="tpu_custom_call" | custom-call | tf_op jit(solution)/shard_map/attend/pallas_call | solution.py:226
  28.3 1.1 %collective-permute-start.7 = (bf16[8,48,512]{2,1,0:T(8,128)(2,1)S(1)}, bf16[8,48,512]{2,1,0:T(8,128)(2,1)S(1)}, u32[]{:S(2)}, u32[]{:S(2)}) collective-permute-start(bf16[8,48,512]{2,1,0:T(8,128)(2,1)S(1)} %attend.1.own_refs_0_), channel_id=1, source_target_pairs={{0,2},{2,0},{1,3},{3,1},{4,6},{6,4},{5,7},{7,5},{8,10},{10,8},{9,1... | collective-permute-start | bytes 1179656 | tf_op jit(solution)/shard_map/ppermute | solution.py:236
  29.4 0.0 copy-done.2
  29.4 0.0 copy-done.3
  29.4 0.9 %choose.1.chosen_ref = bf16[240,384]{1,0:T(8,128)(2,1)S(1)} custom-call(s32[4]{0:T(128)S(1)} %copy-done.3, s32[8,48]{1,0:T(8,128)S(1)} %copy-done.2), custom_call_target="tpu_custom_call" | custom-call | tf_op jit(solution)/shard_map/choose/pallas_call | solution.py:238
  30.3 0.5 %collective-permute-done.7.other_refs_0_ = bf16[8,48,512]{2,1,0:T(8,128)(2,1)S(1)} collective-permute-done((bf16[8,48,512]{2,1,0:T(8,128)(2,1)S(1)}, bf16[8,48,512]{2,1,0:T(8,128)(2,1)S(1)}, u32[]{:S(2)}, u32[]{:S(2)}) %collective-permute-start.7) | collective-permute-done | bytes 393248 | tf_op jit(solution)/shard_map/ppermute | solution.py:236
  30.8 0.0 copy-done.1
  30.8 0.3 join.1
  31.1 2.6 %collective-permute-start.8 = (bf16[2,48,512]{2,1,0:T(8,128)(2,1)S(1)}, bf16[2,48,512]{2,1,0:T(8,128)(2,1)S(1)}, u32[]{:S(2)}, u32[]{:S(2)}) collective-permute-start(bf16[2,48,512]{2,1,0:T(8,128)(2,1)S(1)} %get-tuple-element.30), channel_id=1, source_target_pairs={{0,12},{2,15},{1,13},{3,14},{4,8},{6,11},{5,9},{7,10},{8,4},{10,7}... | collective-permute-start | bytes 294920 | tf_op jit(solution)/shard_map/ppermute | solution.py:199
  33.7 4.6 %collective-permute-start.9 = (bf16[2,48,512]{2,1,0:T(8,128)(2,1)S(1)}, bf16[2,48,512]{2,1,0:T(8,128)(2,1)S(1)}, u32[]{:S(2)}, u32[]{:S(2)}) collective-permute-start(bf16[2,48,512]{2,1,0:T(8,128)(2,1)S(1)} %get-tuple-element.31), channel_id=1, source_target_pairs={{0,5},{2,11},{1,4},{3,10},{4,1},{6,15},{5,0},{7,14},{8,13},{10,3},... | collective-permute-start | bytes 294920 | tf_op jit(solution)/shard_map/ppermute | solution.py:199
  38.3 0.5 %collective-permute-start.10 = (bf16[2,48,512]{2,1,0:T(8,128)(2,1)S(1)}, bf16[2,48,512]{2,1,0:T(8,128)(2,1)S(1)}, u32[]{:S(2)}, u32[]{:S(2)}) collective-permute-start(bf16[2,48,512]{2,1,0:T(8,128)(2,1)S(1)} %get-tuple-element.32), channel_id=1, source_target_pairs={{0,1},{2,6},{1,0},{3,7},{4,5},{6,2},{5,4},{7,3},{8,9},{10,14},{9,8... | collective-permute-start | bytes 294920 | tf_op jit(solution)/shard_map/ppermute | solution.py:199
  38.8 0.0 collective-permute-start.14
  38.8 0.0 collective-permute-done.8.in_ref.refs_0__0_
  38.8 1.4 %collective-permute-start.11 = (bf16[48,512]{1,0:T(8,128)(2,1)S(1)}, bf16[48,512]{1,0:T(8,128)(2,1)S(1)}, u32[]{:S(2)}, u32[]{:S(2)}) collective-permute-start(bf16[48,512]{1,0:T(8,128)(2,1)S(1)} %take.3), channel_id=1, source_target_pairs={{0,2},{2,0},{1,3},{3,1},{4,6},{6,4},{5,7},{7,5},{8,10},{10,8},{9,1... | collective-permute-start | bytes 147464 | tf_op jit(solution)/shard_map/ppermute | solution.py:266
  40.3 1.3 %collective-permute-done.9.in_ref.refs_0__1_ = bf16[2,48,512]{2,1,0:T(8,128)(2,1)S(1)} collective-permute-done((bf16[2,48,512]{2,1,0:T(8,128)(2,1)S(1)}, bf16[2,48,512]{2,1,0:T(8,128)(2,1)S(1)}, u32[]{:S(2)}, u32[]{:S(2)}) %collective-permute-start.9) | collective-permute-done | bytes 98336 | tf_op jit(solution)/shard_map/ppermute | solution.py:199
  41.5 1.8 %collective-permute-start.12 = (bf16[48,512]{1,0:T(8,128)(2,1)S(1)}, bf16[48,512]{1,0:T(8,128)(2,1)S(1)}, u32[]{:S(2)}, u32[]{:S(2)}) collective-permute-start(bf16[48,512]{1,0:T(8,128)(2,1)S(1)} %take.4), channel_id=1, source_target_pairs={{0,2},{2,0},{1,3},{3,1},{4,6},{6,4},{5,7},{7,5},{8,10},{10,8},{9,1... | collective-permute-start | bytes 147464 | tf_op jit(solution)/shard_map/ppermute | solution.py:266
  43.3 0.0 collective-permute-done.10.in_ref.refs_0__2_
  43.3 0.1 collective-permute-start.13
  43.4 0.9 %collective-permute-done.14.refs_2__0_ = bf16[48,512]{1,0:T(8,128)(2,1)S(1)} collective-permute-done((bf16[48,512]{1,0:T(8,128)(2,1)S(1)}, bf16[48,512]{1,0:T(8,128)(2,1)S(1)}, u32[]{:S(2)}, u32[]{:S(2)}) %collective-permute-start.14) | collective-permute-done | bytes 49184 | tf_op jit(solution)/shard_map/ppermute | solution.py:199
  44.3 0.0 collective-permute-done.11.refs_1__0_
  44.3 0.0 collective-permute-done.12.refs_1__1_
  44.3 0.3 collective-permute-done.13.refs_1__2_
  44.6 0.8 %merge.1 = bf16[48,4096]{1,0:T(8,128)(2,1)} custom-call(bf16[2,48,512]{2,1,0:T(8,128)(2,1)S(1)} %collective-permute-done.8.in_ref.refs_0__0_, bf16[2,48,512]{2,1,0:T(8,128)(2,1)S(1)} %collective-permute-done.9.in_ref.refs_0__1_, bf16[2,48,512]{2,1,0:T(8,128)(2,1)S(1)} %collective-permute-done.10.in_ref.refs_0__2_, ...), custom_call_target="tpu_custom_call" | custom-call | tf_op jit(solution)/shard_map/merge/pallas_call | solution.py:269
  (3 shorter events, 0.0 us)
Async XLA Ops:
  0.0 1.3 %copy-start = (bf16[1,48,3,4096]{3,1,2,0:T(8,128)(2,1)S(1)}, bf16[1,48,3,4096]{3,1,2,0:T(8,128)(2,1)}, u32[]{:S(2)}) copy-start(bf16[1,48,3,4096]{3,1,2,0:T(8,128)(2,1)} %param.4) | copy-start | bytes 3538948
  1.3 28.2 %copy-start.2 = (s32[8,48]{1,0:T(8,128)S(1)}, s32[8,48]{1,0:T(8,128)}, u32[]{:S(2)}) copy-start(s32[8,48]{1,0:T(8,128)} %perm_ref.1) | copy-start | bytes 4612
  1.3 28.2 %copy-start.3 = (s32[4]{0:T(128)S(1)}, s32[4]{0:T(128)}, u32[]{:S(2)}) copy-start(s32[4]{0:T(128)} %map_ref) | copy-start | bytes 52
  1.5 29.2 %copy-start.1 = (f32[4096]{0:T(1024)S(1)}, f32[4096]{0:T(1024)}, u32[]{:S(2)}) copy-start(f32[4096]{0:T(1024)} %param.5) | copy-start | bytes 49156
  1.6 12.8 %collective-permute-start = (bf16[3,48,512]{2,1,0:T(8,128)(2,1)S(1)}, bf16[3,48,512]{2,1,0:T(8,128)(2,1)S(1)}, u32[]{:S(2)}, u32[]{:S(2)}) collective-permute-start(bf16[3,48,512]{2,1,0:T(8,128)(2,1)S(1)} %get-tuple-element.20), channel_id=1, source_target_pairs={{0,8},{2,14},{1,9},{3,15},{4,12},{6,10},{5,13},{7,11},{8,0},{10,6}... | collective-permute-start | bytes 442376 | tf_op jit(solution)/shard_map/ppermute | solution.py:199
  5.7 11.5 %collective-permute-start.1 = (bf16[3,48,512]{2,1,0:T(8,128)(2,1)S(1)}, bf16[3,48,512]{2,1,0:T(8,128)(2,1)S(1)}, u32[]{:S(2)}, u32[]{:S(2)}) collective-permute-start(bf16[3,48,512]{2,1,0:T(8,128)(2,1)S(1)} %get-tuple-element.21), channel_id=1, source_target_pairs={{0,5},{2,3},{1,4},{3,2},{4,1},{6,7},{5,0},{7,6},{8,13},{10,11},{9,... | collective-permute-start | bytes 442376 | tf_op jit(solution)/shard_map/ppermute | solution.py:199
  8.2 12.0 %collective-permute-start.2 = (bf16[3,48,512]{2,1,0:T(8,128)(2,1)S(1)}, bf16[3,48,512]{2,1,0:T(8,128)(2,1)S(1)}, u32[]{:S(2)}, u32[]{:S(2)}) collective-permute-start(bf16[3,48,512]{2,1,0:T(8,128)(2,1)S(1)} %get-tuple-element.22), channel_id=1, source_target_pairs={{0,4},{2,6},{1,5},{3,7},{4,0},{6,2},{5,1},{7,3},{8,12},{10,14},{9,... | collective-permute-start | bytes 442376 | tf_op jit(solution)/shard_map/ppermute | solution.py:199
  8.6 18.7 %collective-permute-start.3 = (bf16[3,48,512]{2,1,0:T(8,128)(2,1)S(1)}, bf16[3,48,512]{2,1,0:T(8,128)(2,1)S(1)}, u32[]{:S(2)}, u32[]{:S(2)}) collective-permute-start(bf16[3,48,512]{2,1,0:T(8,128)(2,1)S(1)} %get-tuple-element.23), channel_id=1, source_target_pairs={{0,9},{2,10},{1,8},{3,11},{4,13},{6,14},{5,12},{7,15},{8,1},{10,2}... | collective-permute-start | bytes 442376 | tf_op jit(solution)/shard_map/ppermute | solution.py:199
  8.7 18.7 %collective-permute-start.4 = (bf16[3,48,512]{2,1,0:T(8,128)(2,1)S(1)}, bf16[3,48,512]{2,1,0:T(8,128)(2,1)S(1)}, u32[]{:S(2)}, u32[]{:S(2)}) collective-permute-start(bf16[3,48,512]{2,1,0:T(8,128)(2,1)S(1)} %get-tuple-element.24), channel_id=1, source_target_pairs={{0,13},{2,11},{1,12},{3,10},{4,9},{6,15},{5,8},{7,14},{8,5},{10,3}... | collective-permute-start | bytes 442376 | tf_op jit(solution)/shard_map/ppermute | solution.py:199
  14.4 13.0 %collective-permute-start.5 = (bf16[3,48,512]{2,1,0:T(8,128)(2,1)S(1)}, bf16[3,48,512]{2,1,0:T(8,128)(2,1)S(1)}, u32[]{:S(2)}, u32[]{:S(2)}) collective-permute-start(bf16[3,48,512]{2,1,0:T(8,128)(2,1)S(1)} %get-tuple-element.25), channel_id=1, source_target_pairs={{0,12},{2,15},{1,13},{3,14},{4,8},{6,11},{5,9},{7,10},{8,4},{10,7}... | collective-permute-start | bytes 442376 | tf_op jit(solution)/shard_map/ppermute | solution.py:199
  17.1 10.2 %collective-permute-start.6 = (bf16[3,48,512]{2,1,0:T(8,128)(2,1)S(1)}, bf16[3,48,512]{2,1,0:T(8,128)(2,1)S(1)}, u32[]{:S(2)}, u32[]{:S(2)}) collective-permute-start(bf16[3,48,512]{2,1,0:T(8,128)(2,1)S(1)} %get-tuple-element.26), channel_id=1, source_target_pairs={{0,1},{2,7},{1,0},{3,6},{4,5},{6,3},{5,4},{7,2},{8,9},{10,15},{9,8... | collective-permute-start | bytes 442376 | tf_op jit(solution)/shard_map/ppermute | solution.py:199
  28.3 2.5 %collective-permute-start.7 = (bf16[8,48,512]{2,1,0:T(8,128)(2,1)S(1)}, bf16[8,48,512]{2,1,0:T(8,128)(2,1)S(1)}, u32[]{:S(2)}, u32[]{:S(2)}) collective-permute-start(bf16[8,48,512]{2,1,0:T(8,128)(2,1)S(1)} %attend.1.own_refs_0_), channel_id=1, source_target_pairs={{0,2},{2,0},{1,3},{3,1},{4,6},{6,4},{5,7},{7,5},{8,10},{10,8},{9,1... | collective-permute-start | bytes 1179656 | tf_op jit(solution)/shard_map/ppermute | solution.py:236
  31.1 7.7 %collective-permute-start.8 = (bf16[2,48,512]{2,1,0:T(8,128)(2,1)S(1)}, bf16[2,48,512]{2,1,0:T(8,128)(2,1)S(1)}, u32[]{:S(2)}, u32[]{:S(2)}) collective-permute-start(bf16[2,48,512]{2,1,0:T(8,128)(2,1)S(1)} %get-tuple-element.30), channel_id=1, source_target_pairs={{0,12},{2,15},{1,13},{3,14},{4,8},{6,11},{5,9},{7,10},{8,4},{10,7}... | collective-permute-start | bytes 294920 | tf_op jit(solution)/shard_map/ppermute | solution.py:199
  33.7 7.9 %collective-permute-start.9 = (bf16[2,48,512]{2,1,0:T(8,128)(2,1)S(1)}, bf16[2,48,512]{2,1,0:T(8,128)(2,1)S(1)}, u32[]{:S(2)}, u32[]{:S(2)}) collective-permute-start(bf16[2,48,512]{2,1,0:T(8,128)(2,1)S(1)} %get-tuple-element.31), channel_id=1, source_target_pairs={{0,5},{2,11},{1,4},{3,10},{4,1},{6,15},{5,0},{7,14},{8,13},{10,3},... | collective-permute-start | bytes 294920 | tf_op jit(solution)/shard_map/ppermute | solution.py:199
  38.3 5.0 %collective-permute-start.10 = (bf16[2,48,512]{2,1,0:T(8,128)(2,1)S(1)}, bf16[2,48,512]{2,1,0:T(8,128)(2,1)S(1)}, u32[]{:S(2)}, u32[]{:S(2)}) collective-permute-start(bf16[2,48,512]{2,1,0:T(8,128)(2,1)S(1)} %get-tuple-element.32), channel_id=1, source_target_pairs={{0,1},{2,6},{1,0},{3,7},{4,5},{6,2},{5,4},{7,3},{8,9},{10,14},{9,8... | collective-permute-start | bytes 294920 | tf_op jit(solution)/shard_map/ppermute | solution.py:199
  38.8 5.5 %collective-permute-start.14 = (bf16[48,512]{1,0:T(8,128)(2,1)S(1)}, bf16[48,512]{1,0:T(8,128)(2,1)S(1)}, u32[]{:S(2)}, u32[]{:S(2)}) collective-permute-start(bf16[48,512]{1,0:T(8,128)(2,1)S(1)} %get-tuple-element.33), channel_id=1, source_target_pairs={{0,8},{2,10},{1,9},{3,11},{4,12},{6,14},{5,13},{7,15},{8,0},{10,2}... | collective-permute-start | bytes 147464 | tf_op jit(solution)/shard_map/ppermute | solution.py:199
  38.8 5.5 %collective-permute-start.11 = (bf16[48,512]{1,0:T(8,128)(2,1)S(1)}, bf16[48,512]{1,0:T(8,128)(2,1)S(1)}, u32[]{:S(2)}, u32[]{:S(2)}) collective-permute-start(bf16[48,512]{1,0:T(8,128)(2,1)S(1)} %take.3), channel_id=1, source_target_pairs={{0,2},{2,0},{1,3},{3,1},{4,6},{6,4},{5,7},{7,5},{8,10},{10,8},{9,1... | collective-permute-start | bytes 147464 | tf_op jit(solution)/shard_map/ppermute | solution.py:266
  41.5 2.8 %collective-permute-start.12 = (bf16[48,512]{1,0:T(8,128)(2,1)S(1)}, bf16[48,512]{1,0:T(8,128)(2,1)S(1)}, u32[]{:S(2)}, u32[]{:S(2)}) collective-permute-start(bf16[48,512]{1,0:T(8,128)(2,1)S(1)} %take.4), channel_id=1, source_target_pairs={{0,2},{2,0},{1,3},{3,1},{4,6},{6,4},{5,7},{7,5},{8,10},{10,8},{9,1... | collective-permute-start | bytes 147464 | tf_op jit(solution)/shard_map/ppermute | solution.py:266
  43.3 1.3 %collective-permute-start.13 = (bf16[48,512]{1,0:T(8,128)(2,1)S(1)}, bf16[48,512]{1,0:T(8,128)(2,1)S(1)}, u32[]{:S(2)}, u32[]{:S(2)}) collective-permute-start(bf16[48,512]{1,0:T(8,128)(2,1)S(1)} %take.5), channel_id=1, source_target_pairs={{0,2},{2,0},{1,3},{3,1},{4,6},{6,4},{5,7},{7,5},{8,10},{10,8},{9,1... | collective-permute-start | bytes 147464 | tf_op jit(solution)/shard_map/ppermute | solution.py:266

commit v8 on v7

--- a/solution.py
+++ b/solution.py
@@ -13,7 +13,7 @@
 
 key_block = 512
 
-ORDER_IN = ((4, 3, 2, 5, 7, 6, 1), (6, 1, 2, 4, 5, 7, 3))
+ORDER_IN = ((4, 3, 2, 5, 7, 6, 1), (6, 2, 1, 4, 5, 7, 3))
 ORDER_BACK = ((6, 3, 1), (7, 5, 2))
 STRAIGHT = (4,)
 STRAIGHT_FIRST = False

time: 45.6 us -> 45.4 us (level)
  starting transfers between devices: 28.4 us -> 27 us
  waiting for transfers between devices: 12.5 us -> 13.7 us
    ppermute x3, starting transfers between devices: 3.31 us -> 1.9 us  [by_heads(): passed.append(lax.ppermute(taken, 'branch', both))]
    ppermute x11, waiting for transfers between devices: 11.7 us -> 13.1 us  [exchange_by_core(): lax.ppermute(piece, ('seq', 'branch', 'tp'), pairs)]
where the time goes in v8:
time: 45.4 us; the launch traced here: 45.2 us
  starting transfers between devices  27 us (59%)
  waiting for transfers between devices  13.7 us (30%)
  Pallas kernels  3.16 us (7%)
  local copies, waits for them, and re-layouts  1.28 us (3%)
    ppermute x11, starting transfers between devices, exchange_by_core(): lax.ppermute(piece, ('seq', 'branch', 'tp'), pairs)  24 us
    ppermute x11, waiting for transfers between devices, exchange_by_core(): lax.ppermute(piece, ('seq', 'branch', 'tp'), pairs)  13.1 us
    ppermute x3, starting transfers between devices, by_heads(): passed.append(lax.ppermute(taken, 'branch', both))  1.9 us
    unnamed x8, local copies, waits for them, and re-layouts  1.28 us
    ppermute x1, starting transfers between devices, by_heads(): other = [lax.ppermute(part, 'branch', both) for part in attended]  1.14 us
    pallas_call x1, Pallas kernels, by_heads(): pl.pallas_call(functools.partial(attend_kernel, count, rows, start, stop)...  0.94 us
  transfers between devices with their start and end apart: 15, of which 7 were waited for; matrix products, arithmetic and copies ran while one was open for 0% of the time, Pallas kernels for 2%

profile of v8, /device:TPU:0, one launch (start us, length us, event | category | flops | bytes accessed | tf_op | source)
XLA Modules:
  0.0 45.2 jit_solution(15197754919891135041)
XLA Ops:
  0.0 0.0 copy-start
  0.0 1.3 %copy-done = bf16[1,48,3,4096]{3,1,2,0:T(8,128)(2,1)S(1)} copy-done((bf16[1,48,3,4096]{3,1,2,0:T(8,128)(2,1)S(1)}, bf16[1,48,3,4096]{3,1,2,0:T(8,128)(2,1)}, u32[]{:S(2)}) %copy-start) | copy-done | bytes 1179672
  1.3 0.0 copy-start.2
  1.3 0.0 copy-start.3
  1.3 0.3 split.1
  1.5 0.0 copy-start.1
  1.6 4.1 %collective-permute-start = (bf16[3,48,512]{2,1,0:T(8,128)(2,1)S(1)}, bf16[3,48,512]{2,1,0:T(8,128)(2,1)S(1)}, u32[]{:S(2)}, u32[]{:S(2)}) collective-permute-start(bf16[3,48,512]{2,1,0:T(8,128)(2,1)S(1)} %get-tuple-element.20), channel_id=1, source_target_pairs={{0,8},{2,14},{1,9},{3,15},{4,12},{6,10},{5,13},{7,11},{8,0},{10,6}... | collective-permute-start | bytes 442376 | tf_op jit(solution)/shard_map/ppermute | solution.py:199
  5.7 2.5 %collective-permute-start.1 = (bf16[3,48,512]{2,1,0:T(8,128)(2,1)S(1)}, bf16[3,48,512]{2,1,0:T(8,128)(2,1)S(1)}, u32[]{:S(2)}, u32[]{:S(2)}) collective-permute-start(bf16[3,48,512]{2,1,0:T(8,128)(2,1)S(1)} %get-tuple-element.21), channel_id=1, source_target_pairs={{0,5},{2,6},{1,4},{3,7},{4,1},{6,2},{5,0},{7,3},{8,13},{10,14},{9,... | collective-permute-start | bytes 442376 | tf_op jit(solution)/shard_map/ppermute | solution.py:199
  8.2 0.4 collective-permute-start.2
  8.6 0.0 collective-permute-start.3
  8.7 4.8 %collective-permute-start.4 = (bf16[3,48,512]{2,1,0:T(8,128)(2,1)S(1)}, bf16[3,48,512]{2,1,0:T(8,128)(2,1)S(1)}, u32[]{:S(2)}, u32[]{:S(2)}) collective-permute-start(bf16[3,48,512]{2,1,0:T(8,128)(2,1)S(1)} %get-tuple-element.24), channel_id=1, source_target_pairs={{0,13},{2,11},{1,12},{3,10},{4,9},{6,15},{5,8},{7,14},{8,5},{10,3}... | collective-permute-start | bytes 442376 | tf_op jit(solution)/shard_map/ppermute | solution.py:199
  13.4 0.9 %collective-permute-done.refs_0_ = bf16[3,48,512]{2,1,0:T(8,128)(2,1)S(1)} collective-permute-done((bf16[3,48,512]{2,1,0:T(8,128)(2,1)S(1)}, bf16[3,48,512]{2,1,0:T(8,128)(2,1)S(1)}, u32[]{:S(2)}, u32[]{:S(2)}) %collective-permute-start) | collective-permute-done | bytes 147488 | tf_op jit(solution)/shard_map/ppermute | solution.py:199
  14.4 2.7 %collective-permute-start.5 = (bf16[3,48,512]{2,1,0:T(8,128)(2,1)S(1)}, bf16[3,48,512]{2,1,0:T(8,128)(2,1)S(1)}, u32[]{:S(2)}, u32[]{:S(2)}) collective-permute-start(bf16[3,48,512]{2,1,0:T(8,128)(2,1)S(1)} %get-tuple-element.25), channel_id=1, source_target_pairs={{0,12},{2,15},{1,13},{3,14},{4,8},{6,11},{5,9},{7,10},{8,4},{10,7}... | collective-permute-start | bytes 442376 | tf_op jit(solution)/shard_map/ppermute | solution.py:199
  17.1 0.0 collective-permute-done.1.refs_1_
  17.1 1.6 %collective-permute-start.6 = (bf16[3,48,512]{2,1,0:T(8,128)(2,1)S(1)}, bf16[3,48,512]{2,1,0:T(8,128)(2,1)S(1)}, u32[]{:S(2)}, u32[]{:S(2)}) collective-permute-start(bf16[3,48,512]{2,1,0:T(8,128)(2,1)S(1)} %get-tuple-element.26), channel_id=1, source_target_pairs={{0,1},{2,7},{1,0},{3,6},{4,5},{6,3},{5,4},{7,2},{8,9},{10,15},{9,8... | collective-permute-start | bytes 442376 | tf_op jit(solution)/shard_map/ppermute | solution.py:199
  18.7 0.0 collective-permute-done.2.refs_2_
  18.7 8.6 %collective-permute-done.3.refs_3_ = bf16[3,48,512]{2,1,0:T(8,128)(2,1)S(1)} collective-permute-done((bf16[3,48,512]{2,1,0:T(8,128)(2,1)S(1)}, bf16[3,48,512]{2,1,0:T(8,128)(2,1)S(1)}, u32[]{:S(2)}, u32[]{:S(2)}) %collective-permute-start.3) | collective-permute-done | bytes 147488 | tf_op jit(solution)/shard_map/ppermute | solution.py:199
  27.3 0.0 collective-permute-done.4.refs_4_
  27.3 0.0 collective-permute-done.5.refs_5_
  27.3 0.0 collective-permute-done.6.refs_6_
  27.3 0.9 %attend.1.own_refs_0_ = bf16[8,48,512]{2,1,0:T(8,128)(2,1)S(1)} custom-call(bf16[3,48,512]{2,1,0:T(8,128)(2,1)S(1)} %collective-permute-done.refs_0_, bf16[3,48,512]{2,1,0:T(8,128)(2,1)S(1)} %collective-permute-done.1.refs_1_, bf16[3,48,512]{2,1,0:T(8,128)(2,1)S(1)} %collective-permute-done.2.refs_2_, ...), custom_call_target="tpu_custom_call" | custom-call | tf_op jit(solution)/shard_map/attend/pallas_call | solution.py:226
  28.3 1.1 %collective-permute-start.7 = (bf16[8,48,512]{2,1,0:T(8,128)(2,1)S(1)}, bf16[8,48,512]{2,1,0:T(8,128)(2,1)S(1)}, u32[]{:S(2)}, u32[]{:S(2)}) collective-permute-start(bf16[8,48,512]{2,1,0:T(8,128)(2,1)S(1)} %attend.1.own_refs_0_), channel_id=1, source_target_pairs={{0,2},{2,0},{1,3},{3,1},{4,6},{6,4},{5,7},{7,5},{8,10},{10,8},{9,1... | collective-permute-start | bytes 1179656 | tf_op jit(solution)/shard_map/ppermute | solution.py:236
  29.4 0.0 copy-done.2
  29.4 0.0 copy-done.3
  29.4 0.9 %choose.1.chosen_ref = bf16[240,384]{1,0:T(8,128)(2,1)S(1)} custom-call(s32[4]{0:T(128)S(1)} %copy-done.3, s32[8,48]{1,0:T(8,128)S(1)} %copy-done.2), custom_call_target="tpu_custom_call" | custom-call | tf_op jit(solution)/shard_map/choose/pallas_call | solution.py:238
  30.3 0.5 %collective-permute-done.7.other_refs_0_ = bf16[8,48,512]{2,1,0:T(8,128)(2,1)S(1)} collective-permute-done((bf16[8,48,512]{2,1,0:T(8,128)(2,1)S(1)}, bf16[8,48,512]{2,1,0:T(8,128)(2,1)S(1)}, u32[]{:S(2)}, u32[]{:S(2)}) %collective-permute-start.7) | collective-permute-done | bytes 393248 | tf_op jit(solution)/shard_map/ppermute | solution.py:236
  30.8 0.0 copy-done.1
  30.8 0.3 join.1
  31.1 2.5 %collective-permute-start.8 = (bf16[2,48,512]{2,1,0:T(8,128)(2,1)S(1)}, bf16[2,48,512]{2,1,0:T(8,128)(2,1)S(1)}, u32[]{:S(2)}, u32[]{:S(2)}) collective-permute-start(bf16[2,48,512]{2,1,0:T(8,128)(2,1)S(1)} %get-tuple-element.30), channel_id=1, source_target_pairs={{0,12},{2,15},{1,13},{3,14},{4,8},{6,11},{5,9},{7,10},{8,4},{10,7}... | collective-permute-start | bytes 294920 | tf_op jit(solution)/shard_map/ppermute | solution.py:199
  33.6 4.7 %collective-permute-start.9 = (bf16[2,48,512]{2,1,0:T(8,128)(2,1)S(1)}, bf16[2,48,512]{2,1,0:T(8,128)(2,1)S(1)}, u32[]{:S(2)}, u32[]{:S(2)}) collective-permute-start(bf16[2,48,512]{2,1,0:T(8,128)(2,1)S(1)} %get-tuple-element.31), channel_id=1, source_target_pairs={{0,5},{2,11},{1,4},{3,10},{4,1},{6,15},{5,0},{7,14},{8,13},{10,3},... | collective-permute-start | bytes 294920 | tf_op jit(solution)/shard_map/ppermute | solution.py:199
  38.3 0.5 %collective-permute-start.10 = (bf16[2,48,512]{2,1,0:T(8,128)(2,1)S(1)}, bf16[2,48,512]{2,1,0:T(8,128)(2,1)S(1)}, u32[]{:S(2)}, u32[]{:S(2)}) collective-permute-start(bf16[2,48,512]{2,1,0:T(8,128)(2,1)S(1)} %get-tuple-element.32), channel_id=1, source_target_pairs={{0,1},{2,6},{1,0},{3,7},{4,5},{6,2},{5,4},{7,3},{8,9},{10,14},{9,8... | collective-permute-start | bytes 294920 | tf_op jit(solution)/shard_map/ppermute | solution.py:199
  38.8 0.0 collective-permute-start.14
  38.8 0.0 collective-permute-done.8.in_ref.refs_0__0_
  38.8 1.4 %collective-permute-start.11 = (bf16[48,512]{1,0:T(8,128)(2,1)S(1)}, bf16[48,512]{1,0:T(8,128)(2,1)S(1)}, u32[]{:S(2)}, u32[]{:S(2)}) collective-permute-start(bf16[48,512]{1,0:T(8,128)(2,1)S(1)} %take.3), channel_id=1, source_target_pairs={{0,2},{2,0},{1,3},{3,1},{4,6},{6,4},{5,7},{7,5},{8,10},{10,8},{9,1... | collective-permute-start | bytes 147464 | tf_op jit(solution)/shard_map/ppermute | solution.py:266
  40.3 1.3 %collective-permute-done.9.in_ref.refs_0__1_ = bf16[2,48,512]{2,1,0:T(8,128)(2,1)S(1)} collective-permute-done((bf16[2,48,512]{2,1,0:T(8,128)(2,1)S(1)}, bf16[2,48,512]{2,1,0:T(8,128)(2,1)S(1)}, u32[]{:S(2)}, u32[]{:S(2)}) %collective-permute-start.9) | collective-permute-done | bytes 98336 | tf_op jit(solution)/shard_map/ppermute | solution.py:199
  41.5 0.5 %collective-permute-start.12 = (bf16[48,512]{1,0:T(8,128)(2,1)S(1)}, bf16[48,512]{1,0:T(8,128)(2,1)S(1)}, u32[]{:S(2)}, u32[]{:S(2)}) collective-permute-start(bf16[48,512]{1,0:T(8,128)(2,1)S(1)} %take.4), channel_id=1, source_target_pairs={{0,2},{2,0},{1,3},{3,1},{4,6},{6,4},{5,7},{7,5},{8,10},{10,8},{9,1... | collective-permute-start | bytes 147464 | tf_op jit(solution)/shard_map/ppermute | solution.py:266
  42.0 1.2 %collective-permute-done.10.in_ref.refs_0__2_ = bf16[2,48,512]{2,1,0:T(8,128)(2,1)S(1)} collective-permute-done((bf16[2,48,512]{2,1,0:T(8,128)(2,1)S(1)}, bf16[2,48,512]{2,1,0:T(8,128)(2,1)S(1)}, u32[]{:S(2)}, u32[]{:S(2)}) %collective-permute-start.10) | collective-permute-done | bytes 98336 | tf_op jit(solution)/shard_map/ppermute | solution.py:199
  43.2 0.0 collective-permute-start.13
  43.2 1.0 %collective-permute-done.14.refs_2__0_ = bf16[48,512]{1,0:T(8,128)(2,1)S(1)} collective-permute-done((bf16[48,512]{1,0:T(8,128)(2,1)S(1)}, bf16[48,512]{1,0:T(8,128)(2,1)S(1)}, u32[]{:S(2)}, u32[]{:S(2)}) %collective-permute-start.14) | collective-permute-done | bytes 49184 | tf_op jit(solution)/shard_map/ppermute | solution.py:199
  44.3 0.0 collective-permute-done.11.refs_1__0_
  44.3 0.0 collective-permute-done.12.refs_1__1_
  44.3 0.2 collective-permute-done.13.refs_1__2_
  44.4 0.8 %merge.1 = bf16[48,4096]{1,0:T(8,128)(2,1)} custom-call(bf16[2,48,512]{2,1,0:T(8,128)(2,1)S(1)} %collective-permute-done.8.in_ref.refs_0__0_, bf16[2,48,512]{2,1,0:T(8,128)(2,1)S(1)} %collective-permute-done.9.in_ref.refs_0__1_, bf16[2,48,512]{2,1,0:T(8,128)(2,1)S(1)} %collective-permute-done.10.in_ref.refs_0__2_, ...), custom_call_target="tpu_custom_call" | custom-call | tf_op jit(solution)/shard_map/merge/pallas_call | solution.py:269
  (3 shorter events, 0.0 us)
Async XLA Ops:
  0.0 1.3 %copy-start = (bf16[1,48,3,4096]{3,1,2,0:T(8,128)(2,1)S(1)}, bf16[1,48,3,4096]{3,1,2,0:T(8,128)(2,1)}, u32[]{:S(2)}) copy-start(bf16[1,48,3,4096]{3,1,2,0:T(8,128)(2,1)} %param.4) | copy-start | bytes 3538948
  1.3 28.2 %copy-start.2 = (s32[8,48]{1,0:T(8,128)S(1)}, s32[8,48]{1,0:T(8,128)}, u32[]{:S(2)}) copy-start(s32[8,48]{1,0:T(8,128)} %perm_ref.1) | copy-start | bytes 4612
  1.3 28.2 %copy-start.3 = (s32[4]{0:T(128)S(1)}, s32[4]{0:T(128)}, u32[]{:S(2)}) copy-start(s32[4]{0:T(128)} %map_ref) | copy-start | bytes 52
  1.5 29.2 %copy-start.1 = (f32[4096]{0:T(1024)S(1)}, f32[4096]{0:T(1024)}, u32[]{:S(2)}) copy-start(f32[4096]{0:T(1024)} %param.5) | copy-start | bytes 49156
  1.6 12.8 %collective-permute-start = (bf16[3,48,512]{2,1,0:T(8,128)(2,1)S(1)}, bf16[3,48,512]{2,1,0:T(8,128)(2,1)S(1)}, u32[]{:S(2)}, u32[]{:S(2)}) collective-permute-start(bf16[3,48,512]{2,1,0:T(8,128)(2,1)S(1)} %get-tuple-element.20), channel_id=1, source_target_pairs={{0,8},{2,14},{1,9},{3,15},{4,12},{6,10},{5,13},{7,11},{8,0},{10,6}... | collective-permute-start | bytes 442376 | tf_op jit(solution)/shard_map/ppermute | solution.py:199
  5.7 11.5 %collective-permute-start.1 = (bf16[3,48,512]{2,1,0:T(8,128)(2,1)S(1)}, bf16[3,48,512]{2,1,0:T(8,128)(2,1)S(1)}, u32[]{:S(2)}, u32[]{:S(2)}) collective-permute-start(bf16[3,48,512]{2,1,0:T(8,128)(2,1)S(1)} %get-tuple-element.21), channel_id=1, source_target_pairs={{0,5},{2,6},{1,4},{3,7},{4,1},{6,2},{5,0},{7,3},{8,13},{10,14},{9,... | collective-permute-start | bytes 442376 | tf_op jit(solution)/shard_map/ppermute | solution.py:199
  8.2 10.6 %collective-permute-start.2 = (bf16[3,48,512]{2,1,0:T(8,128)(2,1)S(1)}, bf16[3,48,512]{2,1,0:T(8,128)(2,1)S(1)}, u32[]{:S(2)}, u32[]{:S(2)}) collective-permute-start(bf16[3,48,512]{2,1,0:T(8,128)(2,1)S(1)} %get-tuple-element.22), channel_id=1, source_target_pairs={{0,4},{2,3},{1,5},{3,2},{4,0},{6,7},{5,1},{7,6},{8,12},{10,11},{9,... | collective-permute-start | bytes 442376 | tf_op jit(solution)/shard_map/ppermute | solution.py:199
  8.6 18.7 %collective-permute-start.3 = (bf16[3,48,512]{2,1,0:T(8,128)(2,1)S(1)}, bf16[3,48,512]{2,1,0:T(8,128)(2,1)S(1)}, u32[]{:S(2)}, u32[]{:S(2)}) collective-permute-start(bf16[3,48,512]{2,1,0:T(8,128)(2,1)S(1)} %get-tuple-element.23), channel_id=1, source_target_pairs={{0,9},{2,10},{1,8},{3,11},{4,13},{6,14},{5,12},{7,15},{8,1},{10,2}... | collective-permute-start | bytes 442376 | tf_op jit(solution)/shard_map/ppermute | solution.py:199
  8.7 18.7 %collective-permute-start.4 = (bf16[3,48,512]{2,1,0:T(8,128)(2,1)S(1)}, bf16[3,48,512]{2,1,0:T(8,128)(2,1)S(1)}, u32[]{:S(2)}, u32[]{:S(2)}) collective-permute-start(bf16[3,48,512]{2,1,0:T(8,128)(2,1)S(1)} %get-tuple-element.24), channel_id=1, source_target_pairs={{0,13},{2,11},{1,12},{3,10},{4,9},{6,15},{5,8},{7,14},{8,5},{10,3}... | collective-permute-start | bytes 442376 | tf_op jit(solution)/shard_map/ppermute | solution.py:199
  14.4 13.0 %collective-permute-start.5 = (bf16[3,48,512]{2,1,0:T(8,128)(2,1)S(1)}, bf16[3,48,512]{2,1,0:T(8,128)(2,1)S(1)}, u32[]{:S(2)}, u32[]{:S(2)}) collective-permute-start(bf16[3,48,512]{2,1,0:T(8,128)(2,1)S(1)} %get-tuple-element.25), channel_id=1, source_target_pairs={{0,12},{2,15},{1,13},{3,14},{4,8},{6,11},{5,9},{7,10},{8,4},{10,7}... | collective-permute-start | bytes 442376 | tf_op jit(solution)/shard_map/ppermute | solution.py:199
  17.1 10.2 %collective-permute-start.6 = (bf16[3,48,512]{2,1,0:T(8,128)(2,1)S(1)}, bf16[3,48,512]{2,1,0:T(8,128)(2,1)S(1)}, u32[]{:S(2)}, u32[]{:S(2)}) collective-permute-start(bf16[3,48,512]{2,1,0:T(8,128)(2,1)S(1)} %get-tuple-element.26), channel_id=1, source_target_pairs={{0,1},{2,7},{1,0},{3,6},{4,5},{6,3},{5,4},{7,2},{8,9},{10,15},{9,8... | collective-permute-start | bytes 442376 | tf_op jit(solution)/shard_map/ppermute | solution.py:199
  28.3 2.5 %collective-permute-start.7 = (bf16[8,48,512]{2,1,0:T(8,128)(2,1)S(1)}, bf16[8,48,512]{2,1,0:T(8,128)(2,1)S(1)}, u32[]{:S(2)}, u32[]{:S(2)}) collective-permute-start(bf16[8,48,512]{2,1,0:T(8,128)(2,1)S(1)} %attend.1.own_refs_0_), channel_id=1, source_target_pairs={{0,2},{2,0},{1,3},{3,1},{4,6},{6,4},{5,7},{7,5},{8,10},{10,8},{9,1... | collective-permute-start | bytes 1179656 | tf_op jit(solution)/shard_map/ppermute | solution.py:236
  31.1 7.7 %collective-permute-start.8 = (bf16[2,48,512]{2,1,0:T(8,128)(2,1)S(1)}, bf16[2,48,512]{2,1,0:T(8,128)(2,1)S(1)}, u32[]{:S(2)}, u32[]{:S(2)}) collective-permute-start(bf16[2,48,512]{2,1,0:T(8,128)(2,1)S(1)} %get-tuple-element.30), channel_id=1, source_target_pairs={{0,12},{2,15},{1,13},{3,14},{4,8},{6,11},{5,9},{7,10},{8,4},{10,7}... | collective-permute-start | bytes 294920 | tf_op jit(solution)/shard_map/ppermute | solution.py:199
  33.6 7.9 %collective-permute-start.9 = (bf16[2,48,512]{2,1,0:T(8,128)(2,1)S(1)}, bf16[2,48,512]{2,1,0:T(8,128)(2,1)S(1)}, u32[]{:S(2)}, u32[]{:S(2)}) collective-permute-start(bf16[2,48,512]{2,1,0:T(8,128)(2,1)S(1)} %get-tuple-element.31), channel_id=1, source_target_pairs={{0,5},{2,11},{1,4},{3,10},{4,1},{6,15},{5,0},{7,14},{8,13},{10,3},... | collective-permute-start | bytes 294920 | tf_op jit(solution)/shard_map/ppermute | solution.py:199
  38.3 4.9 %collective-permute-start.10 = (bf16[2,48,512]{2,1,0:T(8,128)(2,1)S(1)}, bf16[2,48,512]{2,1,0:T(8,128)(2,1)S(1)}, u32[]{:S(2)}, u32[]{:S(2)}) collective-permute-start(bf16[2,48,512]{2,1,0:T(8,128)(2,1)S(1)} %get-tuple-element.32), channel_id=1, source_target_pairs={{0,1},{2,6},{1,0},{3,7},{4,5},{6,2},{5,4},{7,3},{8,9},{10,14},{9,8... | collective-permute-start | bytes 294920 | tf_op jit(solution)/shard_map/ppermute | solution.py:199
  38.8 5.4 %collective-permute-start.14 = (bf16[48,512]{1,0:T(8,128)(2,1)S(1)}, bf16[48,512]{1,0:T(8,128)(2,1)S(1)}, u32[]{:S(2)}, u32[]{:S(2)}) collective-permute-start(bf16[48,512]{1,0:T(8,128)(2,1)S(1)} %get-tuple-element.33), channel_id=1, source_target_pairs={{0,8},{2,10},{1,9},{3,11},{4,12},{6,14},{5,13},{7,15},{8,0},{10,2}... | collective-permute-start | bytes 147464 | tf_op jit(solution)/shard_map/ppermute | solution.py:199
  38.8 5.4 %collective-permute-start.11 = (bf16[48,512]{1,0:T(8,128)(2,1)S(1)}, bf16[48,512]{1,0:T(8,128)(2,1)S(1)}, u32[]{:S(2)}, u32[]{:S(2)}) collective-permute-start(bf16[48,512]{1,0:T(8,128)(2,1)S(1)} %take.3), channel_id=1, source_target_pairs={{0,2},{2,0},{1,3},{3,1},{4,6},{6,4},{5,7},{7,5},{8,10},{10,8},{9,1... | collective-permute-start | bytes 147464 | tf_op jit(solution)/shard_map/ppermute | solution.py:266
  41.5 2.7 %collective-permute-start.12 = (bf16[48,512]{1,0:T(8,128)(2,1)S(1)}, bf16[48,512]{1,0:T(8,128)(2,1)S(1)}, u32[]{:S(2)}, u32[]{:S(2)}) collective-permute-start(bf16[48,512]{1,0:T(8,128)(2,1)S(1)} %take.4), channel_id=1, source_target_pairs={{0,2},{2,0},{1,3},{3,1},{4,6},{6,4},{5,7},{7,5},{8,10},{10,8},{9,1... | collective-permute-start | bytes 147464 | tf_op jit(solution)/shard_map/ppermute | solution.py:266
  43.2 1.2 %collective-permute-start.13 = (bf16[48,512]{1,0:T(8,128)(2,1)S(1)}, bf16[48,512]{1,0:T(8,128)(2,1)S(1)}, u32[]{:S(2)}, u32[]{:S(2)}) collective-permute-start(bf16[48,512]{1,0:T(8,128)(2,1)S(1)} %take.5), channel_id=1, source_target_pairs={{0,2},{2,0},{1,3},{3,1},{4,6},{6,4},{5,7},{7,5},{8,10},{10,8},{9,1... | collective-permute-start | bytes 147464 | tf_op jit(solution)/shard_map/ppermute | solution.py:266
